TPU v7x, 256 devices: a whole 4x4x8 slice. The times are simulated.
256 devices in a mesh: dp: 16 (over x, y_hi, core), ctx: 16 (over z, y_lo).
Axes of the slice: x: 4, y: 4 (y_hi: 2, y_lo: 2; y = y_hi * 2 + y_lo), z: 8, core: 2. Of those that a mesh axis runs over, the one named last changes fastest.
Arguments:
- queries: bfloat16 [16, 2048, 4096], P('dp', 'ctx'), may hold values from -5.5 to 5.5
- key_rows: bfloat16 [16, 2048, 512], P('dp', 'ctx'), may hold values from -5.5 to 5.5
- value_rows: bfloat16 [16, 2048, 512], P('dp', 'ctx'), may hold values from -6 to 6
- forward_out: bfloat16 [16, 2048, 4096], P('dp', 'ctx'), may hold values from -6 to 6
- out_grads: bfloat16 [16, 2048, 4096], P('dp', 'ctx'), may hold values from -6 to 6
- doc_lengths: int32 [16, 8], P('dp'), may hold values from 1 to 1024, 2048 in all within a row
- mask_tiers: int32 [16, 32, 32], P('dp'), may hold values from 0 to 2, as said below
- row_owners: int32 [16, 2048, 1], P('dp', 'ctx'), may hold values from 0 to 15; in each aligned block of 128 rows (0 to 127, 128 to 255, ..., all dimensions but the last counted through in order) at most 16 rows name the same one
Outputs:
- returned: bfloat16 [16, 16, 16, 16, 5120], P('dp', 'ctx')
Inputs may be any that keep to these rules, and one draw needn't show every extreme that they name: `doc_lengths`: the 8 lengths of a pack sum to 2048. mask_tiers[p, b, b] is 1 or 2. `row_owners`: among the 128 positions of one device at most 16 name the same owner, and some device has an owner named exactly 16 times.
All inputs are finite; a program needn't handle non-finite values.
Results may differ from a plain program's by a relative error of at most 0.0048.
Values may be sent and summed in bfloat16 or wider, within the bound.
No kernel may reach another device: no remote copies, remote signals or barrier semaphores. Data moves between devices by JAX's collectives and lax.ppermute only.
A program may use at most 128 MiB of HBM per device.

v0:
```python
import jax
import jax.numpy as jnp
from jax import lax
from jax.sharding import PartitionSpec as P

H = 32
KV = 4
HD = 128
MASK_BLK = 64
CAP = 16


def shifted(value, axis, by):
    size = lax.axis_size(axis)
    return lax.ppermute(value, axis, [(i, (i + by) % size) for i in range(size)])


def doc_index(lengths, count):
    doc_ends = jnp.cumsum(lengths)
    places = jnp.arange(count, dtype=jnp.int32)
    return jnp.sum((places[:, None] >= doc_ends[None, :]).astype(jnp.int32), axis=1)


def ahead_blocks(key_block, value_block):
    return shifted((key_block, value_block), "ctx", 1)


def ahead_grads(key_grad, value_grad):
    return shifted((key_grad, value_grad), "ctx", 1)


def lane_grads(query_part, grad_part, lse_part, delta_part, key_part, value_part, allowed, factor):
    scores = (
        jnp.einsum("ikgd,jkd->kgij", query_part, key_part, preferred_element_type=jnp.float32)
        * factor
    )
    weights = jnp.where(allowed, jnp.exp(scores - lse_part[..., None]), 0.0)
    weights_low = weights.astype(jnp.bfloat16)
    dprobs = jnp.einsum("ikgd,jkd->kgij", grad_part, value_part, preferred_element_type=jnp.float32)
    dscores = (weights * (dprobs - delta_part[..., None])).astype(jnp.bfloat16)
    dquery = jnp.einsum("kgij,jkd->ikgd", dscores, key_part, preferred_element_type=jnp.float32)
    key_grad = jnp.einsum("kgij,ikgd->jkd", dscores, query_part, preferred_element_type=jnp.float32)
    value_grad = jnp.einsum(
        "kgij,ikgd->jkd", weights_low, grad_part, preferred_element_type=jnp.float32
    )
    return (dquery, key_grad, value_grad)


def per_device(
    queries, key_rows, value_rows, forward_out, out_grads, doc_lengths, mask_tiers, row_owners
):
    local_rows = queries.shape[1]
    groups = H // KV
    factor = HD ** (-0.5)
    ctx_size = lax.axis_size("ctx")
    dp_size = lax.axis_size("dp")
    position = lax.axis_index("ctx")
    total_len = local_rows * ctx_size
    query_start = position * local_rows
    docs_all = doc_index(doc_lengths[0], total_len)
    query_docs = lax.dynamic_slice_in_dim(docs_all, query_start, local_rows, 0)
    query_pos = query_start + jnp.arange(local_rows, dtype=jnp.int32)
    tier_rows = lax.dynamic_slice_in_dim(
        mask_tiers[0], query_start // MASK_BLK, local_rows // MASK_BLK, 0
    )
    query_heads = queries[0].reshape(local_rows, KV, groups, HD)
    grad_heads = out_grads[0].reshape(local_rows, KV, groups, HD)
    out_heads = forward_out[0].reshape(local_rows, KV, groups, HD)
    key_heads = key_rows[0].reshape(local_rows, KV, HD)
    value_heads = value_rows[0].reshape(local_rows, KV, HD)
    delta_rows = jnp.transpose(
        jnp.sum(grad_heads.astype(jnp.float32) * out_heads.astype(jnp.float32), axis=3), (1, 2, 0)
    )

    def allowed_at(key_start, key_count):
        key_pos = key_start + jnp.arange(key_count, dtype=jnp.int32)
        key_docs = lax.dynamic_slice_in_dim(docs_all, key_start, key_count, 0)
        tier_tile = lax.dynamic_slice_in_dim(
            tier_rows, key_start // MASK_BLK, key_count // MASK_BLK, 1
        )
        tier_tile = jnp.repeat(jnp.repeat(tier_tile, MASK_BLK, axis=0), MASK_BLK, axis=1)
        causal = key_pos[None, :] <= query_pos[:, None]
        return (query_docs[:, None] == key_docs[None, :]) & (
            (tier_tile == 2) | (tier_tile == 1) & causal
        )

    key_piece = lax.all_gather(key_heads, "ctx", axis=0, tiled=True)
    row_max = jnp.full((KV, groups, local_rows), -1e30, jnp.float32)
    scores = (
        jnp.einsum("ikgd,jkd->kgij", query_heads, key_piece, preferred_element_type=jnp.float32)
        * factor
    )
    allowed = allowed_at(jnp.int32(0), key_piece.shape[0])
    masked_scores = jnp.where(allowed, scores, -1e30)
    new_max = jnp.maximum(row_max, jnp.max(masked_scores, axis=3))
    fresh = jnp.sum(jnp.where(allowed, jnp.exp(scores - new_max[..., None]), 0.0), axis=3)
    lse = new_max + jnp.log(fresh)
    lane_list = [(0, KV, 1, ahead_blocks, ahead_grads)]

    def lane_work(hop_index, lane_spec, lane_state):
        first_head, last_head, stride = (lane_spec[0], lane_spec[1], lane_spec[2])
        dquery, key_block, value_block, key_grad, value_grad = lane_state
        source = jnp.remainder(position - stride * hop_index, ctx_size)
        key_start = source * local_rows
        part_query, part_key, part_value = lane_grads(
            query_heads,
            grad_heads,
            lse,
            delta_rows,
            key_block,
            value_block,
            allowed_at(key_start, local_rows),
            factor,
        )
        return (
            dquery + part_query,
            key_block,
            value_block,
            key_grad + part_key,
            value_grad + part_value,
        )

    def cycle_step(hop_index, lane_states):
        updated = []
        for lane_spec, lane_state in zip(lane_list, lane_states):
            dquery, key_block, value_block, key_grad, value_grad = lane_work(
                hop_index, lane_spec, lane_state
            )
            key_block, value_block = lane_spec[3](key_block, value_block)
            key_grad, value_grad = lane_spec[4](key_grad, value_grad)
            updated.append((dquery, key_block, value_block, key_grad, value_grad))
        return tuple(updated)

    lane_spec = lane_list[0]
    first_head = lane_spec[0]
    last_head = lane_spec[1]
    head_count = last_head - first_head
    initial = [
        (
            jnp.zeros((local_rows, head_count, groups, HD), jnp.float32),
            key_heads,
            value_heads,
            jnp.zeros((local_rows, head_count, HD), jnp.float32),
            jnp.zeros((local_rows, head_count, HD), jnp.float32),
        )
    ]
    lane_states = lax.fori_loop(0, ctx_size - 1, cycle_step, tuple(initial))
    query_parts = []
    key_parts = []
    value_parts = []
    for lane_spec, lane_state in zip(lane_list, lane_states):
        dquery, key_block, value_block, key_grad, value_grad = lane_work(
            ctx_size - 1, lane_spec, lane_state
        )
        key_grad, value_grad = lane_spec[4](key_grad, value_grad)
        query_parts.append(dquery)
        key_parts.append(key_grad)
        value_parts.append(value_grad)
    dquery = query_parts[0]
    dkey = key_parts[0]
    dvalue = value_parts[0]
    query_out = (dquery * factor).astype(jnp.bfloat16).reshape(local_rows, H * HD)
    key_out = (dkey * factor).astype(jnp.bfloat16).reshape(local_rows, KV * HD)
    value_out = dvalue.astype(jnp.bfloat16).reshape(local_rows, KV * HD)
    grad_rows = jnp.concatenate([query_out, key_out, value_out], axis=1)
    row_width = grad_rows.shape[1]
    owner_ids = row_owners[0, :, 0]
    onehot = (owner_ids[:, None] == jnp.arange(dp_size, dtype=jnp.int32)[None, :]).astype(jnp.int32)
    before = jnp.cumsum(onehot, axis=0) - onehot
    slot_ids = jnp.sum(before * onehot, axis=1)
    targets = owner_ids * CAP + slot_ids
    packed = jnp.zeros((dp_size * CAP, row_width), jnp.bfloat16).at[targets].set(grad_rows)
    received = lax.all_to_all(
        packed.reshape(dp_size, CAP, row_width), "dp", split_axis=0, concat_axis=0, tiled=True
    )
    return received[None, None]


def solution(mesh):
    return jax.shard_map(
        per_device,
        mesh=mesh,
        in_specs=(
            P("dp", "ctx", None),
            P("dp", "ctx", None),
            P("dp", "ctx", None),
            P("dp", "ctx", None),
            P("dp", "ctx", None),
            P("dp", None),
            P("dp", None, None),
            P("dp", "ctx", None),
        ),
        out_specs=P("dp", "ctx", None, None, None),
        check_vma=False,
    )
```

profile of v0, /device:TPU:1, one launch (start us, length us, event | category | flops | bytes accessed | tf_op | source)
XLA Modules:
  0.0 534.8 jit_solution(17146007700842017525)
XLA Ops:
  14.3 2.6 copy.56
  27.7 49.0 %all-gather.2.cloned.1.call-done = bf16[2048,4,128]{2,0,1:T(8,128)(2,1)} async-done(((bf16[128,4,128]{2,0,1:T(8,128)(2,1)}), bf16[2048,4,128]{2,0,1:T(8,128)(2,1)}) %all-gather.2.cloned.1.call-update) | async-done | bytes 2097168 | tf_op jit(solution)/shard_map/all_gather | solution.py:87
  76.7 14.6 %fusion.14 = (f32[4,8,128]{2,1,0:T(8,128)S(1)}, f32[4,2048,128,8]{2,1,3,0:T(8,128)}) fusion(pred[128,2048]{0,1:T(8,128)(4,1)S(1)} %fusion.39, bf16[128,4,8,128]{0,3,2,1:T(8,128)(2,1)} %bitcast.217, bf16[2048,4,128]{2,0,1:T(8,128)(2,1)} %all-gather.2.cloned.1.call-done), kind=kOutput, calls=%fused_computation.27 | convolution fusion | flops 2172645376 | bytes 36978688 | tf_op jit(solution)/shard_map/ikgd,jkd->kgij/dot_general | solution.py:90
  91.3 14.2 %fusion.17 = f32[4,8,128]{2,1,0:T(8,128)S(1)} fusion(f32[4,2048,128,8]{2,1,3,0:T(8,128)} %get-tuple-element.504, f32[4,8,128]{2,1,0:T(8,128)S(1)} %broadcast_maximum_fusion, pred[128,2048]{0,1:T(8,128)(4,1)S(1)} %fusion.39), kind=kLoop, calls=%fused_computation.30 | loop fusion | flops 33550336 | bytes 33849344 | tf_op jit(solution)/shard_map/reduce_sum | solution.py:96
  107.6 326.2 %while.24 = (s32[]{:T(128)}, f32[128,4,8,128]{3,0,2,1:T(8,128)}, bf16[128,4,128]{2,0,1:T(8,128)(2,1)S(1)}, bf16[128,4,128]{2,0,1:T(8,128)(2,1)}, f32[128,4,128]{...) while((s32[]{:T(128)}, f32[128,4,8,128]{3,0,2,1:T(8,128)}, ...), condition=%wide.region_8.9_spmd.clone, body=%wide.region_7.8_spmd.clone.sunk | while | flops 676020544 | bytes 23010124 | solution.py:147
  122.8 3.7 collective-permute-done.2
  126.5 3.8 collective-permute-done.3
  140.6 2.3 collective-permute-start.3
  142.9 3.5 bitcast_add_fusion.4
  146.4 4.9 collective-permute-done.3
  164.5 3.5 bitcast_add_fusion.4
  168.0 3.5 collective-permute-done.3
  184.8 2.8 collective-permute-start.3
  187.6 3.5 bitcast_add_fusion.4
  191.1 2.9 collective-permute-done.3
  195.8 2.8 collective-permute-start.1
  207.2 3.5 bitcast_add_fusion.4
  212.7 5.2 collective-permute-done.3
  228.9 3.5 bitcast_add_fusion.4
  233.9 2.8 collective-permute-done.3
  248.7 2.9 collective-permute-start.3
  251.7 3.5 bitcast_add_fusion.4
  255.1 3.0 collective-permute-done.3
  258.1 2.3 collective-permute-start
  272.7 3.5 bitcast_add_fusion.4
  277.0 4.6 collective-permute-done.3
  292.8 3.5 bitcast_add_fusion.4
  298.2 4.2 collective-permute-done.3
  303.3 2.4 collective-permute-start.1
  314.4 3.5 bitcast_add_fusion.4
  317.8 4.2 collective-permute-done.2
  322.0 5.6 %collective-permute-done.3 = f32[128,4,128]{2,0,1:T(8,128)} collective-permute-done((f32[128,4,128]{2,0,1:T(8,128)}, f32[128,4,128]{2,0,1:T(8,128)}, u32[]{:S(2)}, u32[]{:S(2)}) %collective-permute-start.3) | collective-permute-done | bytes 262176 | tf_op jit(solution)/shard_map/while/body/eval_jaxpr/ppermute | solution.py:15
  337.4 3.5 bitcast_add_fusion.4
  340.9 3.1 collective-permute-done.2
  344.0 5.6 %collective-permute-done.3 = f32[128,4,128]{2,0,1:T(8,128)} collective-permute-done((f32[128,4,128]{2,0,1:T(8,128)}, f32[128,4,128]{2,0,1:T(8,128)}, u32[]{:S(2)}, u32[]{:S(2)}) %collective-permute-start.3) | collective-permute-done | bytes 262176 | tf_op jit(solution)/shard_map/while/body/eval_jaxpr/ppermute | solution.py:15
  360.2 3.1 collective-permute-start.3
  363.3 3.5 bitcast_add_fusion.4
  366.8 4.2 collective-permute-done.3
  385.0 3.5 bitcast_add_fusion.4
  388.5 4.1 collective-permute-done.3
  405.0 3.5 bitcast_add_fusion.4
  408.9 3.2 collective-permute-done.3
  424.1 3.5 bitcast_add_fusion.4
  429.0 4.9 collective-permute-done.3
  433.8 3.0 copy.68
  443.8 8.2 %collective-permute-done.5 = bf16[128,4,128]{2,0,1:T(8,128)(2,1)S(1)} collective-permute-done((bf16[128,4,128]{2,0,1:T(8,128)(2,1)S(1)}, bf16[128,4,128]{2,0,1:T(8,128)(2,1)S(1)}, u32[]{:S(2)}, u32[]{:S(2)}) %collective-permute-start.5) | collective-permute-done | bytes 131104 | tf_op jit(solution)/shard_map/ppermute | solution.py:15
  452.6 4.4 scatter_custom_fusion
  457.0 69.4 %all_to_all.5 = bf16[16,16,5120]{2,1,0:T(8,128)(2,1)S(1)} all-to-all(bf16[16,16,5120]{2,1,0:T(8,128)(2,1)} %bitcast.220), channel_id=1, replica_groups=mesh['dp'=16,'ctx'=16] {'dp'}, dimensions={0} | all-to-all | bytes 5242880 | tf_op jit(solution)/shard_map/all_to_all | solution.py:173
  (427 shorter events, 214.3 us)
Async XLA Ops:
  6.5 70.1 %all-gather.2.cloned.1.call-start = ((), (), s32[]{:S(2)}) async-start(), calls=%async_computation.1 | async-start | bytes 2228224 | tf_op jit(solution)/shard_map/all_gather | solution.py:87
  107.7 15.2 %collective-permute-start = (bf16[128,4,128]{2,0,1:T(8,128)(2,1)S(1)}, bf16[128,4,128]{2,0,1:T(8,128)(2,1)S(1)}, u32[]{:S(2)}, u32[]{:S(2)}) collective-permute-start(bf16[128,4,128]{2,0,1:T(8,128)(2,1)S(1)} %copy.106), channel_id=1, source_target_pairs={{0,1},{1,2},{2,3},{3,4},{4,5},{5,6},{6,7},{7,8},{8,9},{9,10},{10,1... | collective-permute-start | bytes 393224 | tf_op jit(solution)/shard_map/while/body/eval_jaxpr/ppermute | solution.py:15
  108.8 14.0 %collective-permute-start.1 = (bf16[128,4,128]{2,0,1:T(8,128)(2,1)S(1)}, bf16[128,4,128]{2,0,1:T(8,128)(2,1)}, u32[]{:S(2)}, u32[]{:S(2)}) collective-permute-start(bf16[128,4,128]{2,0,1:T(8,128)(2,1)S(1)} %copy.107), channel_id=1, source_target_pairs={{0,1},{1,2},{2,3},{3,4},{4,5},{5,6},{6,7},{7,8},{8,9},{9,10},{10,1... | collective-permute-start | bytes 393224 | tf_op jit(solution)/shard_map/while/body/eval_jaxpr/ppermute | solution.py:15
  117.0 9.5 %collective-permute-start.2 = (f32[128,4,128]{2,0,1:T(8,128)}, f32[128,4,128]{2,0,1:T(8,128)}, u32[]{:S(2)}, u32[]{:S(2)}) collective-permute-start(f32[128,4,128]{2,0,1:T(8,128)} %fusion.89), channel_id=1, source_target_pairs={{0,1},{1,2},{2,3},{3,4},{4,5},{5,6},{6,7},{7,8},{8,9},{9,10},{10,1... | collective-permute-start | bytes 786440 | tf_op jit(solution)/shard_map/while/body/eval_jaxpr/ppermute | solution.py:15
  119.8 10.5 %collective-permute-start.3 = (f32[128,4,128]{2,0,1:T(8,128)}, f32[128,4,128]{2,0,1:T(8,128)}, u32[]{:S(2)}, u32[]{:S(2)}) collective-permute-start(f32[128,4,128]{2,0,1:T(8,128)} %fusion.90), channel_id=1, source_target_pairs={{0,1},{1,2},{2,3},{3,4},{4,5},{5,6},{6,7},{7,8},{8,9},{9,10},{10,1... | collective-permute-start | bytes 786440 | tf_op jit(solution)/shard_map/while/body/eval_jaxpr/ppermute | solution.py:15
  130.3 16.1 %collective-permute-start = (bf16[128,4,128]{2,0,1:T(8,128)(2,1)S(1)}, bf16[128,4,128]{2,0,1:T(8,128)(2,1)S(1)}, u32[]{:S(2)}, u32[]{:S(2)}) collective-permute-start(bf16[128,4,128]{2,0,1:T(8,128)(2,1)S(1)} %copy.106), channel_id=1, source_target_pairs={{0,1},{1,2},{2,3},{3,4},{4,5},{5,6},{6,7},{7,8},{8,9},{9,10},{10,1... | collective-permute-start | bytes 393224 | tf_op jit(solution)/shard_map/while/body/eval_jaxpr/ppermute | solution.py:15
  131.3 15.1 %collective-permute-start.1 = (bf16[128,4,128]{2,0,1:T(8,128)(2,1)S(1)}, bf16[128,4,128]{2,0,1:T(8,128)(2,1)}, u32[]{:S(2)}, u32[]{:S(2)}) collective-permute-start(bf16[128,4,128]{2,0,1:T(8,128)(2,1)S(1)} %copy.107), channel_id=1, source_target_pairs={{0,1},{1,2},{2,3},{3,4},{4,5},{5,6},{6,7},{7,8},{8,9},{9,10},{10,1... | collective-permute-start | bytes 393224 | tf_op jit(solution)/shard_map/while/body/eval_jaxpr/ppermute | solution.py:15
  140.6 10.7 %collective-permute-start.3 = (f32[128,4,128]{2,0,1:T(8,128)}, f32[128,4,128]{2,0,1:T(8,128)}, u32[]{:S(2)}, u32[]{:S(2)}) collective-permute-start(f32[128,4,128]{2,0,1:T(8,128)} %fusion.90), channel_id=1, source_target_pairs={{0,1},{1,2},{2,3},{3,4},{4,5},{5,6},{6,7},{7,8},{8,9},{9,10},{10,1... | collective-permute-start | bytes 786440 | tf_op jit(solution)/shard_map/while/body/eval_jaxpr/ppermute | solution.py:15
  151.3 16.6 %collective-permute-start = (bf16[128,4,128]{2,0,1:T(8,128)(2,1)S(1)}, bf16[128,4,128]{2,0,1:T(8,128)(2,1)S(1)}, u32[]{:S(2)}, u32[]{:S(2)}) collective-permute-start(bf16[128,4,128]{2,0,1:T(8,128)(2,1)S(1)} %copy.106), channel_id=1, source_target_pairs={{0,1},{1,2},{2,3},{3,4},{4,5},{5,6},{6,7},{7,8},{8,9},{9,10},{10,1... | collective-permute-start | bytes 393224 | tf_op jit(solution)/shard_map/while/body/eval_jaxpr/ppermute | solution.py:15
  152.3 15.6 %collective-permute-start.1 = (bf16[128,4,128]{2,0,1:T(8,128)(2,1)S(1)}, bf16[128,4,128]{2,0,1:T(8,128)(2,1)}, u32[]{:S(2)}, u32[]{:S(2)}) collective-permute-start(bf16[128,4,128]{2,0,1:T(8,128)(2,1)S(1)} %copy.107), channel_id=1, source_target_pairs={{0,1},{1,2},{2,3},{3,4},{4,5},{5,6},{6,7},{7,8},{8,9},{9,10},{10,1... | collective-permute-start | bytes 393224 | tf_op jit(solution)/shard_map/while/body/eval_jaxpr/ppermute | solution.py:15
  171.5 19.6 %collective-permute-start = (bf16[128,4,128]{2,0,1:T(8,128)(2,1)S(1)}, bf16[128,4,128]{2,0,1:T(8,128)(2,1)S(1)}, u32[]{:S(2)}, u32[]{:S(2)}) collective-permute-start(bf16[128,4,128]{2,0,1:T(8,128)(2,1)S(1)} %copy.106), channel_id=1, source_target_pairs={{0,1},{1,2},{2,3},{3,4},{4,5},{5,6},{6,7},{7,8},{8,9},{9,10},{10,1... | collective-permute-start | bytes 393224 | tf_op jit(solution)/shard_map/while/body/eval_jaxpr/ppermute | solution.py:15
  173.5 17.6 %collective-permute-start.1 = (bf16[128,4,128]{2,0,1:T(8,128)(2,1)S(1)}, bf16[128,4,128]{2,0,1:T(8,128)(2,1)}, u32[]{:S(2)}, u32[]{:S(2)}) collective-permute-start(bf16[128,4,128]{2,0,1:T(8,128)(2,1)S(1)} %copy.107), channel_id=1, source_target_pairs={{0,1},{1,2},{2,3},{3,4},{4,5},{5,6},{6,7},{7,8},{8,9},{9,10},{10,1... | collective-permute-start | bytes 393224 | tf_op jit(solution)/shard_map/while/body/eval_jaxpr/ppermute | solution.py:15
  181.9 9.2 %collective-permute-start.2 = (f32[128,4,128]{2,0,1:T(8,128)}, f32[128,4,128]{2,0,1:T(8,128)}, u32[]{:S(2)}, u32[]{:S(2)}) collective-permute-start(f32[128,4,128]{2,0,1:T(8,128)} %fusion.89), channel_id=1, source_target_pairs={{0,1},{1,2},{2,3},{3,4},{4,5},{5,6},{6,7},{7,8},{8,9},{9,10},{10,1... | collective-permute-start | bytes 786440 | tf_op jit(solution)/shard_map/while/body/eval_jaxpr/ppermute | solution.py:15
  184.8 9.2 %collective-permute-start.3 = (f32[128,4,128]{2,0,1:T(8,128)}, f32[128,4,128]{2,0,1:T(8,128)}, u32[]{:S(2)}, u32[]{:S(2)}) collective-permute-start(f32[128,4,128]{2,0,1:T(8,128)} %fusion.90), channel_id=1, source_target_pairs={{0,1},{1,2},{2,3},{3,4},{4,5},{5,6},{6,7},{7,8},{8,9},{9,10},{10,1... | collective-permute-start | bytes 786440 | tf_op jit(solution)/shard_map/while/body/eval_jaxpr/ppermute | solution.py:15
  194.1 16.6 %collective-permute-start = (bf16[128,4,128]{2,0,1:T(8,128)(2,1)S(1)}, bf16[128,4,128]{2,0,1:T(8,128)(2,1)S(1)}, u32[]{:S(2)}, u32[]{:S(2)}) collective-permute-start(bf16[128,4,128]{2,0,1:T(8,128)(2,1)S(1)} %copy.106), channel_id=1, source_target_pairs={{0,1},{1,2},{2,3},{3,4},{4,5},{5,6},{6,7},{7,8},{8,9},{9,10},{10,1... | collective-permute-start | bytes 393224 | tf_op jit(solution)/shard_map/while/body/eval_jaxpr/ppermute | solution.py:15
  195.8 14.9 %collective-permute-start.1 = (bf16[128,4,128]{2,0,1:T(8,128)(2,1)S(1)}, bf16[128,4,128]{2,0,1:T(8,128)(2,1)}, u32[]{:S(2)}, u32[]{:S(2)}) collective-permute-start(bf16[128,4,128]{2,0,1:T(8,128)(2,1)S(1)} %copy.107), channel_id=1, source_target_pairs={{0,1},{1,2},{2,3},{3,4},{4,5},{5,6},{6,7},{7,8},{8,9},{9,10},{10,1... | collective-permute-start | bytes 393224 | tf_op jit(solution)/shard_map/while/body/eval_jaxpr/ppermute | solution.py:15
  207.2 10.8 %collective-permute-start.3 = (f32[128,4,128]{2,0,1:T(8,128)}, f32[128,4,128]{2,0,1:T(8,128)}, u32[]{:S(2)}, u32[]{:S(2)}) collective-permute-start(f32[128,4,128]{2,0,1:T(8,128)} %fusion.90), channel_id=1, source_target_pairs={{0,1},{1,2},{2,3},{3,4},{4,5},{5,6},{6,7},{7,8},{8,9},{9,10},{10,1... | collective-permute-start | bytes 786440 | tf_op jit(solution)/shard_map/while/body/eval_jaxpr/ppermute | solution.py:15
  218.0 14.4 %collective-permute-start = (bf16[128,4,128]{2,0,1:T(8,128)(2,1)S(1)}, bf16[128,4,128]{2,0,1:T(8,128)(2,1)S(1)}, u32[]{:S(2)}, u32[]{:S(2)}) collective-permute-start(bf16[128,4,128]{2,0,1:T(8,128)(2,1)S(1)} %copy.106), channel_id=1, source_target_pairs={{0,1},{1,2},{2,3},{3,4},{4,5},{5,6},{6,7},{7,8},{8,9},{9,10},{10,1... | collective-permute-start | bytes 393224 | tf_op jit(solution)/shard_map/while/body/eval_jaxpr/ppermute | solution.py:15
  218.9 13.4 %collective-permute-start.1 = (bf16[128,4,128]{2,0,1:T(8,128)(2,1)S(1)}, bf16[128,4,128]{2,0,1:T(8,128)(2,1)}, u32[]{:S(2)}, u32[]{:S(2)}) collective-permute-start(bf16[128,4,128]{2,0,1:T(8,128)(2,1)S(1)} %copy.107), channel_id=1, source_target_pairs={{0,1},{1,2},{2,3},{3,4},{4,5},{5,6},{6,7},{7,8},{8,9},{9,10},{10,1... | collective-permute-start | bytes 393224 | tf_op jit(solution)/shard_map/while/body/eval_jaxpr/ppermute | solution.py:15
  236.7 18.4 %collective-permute-start = (bf16[128,4,128]{2,0,1:T(8,128)(2,1)S(1)}, bf16[128,4,128]{2,0,1:T(8,128)(2,1)S(1)}, u32[]{:S(2)}, u32[]{:S(2)}) collective-permute-start(bf16[128,4,128]{2,0,1:T(8,128)(2,1)S(1)} %copy.106), channel_id=1, source_target_pairs={{0,1},{1,2},{2,3},{3,4},{4,5},{5,6},{6,7},{7,8},{8,9},{9,10},{10,1... | collective-permute-start | bytes 393224 | tf_op jit(solution)/shard_map/while/body/eval_jaxpr/ppermute | solution.py:15
  237.7 17.4 %collective-permute-start.1 = (bf16[128,4,128]{2,0,1:T(8,128)(2,1)S(1)}, bf16[128,4,128]{2,0,1:T(8,128)(2,1)}, u32[]{:S(2)}, u32[]{:S(2)}) collective-permute-start(bf16[128,4,128]{2,0,1:T(8,128)(2,1)S(1)} %copy.107), channel_id=1, source_target_pairs={{0,1},{1,2},{2,3},{3,4},{4,5},{5,6},{6,7},{7,8},{8,9},{9,10},{10,1... | collective-permute-start | bytes 393224 | tf_op jit(solution)/shard_map/while/body/eval_jaxpr/ppermute | solution.py:15
  248.7 9.3 %collective-permute-start.3 = (f32[128,4,128]{2,0,1:T(8,128)}, f32[128,4,128]{2,0,1:T(8,128)}, u32[]{:S(2)}, u32[]{:S(2)}) collective-permute-start(f32[128,4,128]{2,0,1:T(8,128)} %fusion.90), channel_id=1, source_target_pairs={{0,1},{1,2},{2,3},{3,4},{4,5},{5,6},{6,7},{7,8},{8,9},{9,10},{10,1... | collective-permute-start | bytes 786440 | tf_op jit(solution)/shard_map/while/body/eval_jaxpr/ppermute | solution.py:15
  258.1 18.0 %collective-permute-start = (bf16[128,4,128]{2,0,1:T(8,128)(2,1)S(1)}, bf16[128,4,128]{2,0,1:T(8,128)(2,1)S(1)}, u32[]{:S(2)}, u32[]{:S(2)}) collective-permute-start(bf16[128,4,128]{2,0,1:T(8,128)(2,1)S(1)} %copy.106), channel_id=1, source_target_pairs={{0,1},{1,2},{2,3},{3,4},{4,5},{5,6},{6,7},{7,8},{8,9},{9,10},{10,1... | collective-permute-start | bytes 393224 | tf_op jit(solution)/shard_map/while/body/eval_jaxpr/ppermute | solution.py:15
  261.3 14.8 %collective-permute-start.1 = (bf16[128,4,128]{2,0,1:T(8,128)(2,1)S(1)}, bf16[128,4,128]{2,0,1:T(8,128)(2,1)}, u32[]{:S(2)}, u32[]{:S(2)}) collective-permute-start(bf16[128,4,128]{2,0,1:T(8,128)(2,1)S(1)} %copy.107), channel_id=1, source_target_pairs={{0,1},{1,2},{2,3},{3,4},{4,5},{5,6},{6,7},{7,8},{8,9},{9,10},{10,1... | collective-permute-start | bytes 393224 | tf_op jit(solution)/shard_map/while/body/eval_jaxpr/ppermute | solution.py:15
  271.5 10.1 %collective-permute-start.3 = (f32[128,4,128]{2,0,1:T(8,128)}, f32[128,4,128]{2,0,1:T(8,128)}, u32[]{:S(2)}, u32[]{:S(2)}) collective-permute-start(f32[128,4,128]{2,0,1:T(8,128)} %fusion.90), channel_id=1, source_target_pairs={{0,1},{1,2},{2,3},{3,4},{4,5},{5,6},{6,7},{7,8},{8,9},{9,10},{10,1... | collective-permute-start | bytes 786440 | tf_op jit(solution)/shard_map/while/body/eval_jaxpr/ppermute | solution.py:15
  281.6 14.6 %collective-permute-start = (bf16[128,4,128]{2,0,1:T(8,128)(2,1)S(1)}, bf16[128,4,128]{2,0,1:T(8,128)(2,1)S(1)}, u32[]{:S(2)}, u32[]{:S(2)}) collective-permute-start(bf16[128,4,128]{2,0,1:T(8,128)(2,1)S(1)} %copy.106), channel_id=1, source_target_pairs={{0,1},{1,2},{2,3},{3,4},{4,5},{5,6},{6,7},{7,8},{8,9},{9,10},{10,1... | collective-permute-start | bytes 393224 | tf_op jit(solution)/shard_map/while/body/eval_jaxpr/ppermute | solution.py:15
  282.6 13.7 %collective-permute-start.1 = (bf16[128,4,128]{2,0,1:T(8,128)(2,1)S(1)}, bf16[128,4,128]{2,0,1:T(8,128)(2,1)}, u32[]{:S(2)}, u32[]{:S(2)}) collective-permute-start(bf16[128,4,128]{2,0,1:T(8,128)(2,1)S(1)} %copy.107), channel_id=1, source_target_pairs={{0,1},{1,2},{2,3},{3,4},{4,5},{5,6},{6,7},{7,8},{8,9},{9,10},{10,1... | collective-permute-start | bytes 393224 | tf_op jit(solution)/shard_map/while/body/eval_jaxpr/ppermute | solution.py:15
  291.3 11.0 %collective-permute-start.3 = (f32[128,4,128]{2,0,1:T(8,128)}, f32[128,4,128]{2,0,1:T(8,128)}, u32[]{:S(2)}, u32[]{:S(2)}) collective-permute-start(f32[128,4,128]{2,0,1:T(8,128)} %fusion.90), channel_id=1, source_target_pairs={{0,1},{1,2},{2,3},{3,4},{4,5},{5,6},{6,7},{7,8},{8,9},{9,10},{10,1... | collective-permute-start | bytes 786440 | tf_op jit(solution)/shard_map/while/body/eval_jaxpr/ppermute | solution.py:15
  302.3 15.5 %collective-permute-start = (bf16[128,4,128]{2,0,1:T(8,128)(2,1)S(1)}, bf16[128,4,128]{2,0,1:T(8,128)(2,1)S(1)}, u32[]{:S(2)}, u32[]{:S(2)}) collective-permute-start(bf16[128,4,128]{2,0,1:T(8,128)(2,1)S(1)} %copy.106), channel_id=1, source_target_pairs={{0,1},{1,2},{2,3},{3,4},{4,5},{5,6},{6,7},{7,8},{8,9},{9,10},{10,1... | collective-permute-start | bytes 393224 | tf_op jit(solution)/shard_map/while/body/eval_jaxpr/ppermute | solution.py:15
  303.3 14.5 %collective-permute-start.1 = (bf16[128,4,128]{2,0,1:T(8,128)(2,1)S(1)}, bf16[128,4,128]{2,0,1:T(8,128)(2,1)}, u32[]{:S(2)}, u32[]{:S(2)}) collective-permute-start(bf16[128,4,128]{2,0,1:T(8,128)(2,1)S(1)} %copy.107), channel_id=1, source_target_pairs={{0,1},{1,2},{2,3},{3,4},{4,5},{5,6},{6,7},{7,8},{8,9},{9,10},{10,1... | collective-permute-start | bytes 393224 | tf_op jit(solution)/shard_map/while/body/eval_jaxpr/ppermute | solution.py:15
  312.3 9.8 %collective-permute-start.2 = (f32[128,4,128]{2,0,1:T(8,128)}, f32[128,4,128]{2,0,1:T(8,128)}, u32[]{:S(2)}, u32[]{:S(2)}) collective-permute-start(f32[128,4,128]{2,0,1:T(8,128)} %fusion.89), channel_id=1, source_target_pairs={{0,1},{1,2},{2,3},{3,4},{4,5},{5,6},{6,7},{7,8},{8,9},{9,10},{10,1... | collective-permute-start | bytes 786440 | tf_op jit(solution)/shard_map/while/body/eval_jaxpr/ppermute | solution.py:15
  314.4 13.3 %collective-permute-start.3 = (f32[128,4,128]{2,0,1:T(8,128)}, f32[128,4,128]{2,0,1:T(8,128)}, u32[]{:S(2)}, u32[]{:S(2)}) collective-permute-start(f32[128,4,128]{2,0,1:T(8,128)} %fusion.90), channel_id=1, source_target_pairs={{0,1},{1,2},{2,3},{3,4},{4,5},{5,6},{6,7},{7,8},{8,9},{9,10},{10,1... | collective-permute-start | bytes 786440 | tf_op jit(solution)/shard_map/while/body/eval_jaxpr/ppermute | solution.py:15
  327.6 13.2 %collective-permute-start = (bf16[128,4,128]{2,0,1:T(8,128)(2,1)S(1)}, bf16[128,4,128]{2,0,1:T(8,128)(2,1)S(1)}, u32[]{:S(2)}, u32[]{:S(2)}) collective-permute-start(bf16[128,4,128]{2,0,1:T(8,128)(2,1)S(1)} %copy.106), channel_id=1, source_target_pairs={{0,1},{1,2},{2,3},{3,4},{4,5},{5,6},{6,7},{7,8},{8,9},{9,10},{10,1... | collective-permute-start | bytes 393224 | tf_op jit(solution)/shard_map/while/body/eval_jaxpr/ppermute | solution.py:15
  328.6 12.2 %collective-permute-start.1 = (bf16[128,4,128]{2,0,1:T(8,128)(2,1)S(1)}, bf16[128,4,128]{2,0,1:T(8,128)(2,1)}, u32[]{:S(2)}, u32[]{:S(2)}) collective-permute-start(bf16[128,4,128]{2,0,1:T(8,128)(2,1)S(1)} %copy.107), channel_id=1, source_target_pairs={{0,1},{1,2},{2,3},{3,4},{4,5},{5,6},{6,7},{7,8},{8,9},{9,10},{10,1... | collective-permute-start | bytes 393224 | tf_op jit(solution)/shard_map/while/body/eval_jaxpr/ppermute | solution.py:15
  337.2 12.3 %collective-permute-start.3 = (f32[128,4,128]{2,0,1:T(8,128)}, f32[128,4,128]{2,0,1:T(8,128)}, u32[]{:S(2)}, u32[]{:S(2)}) collective-permute-start(f32[128,4,128]{2,0,1:T(8,128)} %fusion.90), channel_id=1, source_target_pairs={{0,1},{1,2},{2,3},{3,4},{4,5},{5,6},{6,7},{7,8},{8,9},{9,10},{10,1... | collective-permute-start | bytes 786440 | tf_op jit(solution)/shard_map/while/body/eval_jaxpr/ppermute | solution.py:15
  349.6 17.2 %collective-permute-start = (bf16[128,4,128]{2,0,1:T(8,128)(2,1)S(1)}, bf16[128,4,128]{2,0,1:T(8,128)(2,1)S(1)}, u32[]{:S(2)}, u32[]{:S(2)}) collective-permute-start(bf16[128,4,128]{2,0,1:T(8,128)(2,1)S(1)} %copy.106), channel_id=1, source_target_pairs={{0,1},{1,2},{2,3},{3,4},{4,5},{5,6},{6,7},{7,8},{8,9},{9,10},{10,1... | collective-permute-start | bytes 393224 | tf_op jit(solution)/shard_map/while/body/eval_jaxpr/ppermute | solution.py:15
  350.6 16.2 %collective-permute-start.1 = (bf16[128,4,128]{2,0,1:T(8,128)(2,1)S(1)}, bf16[128,4,128]{2,0,1:T(8,128)(2,1)}, u32[]{:S(2)}, u32[]{:S(2)}) collective-permute-start(bf16[128,4,128]{2,0,1:T(8,128)(2,1)S(1)} %copy.107), channel_id=1, source_target_pairs={{0,1},{1,2},{2,3},{3,4},{4,5},{5,6},{6,7},{7,8},{8,9},{9,10},{10,1... | collective-permute-start | bytes 393224 | tf_op jit(solution)/shard_map/while/body/eval_jaxpr/ppermute | solution.py:15
  357.1 9.7 %collective-permute-start.2 = (f32[128,4,128]{2,0,1:T(8,128)}, f32[128,4,128]{2,0,1:T(8,128)}, u32[]{:S(2)}, u32[]{:S(2)}) collective-permute-start(f32[128,4,128]{2,0,1:T(8,128)} %fusion.89), channel_id=1, source_target_pairs={{0,1},{1,2},{2,3},{3,4},{4,5},{5,6},{6,7},{7,8},{8,9},{9,10},{10,1... | collective-permute-start | bytes 786440 | tf_op jit(solution)/shard_map/while/body/eval_jaxpr/ppermute | solution.py:15
  360.2 10.7 %collective-permute-start.3 = (f32[128,4,128]{2,0,1:T(8,128)}, f32[128,4,128]{2,0,1:T(8,128)}, u32[]{:S(2)}, u32[]{:S(2)}) collective-permute-start(f32[128,4,128]{2,0,1:T(8,128)} %fusion.90), channel_id=1, source_target_pairs={{0,1},{1,2},{2,3},{3,4},{4,5},{5,6},{6,7},{7,8},{8,9},{9,10},{10,1... | collective-permute-start | bytes 786440 | tf_op jit(solution)/shard_map/while/body/eval_jaxpr/ppermute | solution.py:15
  371.0 17.5 %collective-permute-start = (bf16[128,4,128]{2,0,1:T(8,128)(2,1)S(1)}, bf16[128,4,128]{2,0,1:T(8,128)(2,1)S(1)}, u32[]{:S(2)}, u32[]{:S(2)}) collective-permute-start(bf16[128,4,128]{2,0,1:T(8,128)(2,1)S(1)} %copy.106), channel_id=1, source_target_pairs={{0,1},{1,2},{2,3},{3,4},{4,5},{5,6},{6,7},{7,8},{8,9},{9,10},{10,1... | collective-permute-start | bytes 393224 | tf_op jit(solution)/shard_map/while/body/eval_jaxpr/ppermute | solution.py:15
  372.0 16.5 %collective-permute-start.1 = (bf16[128,4,128]{2,0,1:T(8,128)(2,1)S(1)}, bf16[128,4,128]{2,0,1:T(8,128)(2,1)}, u32[]{:S(2)}, u32[]{:S(2)}) collective-permute-start(bf16[128,4,128]{2,0,1:T(8,128)(2,1)S(1)} %copy.107), channel_id=1, source_target_pairs={{0,1},{1,2},{2,3},{3,4},{4,5},{5,6},{6,7},{7,8},{8,9},{9,10},{10,1... | collective-permute-start | bytes 393224 | tf_op jit(solution)/shard_map/while/body/eval_jaxpr/ppermute | solution.py:15
  392.6 15.9 %collective-permute-start = (bf16[128,4,128]{2,0,1:T(8,128)(2,1)S(1)}, bf16[128,4,128]{2,0,1:T(8,128)(2,1)S(1)}, u32[]{:S(2)}, u32[]{:S(2)}) collective-permute-start(bf16[128,4,128]{2,0,1:T(8,128)(2,1)S(1)} %copy.106), channel_id=1, source_target_pairs={{0,1},{1,2},{2,3},{3,4},{4,5},{5,6},{6,7},{7,8},{8,9},{9,10},{10,1... | collective-permute-start | bytes 393224 | tf_op jit(solution)/shard_map/while/body/eval_jaxpr/ppermute | solution.py:15
  394.1 14.3 %collective-permute-start.1 = (bf16[128,4,128]{2,0,1:T(8,128)(2,1)S(1)}, bf16[128,4,128]{2,0,1:T(8,128)(2,1)}, u32[]{:S(2)}, u32[]{:S(2)}) collective-permute-start(bf16[128,4,128]{2,0,1:T(8,128)(2,1)S(1)} %copy.107), channel_id=1, source_target_pairs={{0,1},{1,2},{2,3},{3,4},{4,5},{5,6},{6,7},{7,8},{8,9},{9,10},{10,1... | collective-permute-start | bytes 393224 | tf_op jit(solution)/shard_map/while/body/eval_jaxpr/ppermute | solution.py:15
  412.2 15.4 %collective-permute-start = (bf16[128,4,128]{2,0,1:T(8,128)(2,1)S(1)}, bf16[128,4,128]{2,0,1:T(8,128)(2,1)S(1)}, u32[]{:S(2)}, u32[]{:S(2)}) collective-permute-start(bf16[128,4,128]{2,0,1:T(8,128)(2,1)S(1)} %copy.106), channel_id=1, source_target_pairs={{0,1},{1,2},{2,3},{3,4},{4,5},{5,6},{6,7},{7,8},{8,9},{9,10},{10,1... | collective-permute-start | bytes 393224 | tf_op jit(solution)/shard_map/while/body/eval_jaxpr/ppermute | solution.py:15
  413.2 14.4 %collective-permute-start.1 = (bf16[128,4,128]{2,0,1:T(8,128)(2,1)S(1)}, bf16[128,4,128]{2,0,1:T(8,128)(2,1)}, u32[]{:S(2)}, u32[]{:S(2)}) collective-permute-start(bf16[128,4,128]{2,0,1:T(8,128)(2,1)S(1)} %copy.107), channel_id=1, source_target_pairs={{0,1},{1,2},{2,3},{3,4},{4,5},{5,6},{6,7},{7,8},{8,9},{9,10},{10,1... | collective-permute-start | bytes 393224 | tf_op jit(solution)/shard_map/while/body/eval_jaxpr/ppermute | solution.py:15
  423.4 10.5 %collective-permute-start.3 = (f32[128,4,128]{2,0,1:T(8,128)}, f32[128,4,128]{2,0,1:T(8,128)}, u32[]{:S(2)}, u32[]{:S(2)}) collective-permute-start(f32[128,4,128]{2,0,1:T(8,128)} %fusion.90), channel_id=1, source_target_pairs={{0,1},{1,2},{2,3},{3,4},{4,5},{5,6},{6,7},{7,8},{8,9},{9,10},{10,1... | collective-permute-start | bytes 786440 | tf_op jit(solution)/shard_map/while/body/eval_jaxpr/ppermute | solution.py:15
  441.0 11.3 %collective-permute-start.4 = (f32[128,4,128]{2,0,1:T(8,128)S(1)}, f32[128,4,128]{2,0,1:T(8,128)S(1)}, u32[]{:S(2)}, u32[]{:S(2)}) collective-permute-start(f32[128,4,128]{2,0,1:T(8,128)S(1)} %fusion.34), channel_id=1, source_target_pairs={{0,1},{1,2},{2,3},{3,4},{4,5},{5,6},{6,7},{7,8},{8,9},{9,10},{10,1... | collective-permute-start | bytes 786440 | tf_op jit(solution)/shard_map/ppermute | solution.py:15
  442.6 9.4 %collective-permute-start.5 = (bf16[128,4,128]{2,0,1:T(8,128)(2,1)S(1)}, bf16[128,4,128]{2,0,1:T(8,128)(2,1)S(1)}, u32[]{:S(2)}, u32[]{:S(2)}) collective-permute-start(bf16[128,4,128]{2,0,1:T(8,128)(2,1)S(1)} %fusion.35), channel_id=1, source_target_pairs={{0,1},{1,2},{2,3},{3,4},{4,5},{5,6},{6,7},{7,8},{8,9},{9,10},{10,1... | collective-permute-start | bytes 393224 | tf_op jit(solution)/shard_map/ppermute | solution.py:15
  (25 other events, 177.7 us)
Sparse Core Ops, SparseCore 0:
  9.2 67.4 all-gather.1
where the time goes:
time: 539 us; the launch traced here: 535 us
  matrix products  159 us (29%)
  waiting for transfers between devices  139 us (26%)
  blocking collectives  69.4 us (13%)
  local copies, waits for them, and re-layouts  59.8 us (11%)
  starting transfers between devices  51.7 us (10%)
  other arithmetic  41 us (8%)
  between operations  13.8 us (3%)
    ppermute x62, waiting for transfers between devices, shifted(): lax.ppermute(value, axis, [(i, (i + by) % size) for i in range(size)])  90.1 us
    all_to_all x1, blocking collectives, per_device(): lax.all_to_all(packed.reshape(dp_size, CAP, row_width), 'dp', split_axis=...  69.4 us
    ppermute x62, starting transfers between devices, shifted(): lax.ppermute(value, axis, [(i, (i + by) % size) for i in range(size)])  51.7 us
    dot_general x16, matrix products, lane_grads(): jnp.einsum('kgij,jkd->ikgd', dscores, key_part, preferred_element_type=jn...  50.7 us
    all_gather x1, waiting for transfers between devices, per_device(): key_piece = lax.all_gather(key_heads, 'ctx', axis=0, tiled=True)  49 us
    dot_general x16, matrix products, lane_grads(): jnp.einsum('kgij,ikgd->jkd', weights_low, grad_part, preferred_element_ty...  33.1 us
    dot_general x16, matrix products, lane_grads(): jnp.einsum('kgij,ikgd->jkd', dscores, query_part, preferred_element_type=...  32.4 us
    dot_general x16, matrix products, lane_grads(): jnp.einsum('ikgd,jkd->kgij', query_part, key_part, preferred_element_type...  20.3 us
  transfers between devices with their start and end apart: 63, of which 26 were waited for; matrix products, arithmetic and copies ran while one was open for 40% of the time, Pallas kernels for 0%

commit v1 on v0

v1 whole, which is shorter than its diff:
```python
import math

import jax
import jax.numpy as jnp
from jax import lax
from jax.experimental import pallas as pl
from jax.experimental.pallas import tpu as pltpu
from jax.sharding import Mesh, PartitionSpec as P

H = 32
KV = 4
HD = 128
CAP = 16
N_DP = 16
NZ = 8
ROWS = 128
BLK = 2 * ROWS
HALF_Q = H * HD // 2
HALF_KV = KV * HD // 2
CHUNK = 2 * HD
STEPS = HALF_Q // CHUNK
SLOTS = N_DP * 2 * CAP
NEG = -1e30
F32 = jnp.float32
BF16 = jnp.bfloat16
NT = (((1,), (1,)), ((), ()))
NN = (((1,), (0,)), ((), ()))


def zshift(x, by):
    return lax.ppermute(x, "z", [(i, (i + by) % NZ) for i in range(NZ)])


def yswap(x):
    return lax.ppermute(x, "yl", [(0, 1), (1, 0)])


def grads_kernel(where_ref, ends_ref, tiers_ref, *refs):
    keys_in = refs[0:16]
    (q_own, q_par, g_own, g_par, delta_own, delta_par, t_own, t_par) = refs[16:24]
    packed_ref = refs[24]
    kv_out = refs[25:41]
    (kbuf, kt, sbuf, bias, acc, dqt, onehot, mx, active) = refs[41:]
    step = pl.program_id(0)
    z = where_ref[0]
    y = where_ref[1]
    factor = HD**-0.5
    to_log2 = factor * math.log2(math.e)

    @pl.when(step == 0)
    def _prepare():
        acc[...] = jnp.zeros_like(acc)
        target = jnp.concatenate([t_own[...], t_par[...]], axis=1)
        slot = lax.broadcasted_iota(jnp.int32, (SLOTS, BLK), 0)
        onehot[...] = jnp.where(slot == target, 1.0, 0.0).astype(BF16)
        lane = lax.broadcasted_iota(jnp.int32, (1, BLK), 1)
        query_pos = z * BLK + ((lane + ROWS * y) & (BLK - 1))
        first = jnp.zeros((1, BLK), jnp.int32)
        last = jnp.full((1, BLK), NZ * BLK, jnp.int32)
        for d in range(8):
            end = ends_ref[d]
            first = jnp.where(end <= query_pos, jnp.maximum(first, end), first)
            last = jnp.where(end > query_pos, jnp.minimum(last, end), last)
        last = last - 1
        low = jnp.int32(0)
        high = jnp.int32(NZ * BLK)
        for d in range(8):
            end = ends_ref[d]
            low = jnp.where(end <= z * BLK, jnp.maximum(low, end), low)
            high = jnp.where(end > z * BLK + BLK - 1, jnp.minimum(high, end), high)
        count = jnp.int32(0)
        for r in range(NZ):
            zb = (z - r) & (NZ - 1)
            kbuf[r, 0:ROWS, :] = keys_in[2 * r][...]
            kbuf[r, ROWS:BLK, :] = keys_in[2 * r + 1][...]
            needed = (zb * BLK < high) & (zb * BLK + BLK > low)
            active[count] = r
            count = count + needed.astype(jnp.int32)

            @pl.when(needed)
            def _block(r=r, zb=zb):
                for g in range(2):
                    kt[r, g] = kbuf[r, :, g * HD : (g + 1) * HD].T
                for jb in range(4):
                    j_base = zb * BLK + ROWS * (y ^ (jb // 2)) + 64 * (jb % 2)
                    j_blk = zb * 4 + 2 * (y ^ (jb // 2)) + jb % 2
                    key_pos = j_base + lax.broadcasted_iota(jnp.int32, (64, ROWS), 0)
                    for ip in range(2):
                        i_blk = z * 4 + 2 * (y ^ ip)
                        tier = jnp.where(
                            lax.broadcasted_iota(jnp.int32, (1, ROWS), 1) < 64,
                            tiers_ref[i_blk * 32 + j_blk],
                            tiers_ref[(i_blk + 1) * 32 + j_blk],
                        )
                        cols = slice(ip * ROWS, (ip + 1) * ROWS)
                        reach = jnp.where(tier == 2, NZ * BLK, jnp.where(tier == 1, query_pos[:, cols], -1))
                        upper = jnp.minimum(reach, last[:, cols])
                        ok = (key_pos >= first[:, cols]) & (key_pos <= upper)
                        bias[r, jb * 64 : (jb + 1) * 64, cols] = jnp.where(ok, 0.0, NEG)

        active[NZ] = count

    kv_head = step // (STEPS // 2)
    n_active = active[NZ]
    q = jnp.concatenate([q_own[:, :HD], q_par[:, :HD], q_own[:, HD:], q_par[:, HD:]], axis=0)
    g = jnp.concatenate([g_own[:, :HD], g_par[:, :HD], g_own[:, HD:], g_par[:, HD:]], axis=0)
    delta = jnp.concatenate(
        [
            delta_own[pl.ds(2 * step, 1), :],
            delta_par[pl.ds(2 * step, 1), :],
            delta_own[pl.ds(2 * step + 1, 1), :],
            delta_par[pl.ds(2 * step + 1, 1), :],
        ],
        axis=1,
    )
    k_cols = pl.ds(pl.multiple_of(kv_head * HD, HD), HD)
    v_cols = pl.ds(pl.multiple_of(HALF_KV + kv_head * HD, HD), HD)
    mx[...] = jnp.full_like(mx, NEG)
    dqt[...] = jnp.zeros_like(dqt)

    def score(n, carry):
        r = active[n]
        s = lax.dot_general(kbuf[r, :, k_cols], q, NT, preferred_element_type=F32)
        b = bias[r]
        s = s * to_log2 + jnp.concatenate([b, b], axis=1)
        sbuf[r] = s
        mx[...] = jnp.maximum(mx[...], jnp.max(s.reshape(BLK // 8, 8, 2 * BLK), axis=0))
        return carry

    lax.fori_loop(0, n_active, score, 0)
    top = jnp.max(mx[...], axis=0, keepdims=True)
    mx[...] = jnp.zeros_like(mx)

    def exponent(n, carry):
        r = active[n]
        p = jnp.exp2(sbuf[r] - top)
        sbuf[r] = p
        mx[...] += jnp.sum(p.reshape(BLK // 8, 8, 2 * BLK), axis=0)
        return carry

    lax.fori_loop(0, n_active, exponent, 0)
    inverse = 1.0 / jnp.sum(mx[...], axis=0, keepdims=True)

    def backward(n, carry):
        r = active[n]
        w = sbuf[r] * inverse
        dp = lax.dot_general(kbuf[r, :, v_cols], g, NT, preferred_element_type=F32)
        ds = (w * (dp - delta)).astype(BF16)
        acc[r, :, v_cols] += lax.dot_general(w.astype(BF16), g, NN, preferred_element_type=F32)
        acc[r, :, k_cols] += lax.dot_general(ds, q, NN, preferred_element_type=F32)
        dqt[...] += lax.dot_general(kt[r, kv_head], ds, NN, preferred_element_type=F32)
        return carry

    lax.fori_loop(0, n_active, backward, 0)
    low_dq = (dqt[...] * factor).astype(BF16)
    for h in range(2):
        packed_ref[:, h * HD : (h + 1) * HD] = lax.dot_general(
            onehot[...], low_dq[:, h * BLK : (h + 1) * BLK], NT, preferred_element_type=F32
        ).astype(BF16)

    @pl.when(step == STEPS - 1)
    def _finish():
        for r in range(NZ):
            for half in range(2):
                out = kv_out[2 * r + half]
                rows = slice(half * ROWS, (half + 1) * ROWS)
                out[:, :HALF_KV] = (acc[r, rows, :HALF_KV] * factor).astype(out.dtype)
                out[:, HALF_KV:] = acc[r, rows, HALF_KV:].astype(out.dtype)


def attention_grads(where, ends, tiers, keys, q_all, q_par, g_all, g_par, delta_own, delta_par, t_own, t_par):
    whole = pl.BlockSpec(memory_space=pltpu.VMEM)
    own = pl.BlockSpec((ROWS, CHUNK), lambda c, where, ends, tiers: (0, where[1] * STEPS + c))
    partner = pl.BlockSpec((ROWS, CHUNK), lambda c, where, ends, tiers: (0, c))
    block = jax.ShapeDtypeStruct((ROWS, 2 * HALF_KV), BF16)
    block_f32 = jax.ShapeDtypeStruct((ROWS, 2 * HALF_KV), F32)
    return pl.pallas_call(
        grads_kernel,
        grid_spec=pltpu.PrefetchScalarGridSpec(
            num_scalar_prefetch=3,
            grid=(STEPS,),
            in_specs=[whole] * 16 + [own, partner, own, partner] + [whole] * 4,
            out_specs=[pl.BlockSpec((SLOTS, CHUNK), lambda c, where, ends, tiers: (0, c))] + [whole] * 16,
            scratch_shapes=[
                pltpu.VMEM((NZ, BLK, 2 * HALF_KV), BF16),
                pltpu.VMEM((NZ, 2, HD, BLK), BF16),
                pltpu.VMEM((NZ, BLK, 2 * BLK), F32),
                pltpu.VMEM((NZ, BLK, BLK), F32),
                pltpu.VMEM((NZ, BLK, 2 * HALF_KV), F32),
                pltpu.VMEM((HD, 2 * BLK), F32),
                pltpu.VMEM((SLOTS, BLK), BF16),
                pltpu.VMEM((8, 2 * BLK), F32),
                pltpu.SMEM((NZ + 1,), jnp.int32),
            ],
        ),
        out_shape=[jax.ShapeDtypeStruct((SLOTS, HALF_Q), BF16)] + [block_f32] * 2 + [block] * 14,
        compiler_params=pltpu.CompilerParams(
            dimension_semantics=("arbitrary",), vmem_limit_bytes=48 * 1024 * 1024
        ),
        cost_estimate=pl.CostEstimate(flops=8 * 10**9, bytes_accessed=10 * 2**20, transcendentals=4 * 10**6),
        name="grads",
    )(where, ends, tiers, *keys, q_all, q_par, g_all, g_par, delta_own, delta_par, t_own, t_par)


def finish_kernel(own_a, own_b, down_a, up_a, down_b, up_b, t_own, t_par, out):
    target = jnp.concatenate([t_own[...], t_par[...]], axis=1)
    slot = lax.broadcasted_iota(jnp.int32, (SLOTS, BLK), 0)
    onehot = jnp.where(slot == target, 1.0, 0.0).astype(BF16)
    a = own_a[...] + down_a[...].astype(F32) + up_a[...].astype(F32)
    b = own_b[...] + down_b[...].astype(F32) + up_b[...].astype(F32)
    rows = jnp.concatenate([a, b], axis=0).astype(BF16)
    out[...] = lax.dot_general(onehot, rows, NN, preferred_element_type=F32).astype(BF16)


def finish_rows(*operands):
    whole = pl.BlockSpec(memory_space=pltpu.VMEM)
    return pl.pallas_call(
        finish_kernel,
        in_specs=[whole] * 8,
        out_specs=whole,
        out_shape=jax.ShapeDtypeStruct((SLOTS, 2 * HALF_KV), BF16),
        compiler_params=pltpu.CompilerParams(vmem_limit_bytes=16 * 1024 * 1024),
        name="finish",
    )(*operands)


def lay_out_kernel(q_ref, kv_ref, out):
    for y in range(2):
        out[0, :, y * HALF_Q : (y + 1) * HALF_Q] = q_ref[y]
        for part in range(2):
            start = 2 * HALF_Q + part * 2 * HALF_KV + y * HALF_KV
            out[0, :, start : start + HALF_KV] = kv_ref[y, :, part * HALF_KV : (part + 1) * HALF_KV]


def lay_out(q_rows, kv_rows):
    width = 2 * HALF_Q + 4 * HALF_KV
    return pl.pallas_call(
        lay_out_kernel,
        grid=(N_DP,),
        in_specs=[
            pl.BlockSpec((2, CAP, HALF_Q), lambda n: (n, 0, 0)),
            pl.BlockSpec((2, CAP, 2 * HALF_KV), lambda n: (n, 0, 0)),
        ],
        out_specs=pl.BlockSpec((1, CAP, width), lambda n: (n, 0, 0)),
        out_shape=jax.ShapeDtypeStruct((N_DP, CAP, width), BF16),
        name="lay_out",
    )(q_rows, kv_rows)


def add_low(a, b):
    return (a.astype(F32) + b.astype(F32)).astype(BF16)


def per_device(queries, key_rows, value_rows, forward_out, out_grads, doc_lengths, mask_tiers, row_owners):
    z = lax.axis_index("z").astype(jnp.int32)
    y = lax.axis_index("yl").astype(jnp.int32)
    q_all, g_all = queries[0], out_grads[0]

    def half(x, which, width):
        return lax.dynamic_slice_in_dim(x, which * width, width, 1)

    def key_values(which):
        return jnp.concatenate(
            [half(key_rows[0], which, HALF_KV), half(value_rows[0], which, HALF_KV)], axis=1
        )

    a = key_values(y)
    b = yswap(key_values(1 - y))
    q_par = yswap(half(q_all, 1 - y, HALF_Q))
    g_par = yswap(half(g_all, 1 - y, HALF_Q))
    keys_a = {0: a}
    keys_b = {0: b}
    for hop in range(1, 4):
        for held in (keys_a, keys_b):
            held[hop] = zshift(held[hop - 1], 1)
            held[NZ - hop] = zshift(held[(NZ - hop + 1) % NZ], -1)
    keys_a[4] = zshift(keys_a[3], 1)
    keys_b[4] = zshift(keys_b[5], -1)

    owners = row_owners[0, :, 0]
    places = jnp.arange(ROWS, dtype=jnp.int32)
    earlier = (places[:, None] < places[None, :]) & (owners[:, None] == owners[None, :])
    slots = jnp.sum(earlier.astype(jnp.int32), axis=0)
    t_own = (owners * (2 * CAP) + y * CAP + slots)[None, :]
    t_par = yswap(t_own)
    delta = jnp.sum(
        g_all.reshape(ROWS, H, HD).astype(F32) * forward_out[0].reshape(ROWS, H, HD).astype(F32), axis=2
    ).T
    delta_own = lax.dynamic_slice_in_dim(delta, y * (H // 2), H // 2, 0)
    delta_par = yswap(lax.dynamic_slice_in_dim(delta, (1 - y) * (H // 2), H // 2, 0))
    ends = jnp.cumsum(doc_lengths[0])

    keys = []
    for r in range(NZ):
        keys += [keys_a[r], keys_b[r]]
    packed, own_a, own_b, *parts = attention_grads(
        jnp.stack([z, y]),
        ends,
        mask_tiers[0].reshape(-1),
        keys,
        q_all,
        q_par,
        g_all,
        g_par,
        delta_own,
        delta_par,
        t_own,
        t_par,
    )
    part_a = {r: parts[2 * (r - 1)] for r in range(1, NZ)}
    part_b = {r: parts[2 * (r - 1) + 1] for r in range(1, NZ)}

    down_a = zshift(part_a[4], -1)
    up_b = zshift(part_b[4], 1)
    for r in (3, 2, 1):
        down_a = zshift(add_low(down_a, part_a[r]), -1)
        up_b = zshift(add_low(up_b, part_b[NZ - r]), 1)
    down_b = zshift(part_b[3], -1)
    up_a = zshift(part_a[5], 1)
    for r in (2, 1):
        down_b = zshift(add_low(down_b, part_b[r]), -1)
        up_a = zshift(add_low(up_a, part_a[NZ - r]), 1)

    def to_owners(rows):
        width = rows.shape[1]
        return lax.all_to_all(
            rows.reshape(2 * N_DP, CAP, width), ("dp", "yl"), split_axis=0, concat_axis=0, tiled=True
        )

    q_rows = to_owners(packed)
    kv_rows = to_owners(finish_rows(own_a, own_b, down_a, up_a, down_b, up_b, t_own, t_par))
    return lay_out(q_rows, kv_rows)[None, None]


def solution(mesh):
    fine = Mesh(mesh.devices.reshape(N_DP, NZ, 2), ("dp", "z", "yl"))
    rows = P("dp", ("z", "yl"), None)
    return jax.shard_map(
        per_device,
        mesh=fine,
        in_specs=(rows, rows, rows, rows, rows, P("dp", None), P("dp", None, None), rows),
        out_specs=P("dp", ("z", "yl"), None, None, None),
        check_vma=False,
    )
```

time: 539 us -> 185 us (0.34)
  matrix products: 159 us -> 0 us
  waiting for transfers between devices: 139 us -> 18.8 us
  local copies, waits for them, and re-layouts: 59.8 us -> 5.4 us
  other arithmetic: 41 us -> 4.52 us
  Pallas kernels: 0 us -> 27.9 us
  between operations: 13.8 us -> 0.25 us
  starting transfers between devices: 51.7 us -> 64.7 us
  blocking collectives: 69.4 us -> 61.8 us
    dot_general x81 -> x0, matrix products: 159 us -> none  [the longest x16 50.7 us: lane_grads(): jnp.einsum('kgij,jkd->ikgd', dscores, key_part, preferred_element_type=jn...]
    ppermute x62 -> x33, waiting for transfers between devices: 90.1 us -> 18.8 us  [the longest x28 18.1 us: zshift(): return lax.ppermute(x, 'z', [(i, (i + by) % NZ) for i in range(NZ)])]
    all_gather x1 -> x0, waiting for transfers between devices: 49 us -> none  [per_device(): key_piece = lax.all_gather(key_heads, 'ctx', axis=0, tiled=True)]
    pallas_call x0 -> x3, Pallas kernels: none -> 27.9 us  [the longest x1 18 us: attention_grads(): pl.pallas_call(grads_kernel, grid_spec=pltpu.PrefetchScalarGridSpec(num_s...]
    dynamic_slice x45 -> x3, local copies, waits for them, and re-layouts: 24 us -> 4.74 us  [half(): return lax.dynamic_slice_in_dim(x, which * width, width, 1)]
    while x31 -> x0, local copies, waits for them, and re-layouts: 16.7 us -> none
    reduce_sum x4 -> x2, other arithmetic: 16.7 us -> 1.44 us  [the longest x1 0.83 us: per_device(): slots = jnp.sum(earlier.astype(jnp.int32), axis=0)]
    and x17 -> x0, other arithmetic: 13.2 us -> none  [allowed_at(): (query_docs[:, None] == key_docs[None, :]) & ((tier_tile == 2) | (tier_ti...]
  transfers between devices with their start and end apart: 63 -> 33, of which waited for: 26 -> 13; matrix products, arithmetic and copies ran while one was open for 40% -> 5% of each run, Pallas kernels for 0% -> 0%
where the time goes in v1:
time: 185 us; the launch traced here: 183 us
  starting transfers between devices  64.7 us (35%)
  blocking collectives  61.8 us (33%)
  Pallas kernels  27.9 us (15%)
  waiting for transfers between devices  18.8 us (10%)
  local copies, waits for them, and re-layouts  5.4 us (3%)
  other arithmetic  4.52 us (2%)
    all_to_all x2, blocking collectives, to_owners(): lax.all_to_all(rows.reshape(2 * N_DP, CAP, width), ('dp', 'yl'), split_ax...  61.8 us
    ppermute x28, starting transfers between devices, zshift(): return lax.ppermute(x, 'z', [(i, (i + by) % NZ) for i in range(NZ)])  60.3 us
    ppermute x28, waiting for transfers between devices, zshift(): return lax.ppermute(x, 'z', [(i, (i + by) % NZ) for i in range(NZ)])  18.1 us
    pallas_call x1, Pallas kernels, attention_grads(): pl.pallas_call(grads_kernel, grid_spec=pltpu.PrefetchScalarGridSpec(num_s...  18 us
    pallas_call x1, Pallas kernels, lay_out(): pl.pallas_call(lay_out_kernel, grid=(N_DP,), in_specs=[pl.BlockSpec((2, C...  9.58 us
    dynamic_slice x3, local copies, waits for them, and re-layouts, half(): return lax.dynamic_slice_in_dim(x, which * width, width, 1)  4.74 us
    ppermute x5, starting transfers between devices, yswap(): return lax.ppermute(x, 'yl', [(0, 1), (1, 0)])  4.38 us
  transfers between devices with their start and end apart: 33, of which 13 were waited for; matrix products, arithmetic and copies ran while one was open for 5% of the time, Pallas kernels for 0%

profile of v1, /device:TPU:1, one launch (start us, length us, event | category | flops | bytes accessed | tf_op | source)
XLA Modules:
  0.0 183.3 jit_solution(9540151624012606462)
XLA Ops:
  0.0 1.0 dynamic-slice_bitcast_fusion.2
  1.0 6.5 %collective-permute-start.12 = (bf16[128,512]{1,0:T(8,128)(2,1)S(1)}, bf16[128,512]{1,0:T(8,128)(2,1)S(1)}, u32[]{:S(2)}, u32[]{:S(2)}) collective-permute-start(bf16[128,512]{1,0:T(8,128)(2,1)S(1)} %pad_maximum_fusion.refs_0_), channel_id=1, source_target_pairs={{0,14},{2,0},{4,2},{6,4},{8,6},{10,8},{12,10},{14,12},{1,15},{3,1}... | collective-permute-start | bytes 393224 | tf_op jit(solution)/shard_map/ppermute | solution.py:31
  7.5 0.8 convert_reduce_fusion
  8.3 0.7 bitcast_add_fusion.refs_22_.t_own
  9.0 1.3 collective-permute-start.18
  10.3 0.3 collective-permute-start
  10.5 1.8 multiply_bitcast_fusion
  12.3 0.4 copy.15
  12.7 0.6 reduce_sum.20
  13.5 1.4 collective-permute-start.17
  14.8 1.9 %dynamic-slice_bitcast_fusion = bf16[128,2048]{1,0:T(8,128)(2,1)} fusion(bf16[1,128,4096]{2,1,0:T(8,128)(2,1)} %param.12, s32[]{:T(128)S(6)} %select_n.20), kind=kLoop, calls=%fused_computation.1 | loop fusion | bytes 1048580 | tf_op jit(solution)/shard_map/dynamic_slice | solution.py:260
  16.8 1.9 %dynamic-slice_bitcast_fusion.1 = bf16[128,2048]{1,0:T(8,128)(2,1)} fusion(bf16[1,128,4096]{2,1,0:T(8,128)(2,1)} %param.8, s32[]{:T(128)S(6)} %select_n.20), kind=kLoop, calls=%fused_computation.2 | loop fusion | bytes 1048580 | tf_op jit(solution)/shard_map/dynamic_slice | solution.py:260
  18.6 2.7 %collective-permute-start.13 = (bf16[128,512]{1,0:T(8,128)(2,1)S(1)}, bf16[128,512]{1,0:T(8,128)(2,1)S(1)}, u32[]{:S(2)}, u32[]{:S(2)}) collective-permute-start(bf16[128,512]{1,0:T(8,128)(2,1)S(1)} %collective-permute-done.12.refs_14_), channel_id=1, source_target_pairs={{0,14},{2,0},{4,2},{6,4},{8,6},{10,8},{12,10},{14,12},{1,15},{3,1}... | collective-permute-start | bytes 393224 | tf_op jit(solution)/shard_map/ppermute | solution.py:31
  21.3 2.7 %collective-permute-start.8 = (bf16[128,512]{1,0:T(8,128)(2,1)S(1)}, bf16[128,512]{1,0:T(8,128)(2,1)S(1)}, u32[]{:S(2)}, u32[]{:S(2)}) collective-permute-start(bf16[128,512]{1,0:T(8,128)(2,1)S(1)} %collective-permute-done.refs_1_), channel_id=1, source_target_pairs={{0,14},{2,0},{4,2},{6,4},{8,6},{10,8},{12,10},{14,12},{1,15},{3,1}... | collective-permute-start | bytes 393224 | tf_op jit(solution)/shard_map/ppermute | solution.py:31
  24.0 0.2 collective-permute-start.16
  24.2 1.3 collective-permute-start.15
  25.5 0.9 collective-permute-done.3.refs_4_
  26.3 1.8 collective-permute-start.14
  28.2 2.3 %collective-permute-start.9 = (bf16[128,512]{1,0:T(8,128)(2,1)S(1)}, bf16[128,512]{1,0:T(8,128)(2,1)S(1)}, u32[]{:S(2)}, u32[]{:S(2)}) collective-permute-start(bf16[128,512]{1,0:T(8,128)(2,1)S(1)} %collective-permute-done.8.refs_15_), channel_id=1, source_target_pairs={{0,14},{2,0},{4,2},{6,4},{8,6},{10,8},{12,10},{14,12},{1,15},{3,1}... | collective-permute-start | bytes 393224 | tf_op jit(solution)/shard_map/ppermute | solution.py:31
  30.4 0.1 collective-permute-done.2.refs_3_
  30.6 1.8 collective-permute-done.9.refs_13_
  32.4 3.1 %collective-permute-start.10 = (bf16[128,512]{1,0:T(8,128)(2,1)S(1)}, bf16[128,512]{1,0:T(8,128)(2,1)S(1)}, u32[]{:S(2)}, u32[]{:S(2)}) collective-permute-start(bf16[128,512]{1,0:T(8,128)(2,1)S(1)} %collective-permute-done.9.refs_13_), channel_id=1, source_target_pairs={{0,14},{2,0},{4,2},{6,4},{8,6},{10,8},{12,10},{14,12},{1,15},{3,1}... | collective-permute-start | bytes 393224 | tf_op jit(solution)/shard_map/ppermute | solution.py:31
  35.5 0.4 collective-permute-done.5.refs_6_
  35.9 1.4 collective-permute-done.4.refs_5_
  37.3 0.4 collective-permute-done.10.refs_11_
  37.6 2.9 %collective-permute-start.11 = (bf16[128,512]{1,0:T(8,128)(2,1)S(1)}, bf16[128,512]{1,0:T(8,128)(2,1)S(1)}, u32[]{:S(2)}, u32[]{:S(2)}) collective-permute-start(bf16[128,512]{1,0:T(8,128)(2,1)S(1)} %collective-permute-done.10.refs_11_), channel_id=1, source_target_pairs={{0,14},{2,0},{4,2},{6,4},{8,6},{10,8},{12,10},{14,12},{1,15},{3,1}... | collective-permute-start | bytes 393224 | tf_op jit(solution)/shard_map/ppermute | solution.py:31
  40.5 0.2 reduce-window.9
  40.9 1.7 collective-permute-done.7.refs_8_
  42.6 2.7 %collective-permute-done.6.refs_7_ = bf16[128,512]{1,0:T(8,128)(2,1)S(1)} collective-permute-done((bf16[128,512]{1,0:T(8,128)(2,1)S(1)}, bf16[128,512]{1,0:T(8,128)(2,1)S(1)}, u32[]{:S(2)}, u32[]{:S(2)}) %collective-permute-start.6) | collective-permute-done | bytes 131104 | tf_op jit(solution)/shard_map/ppermute | solution.py:31
  45.3 0.6 collective-permute-done.15.refs_17_
  46.0 18.0 %grads.1 = (bf16[512,2048]{1,0:T(8,128)(2,1)}, f32[128,512]{1,0:T(8,128)S(1)}, f32[128,512]{1,0:T(8,128)S(1)}, bf16[128,512]{1,0:T(8,128)(2,1)S(1)}, bf16[128,51...) custom-call(s32[2]{0:T(128)S(1)} %pad_add_fusion.where_ref, ...), custom_call_target="tpu_custom_call" | custom-call | flops 8000000000 | bytes 10485760 | tf_op jit(solution)/shard_map/grads/pallas_call | solution.py:177
  63.9 0.4 collective-permute-start.19
  64.4 4.6 %collective-permute-start.23 = (bf16[128,512]{1,0:T(8,128)(2,1)S(1)}, bf16[128,512]{1,0:T(8,128)(2,1)S(1)}, u32[]{:S(2)}, u32[]{:S(2)}) collective-permute-start(bf16[128,512]{1,0:T(8,128)(2,1)S(1)} %get-tuple-element.29), channel_id=1, source_target_pairs={{0,2},{2,4},{4,6},{6,8},{8,10},{10,12},{12,14},{14,0},{1,3},{3,5},... | collective-permute-start | bytes 393224 | tf_op jit(solution)/shard_map/ppermute | solution.py:31
  68.9 18.4 %collective-permute-start.26 = (bf16[128,512]{1,0:T(8,128)(2,1)S(1)}, bf16[128,512]{1,0:T(8,128)(2,1)S(1)}, u32[]{:S(2)}, u32[]{:S(2)}) collective-permute-start(bf16[128,512]{1,0:T(8,128)(2,1)S(1)} %get-tuple-element.32), channel_id=1, source_target_pairs={{0,14},{2,0},{4,2},{6,4},{8,6},{10,8},{12,10},{14,12},{1,15},{3,1}... | collective-permute-start | bytes 393224 | tf_op jit(solution)/shard_map/ppermute | solution.py:31
  87.4 2.7 %collective-permute-start.20 = (bf16[128,512]{1,0:T(8,128)(2,1)S(1)}, bf16[128,512]{1,0:T(8,128)(2,1)S(1)}, u32[]{:S(2)}, u32[]{:S(2)}) collective-permute-start(bf16[128,512]{1,0:T(8,128)(2,1)S(1)} %add_convert_fusion.9), channel_id=1, source_target_pairs={{0,14},{2,0},{4,2},{6,4},{8,6},{10,8},{12,10},{14,12},{1,15},{3,1}... | collective-permute-start | bytes 393224 | tf_op jit(solution)/shard_map/ppermute | solution.py:31
  90.3 0.1 collective-permute-done.26
  90.4 3.5 %collective-permute-start.27 = (bf16[128,512]{1,0:T(8,128)(2,1)S(1)}, bf16[128,512]{1,0:T(8,128)(2,1)S(1)}, u32[]{:S(2)}, u32[]{:S(2)}) collective-permute-start(bf16[128,512]{1,0:T(8,128)(2,1)S(1)} %add_convert_fusion.4), channel_id=1, source_target_pairs={{0,14},{2,0},{4,2},{6,4},{8,6},{10,8},{12,10},{14,12},{1,15},{3,1}... | collective-permute-start | bytes 393224 | tf_op jit(solution)/shard_map/ppermute | solution.py:31
  94.1 2.7 %collective-permute-start.21 = (bf16[128,512]{1,0:T(8,128)(2,1)S(1)}, bf16[128,512]{1,0:T(8,128)(2,1)S(1)}, u32[]{:S(2)}, u32[]{:S(2)}) collective-permute-start(bf16[128,512]{1,0:T(8,128)(2,1)S(1)} %add_convert_fusion.8), channel_id=1, source_target_pairs={{0,14},{2,0},{4,2},{6,4},{8,6},{10,8},{12,10},{14,12},{1,15},{3,1}... | collective-permute-start | bytes 393224 | tf_op jit(solution)/shard_map/ppermute | solution.py:31
  96.9 0.3 collective-permute-start.25
  97.3 2.7 %collective-permute-start.28 = (bf16[128,512]{1,0:T(8,128)(2,1)S(1)}, bf16[128,512]{1,0:T(8,128)(2,1)S(1)}, u32[]{:S(2)}, u32[]{:S(2)}) collective-permute-start(bf16[128,512]{1,0:T(8,128)(2,1)S(1)} %add_convert_fusion.3), channel_id=1, source_target_pairs={{0,14},{2,0},{4,2},{6,4},{8,6},{10,8},{12,10},{14,12},{1,15},{3,1}... | collective-permute-start | bytes 393224 | tf_op jit(solution)/shard_map/ppermute | solution.py:31
  100.2 2.7 %collective-permute-start.22 = (bf16[128,512]{1,0:T(8,128)(2,1)S(1)}, bf16[128,512]{1,0:T(8,128)(2,1)S(1)}, u32[]{:S(2)}, u32[]{:S(2)}) collective-permute-start(bf16[128,512]{1,0:T(8,128)(2,1)S(1)} %add_convert_fusion.7), channel_id=1, source_target_pairs={{0,14},{2,0},{4,2},{6,4},{8,6},{10,8},{12,10},{14,12},{1,15},{3,1}... | collective-permute-start | bytes 393224 | tf_op jit(solution)/shard_map/ppermute | solution.py:31
  102.9 2.5 %collective-permute-done.31 = bf16[128,512]{1,0:T(8,128)(2,1)S(1)} collective-permute-done((bf16[128,512]{1,0:T(8,128)(2,1)S(1)}, bf16[128,512]{1,0:T(8,128)(2,1)S(1)}, u32[]{:S(2)}, u32[]{:S(2)}) %collective-permute-start.31) | collective-permute-done | bytes 131104 | tf_op jit(solution)/shard_map/ppermute | solution.py:31
  105.5 0.2 collective-permute-done.22.down_a
  105.7 5.9 %collective-permute-done.32.up_b = bf16[128,512]{1,0:T(8,128)(2,1)S(1)} collective-permute-done((bf16[128,512]{1,0:T(8,128)(2,1)S(1)}, bf16[128,512]{1,0:T(8,128)(2,1)S(1)}, u32[]{:S(2)}, u32[]{:S(2)}) %collective-permute-start.32) | collective-permute-done | bytes 131104 | tf_op jit(solution)/shard_map/ppermute | solution.py:31
  111.6 0.3 finish.1
  112.0 28.0 %all_to_all.10.kv_ref = bf16[32,16,512]{2,1,0:T(8,128)(2,1)} all-to-all(bf16[32,16,512]{2,1,0:T(8,128)(2,1)S(1)} %bitcast.32), channel_id=1, replica_groups=mesh['dp'=16,'z'=8,'yl'=2] {'dp','yl'}, dimensions={0} | all-to-all | bytes 1048576 | tf_op jit(solution)/shard_map/all_to_all | solution.py:326
  140.0 33.8 %all_to_all.11.q_ref = bf16[32,16,2048]{2,1,0:T(8,128)(2,1)} all-to-all(bf16[32,16,2048]{2,1,0:T(8,128)(2,1)S(1)} %bitcast.37), channel_id=1, replica_groups=mesh['dp'=16,'z'=8,'yl'=2] {'dp','yl'}, dimensions={0} | all-to-all | bytes 4194304 | tf_op jit(solution)/shard_map/all_to_all | solution.py:326
  173.7 9.6 %lay_out.1 = bf16[16,16,5120]{2,1,0:T(8,128)(2,1)} custom-call(bf16[32,16,2048]{2,1,0:T(8,128)(2,1)} %all_to_all.11.q_ref, bf16[32,16,512]{2,1,0:T(8,128)(2,1)} %all_to_all.10.kv_ref), custom_call_target="tpu_custom_call" | custom-call | tf_op jit(solution)/shard_map/lay_out/pallas_call | solution.py:237
  (55 shorter events, 1.1 us)
Async XLA Ops:
  1.0 17.7 %collective-permute-start.12 = (bf16[128,512]{1,0:T(8,128)(2,1)S(1)}, bf16[128,512]{1,0:T(8,128)(2,1)S(1)}, u32[]{:S(2)}, u32[]{:S(2)}) collective-permute-start(bf16[128,512]{1,0:T(8,128)(2,1)S(1)} %pad_maximum_fusion.refs_0_), channel_id=1, source_target_pairs={{0,14},{2,0},{4,2},{6,4},{8,6},{10,8},{12,10},{14,12},{1,15},{3,1}... | collective-permute-start | bytes 393224 | tf_op jit(solution)/shard_map/ppermute | solution.py:31
  7.5 13.9 %collective-permute-start.1 = (bf16[128,512]{1,0:T(8,128)(2,1)S(1)}, bf16[128,512]{1,0:T(8,128)(2,1)S(1)}, u32[]{:S(2)}, u32[]{:S(2)}) collective-permute-start(bf16[128,512]{1,0:T(8,128)(2,1)S(1)} %pad_maximum_fusion.refs_0_), channel_id=1, source_target_pairs={{0,2},{2,4},{4,6},{6,8},{8,10},{10,12},{12,14},{14,0},{1,3},{3,5},... | collective-permute-start | bytes 393224 | tf_op jit(solution)/shard_map/ppermute | solution.py:31
  9.0 15.1 %collective-permute-start.18 = (s32[1,128]{1,0:T(1,128)S(1)}, s32[1,128]{1,0:T(1,128)S(1)}, u32[]{:S(2)}, u32[]{:S(2)}) collective-permute-start(s32[1,128]{1,0:T(1,128)S(1)} %bitcast_add_fusion.refs_22_.t_own), channel_id=1, source_target_pairs={{0,1},{1,0},{2,3},{3,2},{4,5},{5,4},{6,7},{7,6},{8,9},{9,8},{10,11... | collective-permute-start | bytes 1544 | tf_op jit(solution)/shard_map/ppermute | solution.py:35
  10.3 11.1 %collective-permute-start = (bf16[128,512]{1,0:T(8,128)(2,1)S(1)}, bf16[128,512]{1,0:T(8,128)(2,1)S(1)}, u32[]{:S(2)}, u32[]{:S(2)}) collective-permute-start(bf16[128,512]{1,0:T(8,128)(2,1)S(1)} %pad_maximum_fusion.1), channel_id=1, source_target_pairs={{0,1},{1,0},{2,3},{3,2},{4,5},{5,4},{6,7},{7,6},{8,9},{9,8},{10,11... | collective-permute-start | bytes 393224 | tf_op jit(solution)/shard_map/ppermute | solution.py:35
  12.7 27.8 %copy-start.2 = (s32[1,8]{1,0:T(1,128)S(1)}, s32[1,8]{1,0:T(1,128)}, u32[]{:S(2)}) copy-start(s32[1,8]{1,0:T(1,128)} %param.13) | copy-start | bytes 100
  12.7 28.0 %copy-start.1 = (s32[1,32,32]{2,1,0:T(8,128)S(1)}, s32[1,32,32]{2,1,0:T(8,128)}, u32[]{:S(2)}) copy-start(s32[1,32,32]{2,1,0:T(8,128)} %param.14) | copy-start | bytes 12292
  13.5 10.7 %collective-permute-start.17 = (f32[16,128]{1,0:T(8,128)S(1)}, f32[16,128]{1,0:T(8,128)S(1)}, u32[]{:S(2)}, u32[]{:S(2)}) collective-permute-start(f32[16,128]{1,0:T(8,128)S(1)} %bitcast.39), channel_id=1, source_target_pairs={{0,1},{1,0},{2,3},{3,2},{4,5},{5,4},{6,7},{7,6},{8,9},{9,8},{10,11... | collective-permute-start | bytes 24584 | tf_op jit(solution)/shard_map/ppermute | solution.py:35
  18.6 6.8 %collective-permute-start.13 = (bf16[128,512]{1,0:T(8,128)(2,1)S(1)}, bf16[128,512]{1,0:T(8,128)(2,1)S(1)}, u32[]{:S(2)}, u32[]{:S(2)}) collective-permute-start(bf16[128,512]{1,0:T(8,128)(2,1)S(1)} %collective-permute-done.12.refs_14_), channel_id=1, source_target_pairs={{0,14},{2,0},{4,2},{6,4},{8,6},{10,8},{12,10},{14,12},{1,15},{3,1}... | collective-permute-start | bytes 393224 | tf_op jit(solution)/shard_map/ppermute | solution.py:31
  21.3 5.0 %collective-permute-start.3 = (bf16[128,512]{1,0:T(8,128)(2,1)S(1)}, bf16[128,512]{1,0:T(8,128)(2,1)S(1)}, u32[]{:S(2)}, u32[]{:S(2)}) collective-permute-start(bf16[128,512]{1,0:T(8,128)(2,1)S(1)} %collective-permute-done.1.refs_2_), channel_id=1, source_target_pairs={{0,2},{2,4},{4,6},{6,8},{8,10},{10,12},{12,14},{14,0},{1,3},{3,5},... | collective-permute-start | bytes 393224 | tf_op jit(solution)/shard_map/ppermute | solution.py:31
  21.3 6.8 %collective-permute-start.8 = (bf16[128,512]{1,0:T(8,128)(2,1)S(1)}, bf16[128,512]{1,0:T(8,128)(2,1)S(1)}, u32[]{:S(2)}, u32[]{:S(2)}) collective-permute-start(bf16[128,512]{1,0:T(8,128)(2,1)S(1)} %collective-permute-done.refs_1_), channel_id=1, source_target_pairs={{0,14},{2,0},{4,2},{6,4},{8,6},{10,8},{12,10},{14,12},{1,15},{3,1}... | collective-permute-start | bytes 393224 | tf_op jit(solution)/shard_map/ppermute | solution.py:31
  24.0 21.3 %collective-permute-start.16 = (bf16[128,2048]{1,0:T(8,128)(2,1)}, bf16[128,2048]{1,0:T(8,128)(2,1)S(1)}, u32[]{:S(2)}, u32[]{:S(2)}) collective-permute-start(bf16[128,2048]{1,0:T(8,128)(2,1)} %dynamic-slice_bitcast_fusion), channel_id=1, source_target_pairs={{0,1},{1,0},{2,3},{3,2},{4,5},{5,4},{6,7},{7,6},{8,9},{9,8},{10,11... | collective-permute-start | bytes 1572872 | tf_op jit(solution)/shard_map/ppermute | solution.py:35
  24.2 21.8 %collective-permute-start.15 = (bf16[128,2048]{1,0:T(8,128)(2,1)}, bf16[128,2048]{1,0:T(8,128)(2,1)S(1)}, u32[]{:S(2)}, u32[]{:S(2)}) collective-permute-start(bf16[128,2048]{1,0:T(8,128)(2,1)} %dynamic-slice_bitcast_fusion.1), channel_id=1, source_target_pairs={{0,1},{1,0},{2,3},{3,2},{4,5},{5,4},{6,7},{7,6},{8,9},{9,8},{10,11... | collective-permute-start | bytes 1572872 | tf_op jit(solution)/shard_map/ppermute | solution.py:35
  25.5 5.1 %collective-permute-start.2 = (bf16[128,512]{1,0:T(8,128)(2,1)S(1)}, bf16[128,512]{1,0:T(8,128)(2,1)S(1)}, u32[]{:S(2)}, u32[]{:S(2)}) collective-permute-start(bf16[128,512]{1,0:T(8,128)(2,1)S(1)} %collective-permute-done.refs_1_), channel_id=1, source_target_pairs={{0,2},{2,4},{4,6},{6,8},{8,10},{10,12},{12,14},{14,0},{1,3},{3,5},... | collective-permute-start | bytes 393224 | tf_op jit(solution)/shard_map/ppermute | solution.py:31
  26.3 4.2 %collective-permute-start.14 = (bf16[128,512]{1,0:T(8,128)(2,1)S(1)}, bf16[128,512]{1,0:T(8,128)(2,1)S(1)}, u32[]{:S(2)}, u32[]{:S(2)}) collective-permute-start(bf16[128,512]{1,0:T(8,128)(2,1)S(1)} %collective-permute-done.13.refs_12_), channel_id=1, source_target_pairs={{0,14},{2,0},{4,2},{6,4},{8,6},{10,8},{12,10},{14,12},{1,15},{3,1}... | collective-permute-start | bytes 393224 | tf_op jit(solution)/shard_map/ppermute | solution.py:31
  28.2 4.2 %collective-permute-start.9 = (bf16[128,512]{1,0:T(8,128)(2,1)S(1)}, bf16[128,512]{1,0:T(8,128)(2,1)S(1)}, u32[]{:S(2)}, u32[]{:S(2)}) collective-permute-start(bf16[128,512]{1,0:T(8,128)(2,1)S(1)} %collective-permute-done.8.refs_15_), channel_id=1, source_target_pairs={{0,14},{2,0},{4,2},{6,4},{8,6},{10,8},{12,10},{14,12},{1,15},{3,1}... | collective-permute-start | bytes 393224 | tf_op jit(solution)/shard_map/ppermute | solution.py:31
  30.6 5.3 %collective-permute-start.5 = (bf16[128,512]{1,0:T(8,128)(2,1)S(1)}, bf16[128,512]{1,0:T(8,128)(2,1)S(1)}, u32[]{:S(2)}, u32[]{:S(2)}) collective-permute-start(bf16[128,512]{1,0:T(8,128)(2,1)S(1)} %collective-permute-done.3.refs_4_), channel_id=1, source_target_pairs={{0,2},{2,4},{4,6},{6,8},{8,10},{10,12},{12,14},{14,0},{1,3},{3,5},... | collective-permute-start | bytes 393224 | tf_op jit(solution)/shard_map/ppermute | solution.py:31
  30.6 6.7 %collective-permute-start.4 = (bf16[128,512]{1,0:T(8,128)(2,1)S(1)}, bf16[128,512]{1,0:T(8,128)(2,1)S(1)}, u32[]{:S(2)}, u32[]{:S(2)}) collective-permute-start(bf16[128,512]{1,0:T(8,128)(2,1)S(1)} %collective-permute-done.2.refs_3_), channel_id=1, source_target_pairs={{0,2},{2,4},{4,6},{6,8},{8,10},{10,12},{12,14},{14,0},{1,3},{3,5},... | collective-permute-start | bytes 393224 | tf_op jit(solution)/shard_map/ppermute | solution.py:31
  32.4 5.2 %collective-permute-start.10 = (bf16[128,512]{1,0:T(8,128)(2,1)S(1)}, bf16[128,512]{1,0:T(8,128)(2,1)S(1)}, u32[]{:S(2)}, u32[]{:S(2)}) collective-permute-start(bf16[128,512]{1,0:T(8,128)(2,1)S(1)} %collective-permute-done.9.refs_13_), channel_id=1, source_target_pairs={{0,14},{2,0},{4,2},{6,4},{8,6},{10,8},{12,10},{14,12},{1,15},{3,1}... | collective-permute-start | bytes 393224 | tf_op jit(solution)/shard_map/ppermute | solution.py:31
  35.8 6.7 %collective-permute-start.7 = (bf16[128,512]{1,0:T(8,128)(2,1)S(1)}, bf16[128,512]{1,0:T(8,128)(2,1)S(1)}, u32[]{:S(2)}, u32[]{:S(2)}) collective-permute-start(bf16[128,512]{1,0:T(8,128)(2,1)S(1)} %collective-permute-done.5.refs_6_), channel_id=1, source_target_pairs={{0,2},{2,4},{4,6},{6,8},{8,10},{10,12},{12,14},{14,0},{1,3},{3,5},... | collective-permute-start | bytes 393224 | tf_op jit(solution)/shard_map/ppermute | solution.py:31
  37.3 8.1 %collective-permute-start.6 = (bf16[128,512]{1,0:T(8,128)(2,1)S(1)}, bf16[128,512]{1,0:T(8,128)(2,1)S(1)}, u32[]{:S(2)}, u32[]{:S(2)}) collective-permute-start(bf16[128,512]{1,0:T(8,128)(2,1)S(1)} %collective-permute-done.4.refs_5_), channel_id=1, source_target_pairs={{0,2},{2,4},{4,6},{6,8},{8,10},{10,12},{12,14},{14,0},{1,3},{3,5},... | collective-permute-start | bytes 393224 | tf_op jit(solution)/shard_map/ppermute | solution.py:31
  37.6 8.3 %collective-permute-start.11 = (bf16[128,512]{1,0:T(8,128)(2,1)S(1)}, bf16[128,512]{1,0:T(8,128)(2,1)S(1)}, u32[]{:S(2)}, u32[]{:S(2)}) collective-permute-start(bf16[128,512]{1,0:T(8,128)(2,1)S(1)} %collective-permute-done.10.refs_11_), channel_id=1, source_target_pairs={{0,14},{2,0},{4,2},{6,4},{8,6},{10,8},{12,10},{14,12},{1,15},{3,1}... | collective-permute-start | bytes 393224 | tf_op jit(solution)/shard_map/ppermute | solution.py:31
  63.9 23.4 %collective-permute-start.19 = (bf16[128,512]{1,0:T(8,128)(2,1)S(1)}, bf16[128,512]{1,0:T(8,128)(2,1)S(1)}, u32[]{:S(2)}, u32[]{:S(2)}) collective-permute-start(bf16[128,512]{1,0:T(8,128)(2,1)S(1)} %get-tuple-element.25), channel_id=1, source_target_pairs={{0,14},{2,0},{4,2},{6,4},{8,6},{10,8},{12,10},{14,12},{1,15},{3,1}... | collective-permute-start | bytes 393224 | tf_op jit(solution)/shard_map/ppermute | solution.py:31
  64.4 25.8 %collective-permute-start.23 = (bf16[128,512]{1,0:T(8,128)(2,1)S(1)}, bf16[128,512]{1,0:T(8,128)(2,1)S(1)}, u32[]{:S(2)}, u32[]{:S(2)}) collective-permute-start(bf16[128,512]{1,0:T(8,128)(2,1)S(1)} %get-tuple-element.29), channel_id=1, source_target_pairs={{0,2},{2,4},{4,6},{6,8},{8,10},{10,12},{12,14},{14,0},{1,3},{3,5},... | collective-permute-start | bytes 393224 | tf_op jit(solution)/shard_map/ppermute | solution.py:31
  68.9 21.5 %collective-permute-start.26 = (bf16[128,512]{1,0:T(8,128)(2,1)S(1)}, bf16[128,512]{1,0:T(8,128)(2,1)S(1)}, u32[]{:S(2)}, u32[]{:S(2)}) collective-permute-start(bf16[128,512]{1,0:T(8,128)(2,1)S(1)} %get-tuple-element.32), channel_id=1, source_target_pairs={{0,14},{2,0},{4,2},{6,4},{8,6},{10,8},{12,10},{14,12},{1,15},{3,1}... | collective-permute-start | bytes 393224 | tf_op jit(solution)/shard_map/ppermute | solution.py:31
  87.3 6.6 %collective-permute-start.29 = (bf16[128,512]{1,0:T(8,128)(2,1)S(1)}, bf16[128,512]{1,0:T(8,128)(2,1)S(1)}, u32[]{:S(2)}, u32[]{:S(2)}) collective-permute-start(bf16[128,512]{1,0:T(8,128)(2,1)S(1)} %get-tuple-element.35), channel_id=1, source_target_pairs={{0,2},{2,4},{4,6},{6,8},{8,10},{10,12},{12,14},{14,0},{1,3},{3,5},... | collective-permute-start | bytes 393224 | tf_op jit(solution)/shard_map/ppermute | solution.py:31
  87.4 6.7 %collective-permute-start.20 = (bf16[128,512]{1,0:T(8,128)(2,1)S(1)}, bf16[128,512]{1,0:T(8,128)(2,1)S(1)}, u32[]{:S(2)}, u32[]{:S(2)}) collective-permute-start(bf16[128,512]{1,0:T(8,128)(2,1)S(1)} %add_convert_fusion.9), channel_id=1, source_target_pairs={{0,14},{2,0},{4,2},{6,4},{8,6},{10,8},{12,10},{14,12},{1,15},{3,1}... | collective-permute-start | bytes 393224 | tf_op jit(solution)/shard_map/ppermute | solution.py:31
  90.2 6.7 %collective-permute-start.24 = (bf16[128,512]{1,0:T(8,128)(2,1)S(1)}, bf16[128,512]{1,0:T(8,128)(2,1)S(1)}, u32[]{:S(2)}, u32[]{:S(2)}) collective-permute-start(bf16[128,512]{1,0:T(8,128)(2,1)S(1)} %add_convert_fusion.6), channel_id=1, source_target_pairs={{0,2},{2,4},{4,6},{6,8},{8,10},{10,12},{12,14},{14,0},{1,3},{3,5},... | collective-permute-start | bytes 393224 | tf_op jit(solution)/shard_map/ppermute | solution.py:31
  90.4 6.8 %collective-permute-start.27 = (bf16[128,512]{1,0:T(8,128)(2,1)S(1)}, bf16[128,512]{1,0:T(8,128)(2,1)S(1)}, u32[]{:S(2)}, u32[]{:S(2)}) collective-permute-start(bf16[128,512]{1,0:T(8,128)(2,1)S(1)} %add_convert_fusion.4), channel_id=1, source_target_pairs={{0,14},{2,0},{4,2},{6,4},{8,6},{10,8},{12,10},{14,12},{1,15},{3,1}... | collective-permute-start | bytes 393224 | tf_op jit(solution)/shard_map/ppermute | solution.py:31
  94.0 6.0 %collective-permute-start.30 = (bf16[128,512]{1,0:T(8,128)(2,1)S(1)}, bf16[128,512]{1,0:T(8,128)(2,1)S(1)}, u32[]{:S(2)}, u32[]{:S(2)}) collective-permute-start(bf16[128,512]{1,0:T(8,128)(2,1)S(1)} %add_convert_fusion.2), channel_id=1, source_target_pairs={{0,2},{2,4},{4,6},{6,8},{8,10},{10,12},{12,14},{14,0},{1,3},{3,5},... | collective-permute-start | bytes 393224 | tf_op jit(solution)/shard_map/ppermute | solution.py:31
  94.1 6.0 %collective-permute-start.21 = (bf16[128,512]{1,0:T(8,128)(2,1)S(1)}, bf16[128,512]{1,0:T(8,128)(2,1)S(1)}, u32[]{:S(2)}, u32[]{:S(2)}) collective-permute-start(bf16[128,512]{1,0:T(8,128)(2,1)S(1)} %add_convert_fusion.8), channel_id=1, source_target_pairs={{0,14},{2,0},{4,2},{6,4},{8,6},{10,8},{12,10},{14,12},{1,15},{3,1}... | collective-permute-start | bytes 393224 | tf_op jit(solution)/shard_map/ppermute | solution.py:31
  96.9 8.6 %collective-permute-start.25 = (bf16[128,512]{1,0:T(8,128)(2,1)S(1)}, bf16[128,512]{1,0:T(8,128)(2,1)S(1)}, u32[]{:S(2)}, u32[]{:S(2)}) collective-permute-start(bf16[128,512]{1,0:T(8,128)(2,1)S(1)} %add_convert_fusion.5), channel_id=1, source_target_pairs={{0,2},{2,4},{4,6},{6,8},{8,10},{10,12},{12,14},{14,0},{1,3},{3,5},... | collective-permute-start | bytes 393224 | tf_op jit(solution)/shard_map/ppermute | solution.py:31
  97.2 42.8 %copy-start = (bf16[512,2048]{1,0:T(8,128)(2,1)S(1)}, bf16[512,2048]{1,0:T(8,128)(2,1)}, u32[]{:S(2)}) copy-start(bf16[512,2048]{1,0:T(8,128)(2,1)} %get-tuple-element.22) | copy-start | bytes 6291460
  97.3 8.2 %collective-permute-start.28 = (bf16[128,512]{1,0:T(8,128)(2,1)S(1)}, bf16[128,512]{1,0:T(8,128)(2,1)S(1)}, u32[]{:S(2)}, u32[]{:S(2)}) collective-permute-start(bf16[128,512]{1,0:T(8,128)(2,1)S(1)} %add_convert_fusion.3), channel_id=1, source_target_pairs={{0,14},{2,0},{4,2},{6,4},{8,6},{10,8},{12,10},{14,12},{1,15},{3,1}... | collective-permute-start | bytes 393224 | tf_op jit(solution)/shard_map/ppermute | solution.py:31
  100.0 5.3 %collective-permute-start.31 = (bf16[128,512]{1,0:T(8,128)(2,1)S(1)}, bf16[128,512]{1,0:T(8,128)(2,1)S(1)}, u32[]{:S(2)}, u32[]{:S(2)}) collective-permute-start(bf16[128,512]{1,0:T(8,128)(2,1)S(1)} %add_convert_fusion.1), channel_id=1, source_target_pairs={{0,2},{2,4},{4,6},{6,8},{8,10},{10,12},{12,14},{14,0},{1,3},{3,5},... | collective-permute-start | bytes 393224 | tf_op jit(solution)/shard_map/ppermute | solution.py:31
  100.2 5.5 %collective-permute-start.22 = (bf16[128,512]{1,0:T(8,128)(2,1)S(1)}, bf16[128,512]{1,0:T(8,128)(2,1)S(1)}, u32[]{:S(2)}, u32[]{:S(2)}) collective-permute-start(bf16[128,512]{1,0:T(8,128)(2,1)S(1)} %add_convert_fusion.7), channel_id=1, source_target_pairs={{0,14},{2,0},{4,2},{6,4},{8,6},{10,8},{12,10},{14,12},{1,15},{3,1}... | collective-permute-start | bytes 393224 | tf_op jit(solution)/shard_map/ppermute | solution.py:31
  105.4 6.2 %collective-permute-start.32 = (bf16[128,512]{1,0:T(8,128)(2,1)S(1)}, bf16[128,512]{1,0:T(8,128)(2,1)S(1)}, u32[]{:S(2)}, u32[]{:S(2)}) collective-permute-start(bf16[128,512]{1,0:T(8,128)(2,1)S(1)} %add_convert_fusion), channel_id=1, source_target_pairs={{0,2},{2,4},{4,6},{6,8},{8,10},{10,12},{12,14},{14,0},{1,3},{3,5},... | collective-permute-start | bytes 393224 | tf_op jit(solution)/shard_map/ppermute | solution.py:31

commit v2 on v1

v2 whole, which is shorter than its diff:
```python
import math

import jax
import jax.numpy as jnp
from jax import lax
from jax.experimental import pallas as pl
from jax.experimental.pallas import tpu as pltpu
from jax.sharding import Mesh, PartitionSpec as P

H = 32
KV = 4
HD = 128
CAP = 16
N_DP = 16
NZ = 8
ROWS = 128
BLK = 2 * ROWS
HALF_Q = H * HD // 2
HALF_KV = KV * HD // 2
HEADS_KV = H // KV
STEP_HEADS = 8
CHUNK = STEP_HEADS * HD
WIDTH = STEP_HEADS * ROWS
STEPS = 2 * HALF_Q // CHUNK
SLOTS = N_DP * 2 * CAP
LAY_OUT = 4
NEG = -1e30
F32 = jnp.float32
BF16 = jnp.bfloat16
NT = (((1,), (1,)), ((), ()))
NN = (((1,), (0,)), ((), ()))


def zshift(x, by):
    return lax.ppermute(x, "z", [(i, (i + by) % NZ) for i in range(NZ)])


def yswap(x):
    return lax.ppermute(x, "yl", [(0, 1), (1, 0)])


def zshift_yswap(x, by):
    pairs = [(2 * i + y, 2 * ((i + by) % NZ) + 1 - y) for i in range(NZ) for y in range(2)]
    return lax.ppermute(x, ("z", "yl"), pairs)


def slots_of(extra, pair_place):
    owner = extra[3 * H // 2 : 3 * H // 2 + 1].astype(jnp.int32)
    return owner * (2 * CAP) + pair_place * CAP + extra[3 * H // 2 + 1 : 3 * H // 2 + 2].astype(jnp.int32)


def grads_kernel(where_ref, ends_ref, tiers_ref, *refs):
    keys_in = refs[0:16]
    q_own, q_par, g_own, g_par, extra_own, extra_par, packed_ref = refs[16:23]
    kv_out = refs[23:39]
    (kbuf, kt, sbuf, bias, acc, dqt, onehot, mx, den, deltas, active) = refs[39:]
    step = pl.program_id(0)
    half = step // (STEPS // 2)
    z = where_ref[0]
    y = where_ref[1]
    factor = HD**-0.5
    to_log2 = factor * math.log2(math.e)

    @pl.when(step == 0)
    def _prepare():
        acc[...] = jnp.zeros_like(acc)
        for r in range(NZ):
            kbuf[r, 0:ROWS, :] = keys_in[2 * r][...]
            kbuf[r, ROWS:BLK, :] = keys_in[2 * r + 1][...]
            for g in range(2):
                kt[r, g] = kbuf[r, :, g * HD : (g + 1) * HD].T

    @pl.when(step % (STEPS // 2) == 0)
    def _mask():
        extra = jnp.where(half == 0, extra_own[...], extra_par[...]).astype(F32).T
        deltas[...] = extra[0 : H // 2] + extra[H // 2 : H] + extra[H : 3 * H // 2]
        target = slots_of(extra, y ^ half)
        base = z * BLK + ROWS * (y ^ half)
        slot = lax.broadcasted_iota(jnp.int32, (SLOTS // 2, ROWS), 0)
        slot = (slot // CAP) * (2 * CAP) + (y ^ half) * CAP + slot % CAP
        onehot[...] = jnp.where(slot == target, 1.0, 0.0).astype(BF16)
        query_pos = base + lax.broadcasted_iota(jnp.int32, (1, ROWS), 1)
        first = jnp.zeros((1, ROWS), jnp.int32)
        last = jnp.full((1, ROWS), NZ * BLK, jnp.int32)
        low = jnp.int32(0)
        high = jnp.int32(NZ * BLK)
        for d in range(8):
            end = ends_ref[d]
            first = jnp.where(end <= query_pos, jnp.maximum(first, end), first)
            last = jnp.where(end > query_pos, jnp.minimum(last, end), last)
            low = jnp.where(end <= base, jnp.maximum(low, end), low)
            high = jnp.where(end > base + ROWS - 1, jnp.minimum(high, end), high)
        last = last - 1
        i_blk = 4 * z + 2 * (y ^ half)
        count = jnp.int32(0)
        for r in range(NZ):
            zb = (z - r) & (NZ - 1)
            needed = (zb * BLK < high) & (zb * BLK + BLK > low)
            active[count] = r
            count = count + needed.astype(jnp.int32)

            @pl.when(needed)
            def _block(r=r, zb=zb):
                for jb in range(4):
                    j_blk = zb * 4 + 2 * (y ^ (jb // 2)) + jb % 2
                    key_pos = j_blk * 64 + lax.broadcasted_iota(jnp.int32, (64, ROWS), 0)
                    tier = jnp.where(
                        lax.broadcasted_iota(jnp.int32, (1, ROWS), 1) < 64,
                        tiers_ref[i_blk * 32 + j_blk],
                        tiers_ref[(i_blk + 1) * 32 + j_blk],
                    )
                    reach = jnp.where(tier == 2, NZ * BLK, jnp.where(tier == 1, query_pos, -1))
                    ok = (key_pos >= first) & (key_pos <= jnp.minimum(reach, last))
                    bias[r, jb * 64 : (jb + 1) * 64, :] = jnp.where(ok, 0.0, NEG)

        active[NZ] = count

    kv_head = (step // (HEADS_KV // STEP_HEADS)) % 2
    n_active = active[NZ]
    own = half == 0
    q_all = jnp.where(own, q_own[...], q_par[...])
    g_all = jnp.where(own, g_own[...], g_par[...])
    q = jnp.concatenate([q_all[:, h * HD : (h + 1) * HD] for h in range(STEP_HEADS)], axis=0)
    g = jnp.concatenate([g_all[:, h * HD : (h + 1) * HD] for h in range(STEP_HEADS)], axis=0)
    head = (step % (STEPS // 2)) * STEP_HEADS
    delta = jnp.concatenate([deltas[pl.ds(head + h, 1), :] for h in range(STEP_HEADS)], axis=1)
    k_cols = pl.ds(pl.multiple_of(kv_head * HD, HD), HD)
    v_cols = pl.ds(pl.multiple_of(HALF_KV + kv_head * HD, HD), HD)
    mx[...] = jnp.full_like(mx, NEG)
    den[...] = jnp.zeros_like(den)
    dqt[...] = jnp.zeros_like(dqt)

    def score(n, carry):
        r = active[n]
        s = lax.dot_general(kbuf[r, :, k_cols], q, NT, preferred_element_type=F32)
        b = bias[r]
        s = s * to_log2 + jnp.concatenate([b] * STEP_HEADS, axis=1)
        sbuf[r] = s
        s = s.reshape(BLK // 8, 8, WIDTH)
        old = mx[...]
        new = jnp.maximum(old, jnp.max(s, axis=0))
        mx[...] = new
        den[...] = den[...] * jnp.exp2(old - new) + jnp.sum(jnp.exp2(s - new[None]), axis=0)
        return carry

    def score_pair(n, carry):
        score(2 * n, 0)
        score(2 * n + 1, 0)
        return carry

    lax.fori_loop(0, n_active // 2, score_pair, 0)

    @pl.when(n_active % 2 == 1)
    def _score_last():
        score(n_active - 1, 0)

    top = jnp.max(mx[...], axis=0, keepdims=True)
    lse = top + jnp.log2(jnp.sum(den[...] * jnp.exp2(mx[...] - top), axis=0, keepdims=True))

    def backward(n, carry):
        r = active[n]
        w = jnp.exp2(sbuf[r] - lse)
        dp = lax.dot_general(kbuf[r, :, v_cols], g, NT, preferred_element_type=F32)
        ds = (w * (dp - delta)).astype(BF16)
        acc[r, :, v_cols] += lax.dot_general(w.astype(BF16), g, NN, preferred_element_type=F32)
        acc[r, :, k_cols] += lax.dot_general(ds, q, NN, preferred_element_type=F32)
        dqt[...] += lax.dot_general(kt[r, kv_head], ds, NN, preferred_element_type=F32)
        return carry

    def backward_pair(n, carry):
        backward(2 * n, 0)
        backward(2 * n + 1, 0)
        return carry

    lax.fori_loop(0, n_active // 2, backward_pair, 0)

    @pl.when(n_active % 2 == 1)
    def _backward_last():
        backward(n_active - 1, 0)

    low_dq = (dqt[...] * factor).astype(BF16)
    for h in range(STEP_HEADS):
        packed_ref[:, 0, :, h * HD : (h + 1) * HD] = (
            lax.dot_general(onehot[...], low_dq[:, h * ROWS : (h + 1) * ROWS], NT, preferred_element_type=F32)
            .astype(BF16)
            .reshape(N_DP, CAP, HD)
        )

    @pl.when(step == STEPS - 1)
    def _finish():
        for r in range(NZ):
            for part in range(2):
                out = kv_out[2 * r + part]
                rows = slice(part * ROWS, (part + 1) * ROWS)
                out[:, :HALF_KV] = (acc[r, rows, :HALF_KV] * factor).astype(out.dtype)
                out[:, HALF_KV:] = acc[r, rows, HALF_KV:].astype(out.dtype)


def attention_grads(where, ends, tiers, keys, q_all, qg_par, g_all, extra_own):
    block = pl.BlockSpec((ROWS, 2 * HALF_KV), lambda c, where, ends, tiers: (0, 0))
    extra = pl.BlockSpec((ROWS, HD), lambda c, where, ends, tiers: (0, 0))
    extra_par = pl.BlockSpec((ROWS, HD), lambda c, where, ends, tiers: (0, 2 * HALF_Q // HD))
    per_half = STEPS // 2

    def own_at(c, where, ends, tiers):
        return 0, where[1] * per_half + jnp.minimum(c, per_half - 1)

    def partner_at(c, where, ends, tiers):
        return 0, jnp.maximum(c - per_half, 0)

    def partner_g_at(c, where, ends, tiers):
        return 0, per_half + jnp.maximum(c - per_half, 0)

    def out_at(c, where, ends, tiers):
        return 0, where[1] ^ (c // per_half), 0, c % per_half

    own = pl.BlockSpec((ROWS, CHUNK), own_at)
    partner = pl.BlockSpec((ROWS, CHUNK), partner_at)
    partner_g = pl.BlockSpec((ROWS, CHUNK), partner_g_at)
    kv_bf16 = jax.ShapeDtypeStruct((ROWS, 2 * HALF_KV), BF16)
    kv_f32 = jax.ShapeDtypeStruct((ROWS, 2 * HALF_KV), F32)
    return pl.pallas_call(
        grads_kernel,
        grid_spec=pltpu.PrefetchScalarGridSpec(
            num_scalar_prefetch=3,
            grid=(STEPS,),
            in_specs=[block] * 16 + [own, partner, own, partner_g, extra, extra_par],
            out_specs=[pl.BlockSpec((N_DP, 1, CAP, CHUNK), out_at)] + [block] * 16,
            scratch_shapes=[
                pltpu.VMEM((NZ, BLK, 2 * HALF_KV), BF16),
                pltpu.VMEM((NZ, 2, HD, BLK), BF16),
                pltpu.VMEM((NZ, BLK, WIDTH), F32),
                pltpu.VMEM((NZ, BLK, ROWS), F32),
                pltpu.VMEM((NZ, BLK, 2 * HALF_KV), F32),
                pltpu.VMEM((HD, WIDTH), F32),
                pltpu.VMEM((SLOTS // 2, ROWS), BF16),
                pltpu.VMEM((8, WIDTH), F32),
                pltpu.VMEM((8, WIDTH), F32),
                pltpu.VMEM((H // 2, ROWS), F32),
                pltpu.SMEM((NZ + 1,), jnp.int32),
            ],
        ),
        out_shape=[jax.ShapeDtypeStruct((N_DP, 2, CAP, HALF_Q), BF16)] + [kv_f32] * 2 + [kv_bf16] * 14,
        compiler_params=pltpu.CompilerParams(
            dimension_semantics=("arbitrary",), vmem_limit_bytes=56 * 1024 * 1024
        ),
        cost_estimate=pl.CostEstimate(flops=8 * 10**9, bytes_accessed=10 * 2**20, transcendentals=4 * 10**6),
        name="grads",
    )(where, ends, tiers, *keys, q_all, qg_par, g_all, qg_par, extra_own, qg_par)


def finish_kernel(where_ref, own_a, own_b, down_a, up_a, down_b, up_b, extra_own, extra_par, out):
    y = where_ref[1]
    target = jnp.concatenate(
        [slots_of(extra_own[...].astype(F32).T, y), slots_of(extra_par[...].astype(F32).T, 1 - y)], axis=1
    )
    slot = lax.broadcasted_iota(jnp.int32, (SLOTS, BLK), 0)
    onehot = jnp.where(slot == target, 1.0, 0.0).astype(BF16)
    a = own_a[...] + down_a[...].astype(F32) + up_a[...].astype(F32)
    b = own_b[...] + down_b[...].astype(F32) + up_b[...].astype(F32)
    rows = jnp.concatenate([a, b], axis=0).astype(BF16)
    out[...] = lax.dot_general(onehot, rows, NN, preferred_element_type=F32).astype(BF16)


def finish_rows(*operands):
    block = pl.BlockSpec((ROWS, 2 * HALF_KV), lambda c, where: (0, 0))
    extra = pl.BlockSpec((ROWS, HD), lambda c, where: (0, 0))
    extra_par = pl.BlockSpec((ROWS, HD), lambda c, where: (0, 2 * HALF_Q // HD))
    return pl.pallas_call(
        finish_kernel,
        grid_spec=pltpu.PrefetchScalarGridSpec(
            num_scalar_prefetch=1,
            grid=(1,),
            in_specs=[block] * 6 + [extra, extra_par],
            out_specs=pl.BlockSpec((SLOTS, 2 * HALF_KV), lambda c, where: (0, 0)),
        ),
        out_shape=jax.ShapeDtypeStruct((SLOTS, 2 * HALF_KV), BF16),
        compiler_params=pltpu.CompilerParams(vmem_limit_bytes=16 * 1024 * 1024),
        name="finish",
    )(*operands)


def lay_out_kernel(q_ref, kv_ref, out):
    first = pl.program_id(0) * LAY_OUT
    for n in range(LAY_OUT):
        for y in range(2):
            out[n, :, y * HALF_Q : (y + 1) * HALF_Q] = q_ref[2 * (first + n) + y]
            for part in range(2):
                start = 2 * HALF_Q + part * 2 * HALF_KV + y * HALF_KV
                out[n, :, start : start + HALF_KV] = kv_ref[2 * (first + n) + y, :, part * HALF_KV : (part + 1) * HALF_KV]


def lay_out(q_rows, kv_rows):
    width = 2 * HALF_Q + 4 * HALF_KV
    whole = pl.BlockSpec(memory_space=pltpu.VMEM)
    return pl.pallas_call(
        lay_out_kernel,
        grid=(N_DP // LAY_OUT,),
        in_specs=[whole, whole],
        out_specs=pl.BlockSpec((LAY_OUT, CAP, width), lambda n: (n, 0, 0)),
        out_shape=jax.ShapeDtypeStruct((N_DP, CAP, width), BF16),
        compiler_params=pltpu.CompilerParams(vmem_limit_bytes=16 * 1024 * 1024),
        name="lay_out",
    )(q_rows, kv_rows)


def add_low(a, b):
    return (a.astype(F32) + b.astype(F32)).astype(BF16)


def prepare_kernel(where_ref, q_half, g_all, out_all, owners_ref, send, extra_own):
    y = where_ref[0]
    lane = lax.broadcasted_iota(jnp.int32, (ROWS, HD), 1)
    row = lax.broadcasted_iota(jnp.int32, (ROWS, HD), 0)
    owners = jnp.broadcast_to(owners_ref[...].astype(F32), (ROWS, HD))
    earlier = (owners == owners.T) & (lane < row)
    slots = jnp.sum(jnp.where(earlier, 1.0, 0.0), axis=1, keepdims=True)
    head = lax.broadcasted_iota(jnp.int32, (HALF_Q, HD), 0) // HD
    pick = jnp.where(head == lax.broadcasted_iota(jnp.int32, (HALF_Q, HD), 1), 1.0, 0.0).astype(BF16)

    def extras(which):
        cols = pl.ds(pl.multiple_of(which * HALF_Q, HALF_Q), HALF_Q)
        product = g_all[:, cols].astype(F32) * out_all[:, cols].astype(F32)
        upper = product.astype(BF16)
        lower = (product - upper.astype(F32)).astype(BF16)
        delta = lax.dot_general(upper, pick, NN, preferred_element_type=F32)
        delta += lax.dot_general(lower, pick, NN, preferred_element_type=F32)
        high = delta.astype(BF16).astype(F32)
        middle = (delta - high).astype(BF16).astype(F32)
        low = delta - high - middle
        terms = high + pltpu.roll(middle, H // 2, 1) + pltpu.roll(low, H, 1)
        terms = jnp.where(lane == 3 * H // 2, owners, jnp.where(lane == 3 * H // 2 + 1, slots, terms))
        return terms.astype(BF16)

    send[:, :HALF_Q] = q_half[...]
    send[:, HALF_Q : 2 * HALF_Q] = g_all[:, pl.ds(pl.multiple_of((1 - y) * HALF_Q, HALF_Q), HALF_Q)]
    send[:, 2 * HALF_Q :] = extras(1 - y)
    extra_own[...] = extras(y)


def prepare(y, q_all, g_all, out_all, owners):
    width = 2 * HALF_Q + HD

    def whole(shape):
        return pl.BlockSpec(shape, lambda n, where: (0, 0))

    return pl.pallas_call(
        prepare_kernel,
        grid_spec=pltpu.PrefetchScalarGridSpec(
            num_scalar_prefetch=1,
            grid=(1,),
            in_specs=[
                pl.BlockSpec((ROWS, HALF_Q), lambda n, where: (0, 1 - where[0])),
                whole((ROWS, 2 * HALF_Q)),
                whole((ROWS, 2 * HALF_Q)),
                whole((ROWS, 1)),
            ],
            out_specs=[whole((ROWS, width)), whole((ROWS, HD))],
        ),
        out_shape=[jax.ShapeDtypeStruct((ROWS, width), BF16), jax.ShapeDtypeStruct((ROWS, HD), BF16)],
        compiler_params=pltpu.CompilerParams(vmem_limit_bytes=56 * 1024 * 1024),
        name="prepare",
    )(y[None], q_all, g_all, out_all, owners)


def per_device(queries, key_rows, value_rows, forward_out, out_grads, doc_lengths, mask_tiers, row_owners):
    z = lax.axis_index("z").astype(jnp.int32)
    y = lax.axis_index("yl").astype(jnp.int32)
    q_all, g_all = queries[0], out_grads[0]

    def half(x, which, width):
        return lax.dynamic_slice_in_dim(x, which * width, width, 1)

    def key_values(which):
        return jnp.concatenate(
            [half(key_rows[0], which, HALF_KV), half(value_rows[0], which, HALF_KV)], axis=1
        )

    a = key_values(y)
    b = key_values(1 - y)
    keys_a = {0: a, 1: zshift(a, 1), 7: zshift(a, -1)}
    keys_b = {0: yswap(b), 1: zshift_yswap(b, 1), 7: zshift_yswap(b, -1)}
    send, extra_own = prepare(y, q_all, g_all, forward_out[0], row_owners[0])
    send, keys_b[0] = lax.optimization_barrier((send, keys_b[0]))
    qg_par = yswap(send)
    for hop in range(2, 4):
        for held in (keys_a, keys_b):
            held[hop] = zshift(held[hop - 1], 1)
            held[NZ - hop] = zshift(held[NZ - hop + 1], -1)
    keys_a[4] = zshift(keys_a[3], 1)
    keys_b[4] = zshift(keys_b[5], -1)

    ends = jnp.cumsum(doc_lengths[0])

    where = jnp.stack([z, y])
    keys = []
    for r in range(NZ):
        keys += [keys_a[r], keys_b[r]]
    packed, own_a, own_b, *parts = attention_grads(
        where,
        ends,
        mask_tiers[0].reshape(-1),
        keys,
        q_all,
        qg_par,
        g_all,
        extra_own,
    )
    part_a = {r: parts[2 * (r - 1)] for r in range(1, NZ)}
    part_b = {r: parts[2 * (r - 1) + 1] for r in range(1, NZ)}

    down_a = zshift(part_a[4], -1)
    up_b = zshift(part_b[4], 1)
    for r in (3, 2, 1):
        down_a = zshift(add_low(down_a, part_a[r]), -1)
        up_b = zshift(add_low(up_b, part_b[NZ - r]), 1)
    down_b = zshift(part_b[3], -1)
    up_a = zshift(part_a[5], 1)
    for r in (2, 1):
        down_b = zshift(add_low(down_b, part_b[r]), -1)
        up_a = zshift(add_low(up_a, part_a[NZ - r]), 1)

    def to_owners(rows):
        return lax.all_to_all(
            rows.reshape(2 * N_DP, CAP, -1), ("dp", "yl"), split_axis=0, concat_axis=0, tiled=True
        )

    q_rows = to_owners(packed)
    kv_packed = finish_rows(where, own_a, own_b, down_a, up_a, down_b, up_b, extra_own, qg_par)
    kv_packed, q_rows = lax.optimization_barrier((kv_packed, q_rows))
    kv_rows = to_owners(kv_packed)
    return lay_out(q_rows, kv_rows)[None, None]


def solution(mesh):
    fine = Mesh(mesh.devices.reshape(N_DP, NZ, 2), ("dp", "z", "yl"))
    rows = P("dp", ("z", "yl"), None)
    return jax.shard_map(
        per_device,
        mesh=fine,
        in_specs=(rows, rows, rows, rows, rows, P("dp", None), P("dp", None, None), rows),
        out_specs=P("dp", ("z", "yl"), None, None, None),
        check_vma=False,
    )
```

time: 185 us -> 133 us (0.72); the launches traced: 183 us -> 134 us
  blocking collectives: 61.8 us -> 15.7 us
  starting transfers between devices: 64.7 us -> 61.5 us
  other arithmetic: 4.52 us -> 1.73 us
  Pallas kernels: 27.9 us -> 29.9 us
  waiting for transfers between devices: 18.8 us -> 20.8 us
    all_to_all x2 -> x1, blocking collectives: 61.8 us -> 15.7 us  [to_owners(): lax.all_to_all(rows.reshape(2 * N_DP, CAP, -1), ('dp', 'yl'), split_axis=...]
    ppermute x28 -> x26, starting transfers between devices: 60.3 us -> 34.4 us  [zshift(): return lax.ppermute(x, 'z', [(i, (i + by) % NZ) for i in range(NZ)])]
    all_to_all x0 -> x1, starting transfers between devices: none -> 18 us  [to_owners(): lax.all_to_all(rows.reshape(2 * N_DP, CAP, -1), ('dp', 'yl'), split_axis=...]
    all_to_all x0 -> x1, waiting for transfers between devices: none -> 9.08 us  [to_owners(): lax.all_to_all(rows.reshape(2 * N_DP, CAP, -1), ('dp', 'yl'), split_axis=...]
    ppermute x28 -> x26, waiting for transfers between devices: 18.1 us -> 9.37 us  [zshift(): return lax.ppermute(x, 'z', [(i, (i + by) % NZ) for i in range(NZ)])]
    ppermute x0 -> x2, starting transfers between devices: none -> 6.82 us  [zshift_yswap(): return lax.ppermute(x, ('z', 'yl'), pairs)]
    pallas_call x1, Pallas kernels: 18 us -> 23.3 us  [attention_grads(): pl.pallas_call(grads_kernel, grid_spec=pltpu.PrefetchScalarGridSpec(num_s...]
    dynamic_slice x3 -> x1, local copies, waits for them, and re-layouts: 4.74 us -> 0.98 us  [half(): return lax.dynamic_slice_in_dim(x, which * width, width, 1)]
  transfers between devices with their start and end apart: 33 -> 31, of which waited for: 13 -> 12; matrix products, arithmetic and copies ran while one was open for 5% -> 3% of each run, Pallas kernels for 0% -> 3%
where the time goes in v2:
time: 133 us; the launch traced here: 134 us
  starting transfers between devices  61.5 us (46%)
  Pallas kernels  29.9 us (22%)
  waiting for transfers between devices  20.8 us (16%)
  blocking collectives  15.7 us (12%)
  local copies, waits for them, and re-layouts  4.03 us (3%)
  other arithmetic  1.73 us (1%)
    ppermute x26, starting transfers between devices, zshift(): return lax.ppermute(x, 'z', [(i, (i + by) % NZ) for i in range(NZ)])  34.4 us
    pallas_call x1, Pallas kernels, attention_grads(): pl.pallas_call(grads_kernel, grid_spec=pltpu.PrefetchScalarGridSpec(num_s...  23.3 us
    all_to_all x1, starting transfers between devices, to_owners(): lax.all_to_all(rows.reshape(2 * N_DP, CAP, -1), ('dp', 'yl'), split_axis=...  18 us
    all_to_all x1, blocking collectives, to_owners(): lax.all_to_all(rows.reshape(2 * N_DP, CAP, -1), ('dp', 'yl'), split_axis=...  15.7 us
    ppermute x26, waiting for transfers between devices, zshift(): return lax.ppermute(x, 'z', [(i, (i + by) % NZ) for i in range(NZ)])  9.37 us
    all_to_all x1, waiting for transfers between devices, to_owners(): lax.all_to_all(rows.reshape(2 * N_DP, CAP, -1), ('dp', 'yl'), split_axis=...  9.08 us
    ppermute x2, starting transfers between devices, zshift_yswap(): return lax.ppermute(x, ('z', 'yl'), pairs)  6.82 us
    pallas_call x1, Pallas kernels, prepare(): pl.pallas_call(prepare_kernel, grid_spec=pltpu.PrefetchScalarGridSpec(num...  3.73 us
  transfers between devices with their start and end apart: 31, of which 12 were waited for; matrix products, arithmetic and copies ran while one was open for 3% of the time, Pallas kernels for 3%

profile of v2, /device:TPU:1, one launch (start us, length us, event | category | flops | bytes accessed | tf_op | source)
XLA Modules:
  0.0 134.3 jit_solution(10671128951777710393)
XLA Ops:
  0.0 1.0 dynamic-slice_bitcast_fusion
  1.0 2.2 %collective-permute-start = (bf16[128,512]{1,0:T(8,128)(2,1)S(1)}, bf16[128,512]{1,0:T(8,128)(2,1)S(1)}, u32[]{:S(2)}, u32[]{:S(2)}) collective-permute-start(bf16[128,512]{1,0:T(8,128)(2,1)S(1)} %pad_maximum_fusion.1), channel_id=1, source_target_pairs={{0,1},{1,0},{2,3},{3,2},{4,5},{5,4},{6,7},{7,6},{8,9},{9,8},{10,11... | collective-permute-start | bytes 393224 | tf_op jit(solution)/shard_map/ppermute | solution.py:39
  3.2 1.4 %copy.9.owners_ref = s32[128,1]{1,0:T(8,128)} copy(s32[128,1]{0,1:T(1,128)} %bitcast.26) | data formatting | bytes 1024 | tf_op jit(solution)/shard_map/squeeze | solution.py:383
  4.6 3.7 %prepare.1 = (bf16[128,4224]{1,0:T(8,128)(2,1)}, bf16[128,128]{1,0:T(8,128)(2,1)}) custom-call(s32[1]{0:T(128)} %bitcast.1.where_ref, bf16[128,4096]{1,0:T(8,128)(2,1)} %bitcast.22, bf16[128,4096]{1,0:T(8,128)(2,1)} %bitcast.24, bf16[128,4096]{1,0:T(8,128)(2,1)} %bitcast.21, s32[128,1]{1,0:T(8,128)} %copy.9.owners_ref), custom_call_target="tpu_custom_call" | custom-call | tf_op jit(solution)/shard_map/prepare/pallas_call | solution.py:347
  8.3 0.1 collective-permute-start.15
  8.4 6.7 %collective-permute-start.8 = (bf16[128,512]{1,0:T(8,128)(2,1)S(1)}, bf16[128,512]{1,0:T(8,128)(2,1)S(1)}, u32[]{:S(2)}, u32[]{:S(2)}) collective-permute-start(bf16[128,512]{1,0:T(8,128)(2,1)S(1)} %pad_maximum_fusion.1), channel_id=1, source_target_pairs={{0,15},{1,14},{2,1},{3,0},{4,3},{5,2},{6,5},{7,4},{8,7},{9,6},{10,... | collective-permute-start | bytes 393224 | tf_op jit(solution)/shard_map/ppermute | solution.py:44
  15.2 0.1 collective-permute-start.1
  15.3 0.1 collective-permute-start.2
  15.4 2.6 %collective-permute-start.12 = (bf16[128,512]{1,0:T(8,128)(2,1)S(1)}, bf16[128,512]{1,0:T(8,128)(2,1)S(1)}, u32[]{:S(2)}, u32[]{:S(2)}) collective-permute-start(bf16[128,512]{1,0:T(8,128)(2,1)S(1)} %pad_maximum_fusion.refs_0_), channel_id=1, source_target_pairs={{0,14},{2,0},{4,2},{6,4},{8,6},{10,8},{12,10},{14,12},{1,15},{3,1}... | collective-permute-start | bytes 393224 | tf_op jit(solution)/shard_map/ppermute | solution.py:35
  18.0 2.2 %collective-permute-start.9 = (bf16[128,512]{1,0:T(8,128)(2,1)S(1)}, bf16[128,512]{1,0:T(8,128)(2,1)S(1)}, u32[]{:S(2)}, u32[]{:S(2)}) collective-permute-start(bf16[128,512]{1,0:T(8,128)(2,1)S(1)} %collective-permute-done.8.refs_15_), channel_id=1, source_target_pairs={{0,14},{2,0},{4,2},{6,4},{8,6},{10,8},{12,10},{14,12},{1,15},{3,1}... | collective-permute-start | bytes 393224 | tf_op jit(solution)/shard_map/ppermute | solution.py:35
  20.2 0.1 collective-permute-done.1.refs_2_
  20.3 2.0 %collective-permute-done.2.refs_3_ = bf16[128,512]{1,0:T(8,128)(2,1)S(1)} collective-permute-done((bf16[128,512]{1,0:T(8,128)(2,1)S(1)}, bf16[128,512]{1,0:T(8,128)(2,1)S(1)}, u32[]{:S(2)}, u32[]{:S(2)}) %collective-permute-start.2) | collective-permute-done | bytes 131104 | tf_op jit(solution)/shard_map/ppermute | solution.py:44
  22.4 2.7 %collective-permute-start.13 = (bf16[128,512]{1,0:T(8,128)(2,1)S(1)}, bf16[128,512]{1,0:T(8,128)(2,1)S(1)}, u32[]{:S(2)}, u32[]{:S(2)}) collective-permute-start(bf16[128,512]{1,0:T(8,128)(2,1)S(1)} %collective-permute-done.12.refs_14_), channel_id=1, source_target_pairs={{0,14},{2,0},{4,2},{6,4},{8,6},{10,8},{12,10},{14,12},{1,15},{3,1}... | collective-permute-start | bytes 393224 | tf_op jit(solution)/shard_map/ppermute | solution.py:35
  25.1 1.9 %collective-permute-start.10 = (bf16[128,512]{1,0:T(8,128)(2,1)S(1)}, bf16[128,512]{1,0:T(8,128)(2,1)S(1)}, u32[]{:S(2)}, u32[]{:S(2)}) collective-permute-start(bf16[128,512]{1,0:T(8,128)(2,1)S(1)} %collective-permute-done.9.refs_13_), channel_id=1, source_target_pairs={{0,14},{2,0},{4,2},{6,4},{8,6},{10,8},{12,10},{14,12},{1,15},{3,1}... | collective-permute-start | bytes 393224 | tf_op jit(solution)/shard_map/ppermute | solution.py:35
  26.9 0.5 collective-permute-done.4.refs_5_
  27.4 2.7 %collective-permute-start.14 = (bf16[128,512]{1,0:T(8,128)(2,1)S(1)}, bf16[128,512]{1,0:T(8,128)(2,1)S(1)}, u32[]{:S(2)}, u32[]{:S(2)}) collective-permute-start(bf16[128,512]{1,0:T(8,128)(2,1)S(1)} %collective-permute-done.13.refs_12_), channel_id=1, source_target_pairs={{0,14},{2,0},{4,2},{6,4},{8,6},{10,8},{12,10},{14,12},{1,15},{3,1}... | collective-permute-start | bytes 393224 | tf_op jit(solution)/shard_map/ppermute | solution.py:35
  30.1 1.9 %collective-permute-start.11 = (bf16[128,512]{1,0:T(8,128)(2,1)S(1)}, bf16[128,512]{1,0:T(8,128)(2,1)S(1)}, u32[]{:S(2)}, u32[]{:S(2)}) collective-permute-start(bf16[128,512]{1,0:T(8,128)(2,1)S(1)} %collective-permute-done.10.refs_11_), channel_id=1, source_target_pairs={{0,14},{2,0},{4,2},{6,4},{8,6},{10,8},{12,10},{14,12},{1,15},{3,1}... | collective-permute-start | bytes 393224 | tf_op jit(solution)/shard_map/ppermute | solution.py:35
  32.0 0.2 collective-permute-done.5.refs_6_
  32.1 0.7 reshape_squeeze.3.tiers_ref
  32.8 0.7 reduce-window.9
  33.5 0.7 pad_add_fusion.where_ref
  34.2 0.6 collective-permute-done.11.refs_9_
  34.8 3.7 %collective-permute-done.7.refs_8_ = bf16[128,512]{1,0:T(8,128)(2,1)S(1)} collective-permute-done((bf16[128,512]{1,0:T(8,128)(2,1)S(1)}, bf16[128,512]{1,0:T(8,128)(2,1)S(1)}, u32[]{:S(2)}, u32[]{:S(2)}) %collective-permute-start.7) | collective-permute-done | bytes 131104 | tf_op jit(solution)/shard_map/ppermute | solution.py:35
  38.5 0.3 collective-permute-done.15.refs_17_.refs_19_.refs_21_.extra_par
  39.0 0.2 copy-done.32
  39.1 0.7 copy-done
  39.8 23.3 %grads.1 = (bf16[16,2,16,2048]{3,2,1,0:T(8,128)(2,1)}, f32[128,512]{1,0:T(8,128)}, f32[128,512]{1,0:T(8,128)}, bf16[128,512]{1,0:T(8,128)(2,1)}, bf16[128,512]{1...) custom-call(s32[2]{0:T(128)} %pad_add_fusion.where_ref, ...), custom_call_target="tpu_custom_call" | custom-call | flops 8000000000 | bytes 10485760 | tf_op jit(solution)/shard_map/grads/pallas_call | solution.py:222
  63.1 1.7 %collective-permute-start.26 = (bf16[128,512]{1,0:T(8,128)(2,1)}, bf16[128,512]{1,0:T(8,128)(2,1)S(1)}, u32[]{:S(2)}, u32[]{:S(2)}) collective-permute-start(bf16[128,512]{1,0:T(8,128)(2,1)} %get-tuple-element.44), channel_id=1, source_target_pairs={{0,2},{2,4},{4,6},{6,8},{8,10},{10,12},{12,14},{14,0},{1,3},{3,5},... | collective-permute-start | bytes 393224 | tf_op jit(solution)/shard_map/ppermute | solution.py:35
  64.8 1.0 collective-permute-start.23
  65.9 0.6 collective-permute-start.20
  66.5 2.1 %collective-permute-start.16 = (bf16[128,512]{1,0:T(8,128)(2,1)}, bf16[128,512]{1,0:T(8,128)(2,1)S(1)}, u32[]{:S(2)}, u32[]{:S(2)}) collective-permute-start(bf16[128,512]{1,0:T(8,128)(2,1)} %get-tuple-element.34), channel_id=1, source_target_pairs={{0,14},{2,0},{4,2},{6,4},{8,6},{10,8},{12,10},{14,12},{1,15},{3,1}... | collective-permute-start | bytes 393224 | tf_op jit(solution)/shard_map/ppermute | solution.py:35
  68.6 18.0 %all-to-all-start = ((bf16[32,16,2048]{2,1,0:T(8,128)(2,1)}), bf16[32,16,2048]{2,1,0:T(8,128)(2,1)S(1)}, u32[]{:S(2)}, u32[]{:S(2)}) async-start(bf16[32,16,2048]{2,1,0:T(8,128)(2,1)} %bitcast.20), calls=%async_computation | async-start | bytes 4194304 | tf_op jit(solution)/shard_map/all_to_all | solution.py:424
  86.7 0.1 collective-permute-start.27
  86.9 2.7 %collective-permute-start.24 = (bf16[128,512]{1,0:T(8,128)(2,1)S(1)}, bf16[128,512]{1,0:T(8,128)(2,1)S(1)}, u32[]{:S(2)}, u32[]{:S(2)}) collective-permute-start(bf16[128,512]{1,0:T(8,128)(2,1)S(1)} %add_convert_fusion.4), channel_id=1, source_target_pairs={{0,14},{2,0},{4,2},{6,4},{8,6},{10,8},{12,10},{14,12},{1,15},{3,1}... | collective-permute-start | bytes 393224 | tf_op jit(solution)/shard_map/ppermute | solution.py:35
  89.6 0.1 collective-permute-start.21
  89.8 2.9 %collective-permute-start.17 = (bf16[128,512]{1,0:T(8,128)(2,1)S(1)}, bf16[128,512]{1,0:T(8,128)(2,1)S(1)}, u32[]{:S(2)}, u32[]{:S(2)}) collective-permute-start(bf16[128,512]{1,0:T(8,128)(2,1)S(1)} %add_convert_fusion.9), channel_id=1, source_target_pairs={{0,14},{2,0},{4,2},{6,4},{8,6},{10,8},{12,10},{14,12},{1,15},{3,1}... | collective-permute-start | bytes 393224 | tf_op jit(solution)/shard_map/ppermute | solution.py:35
  92.7 0.1 collective-permute-done.27
  92.9 0.1 collective-permute-start.28
  93.1 2.7 %collective-permute-start.25 = (bf16[128,512]{1,0:T(8,128)(2,1)S(1)}, bf16[128,512]{1,0:T(8,128)(2,1)S(1)}, u32[]{:S(2)}, u32[]{:S(2)}) collective-permute-start(bf16[128,512]{1,0:T(8,128)(2,1)S(1)} %add_convert_fusion.3), channel_id=1, source_target_pairs={{0,14},{2,0},{4,2},{6,4},{8,6},{10,8},{12,10},{14,12},{1,15},{3,1}... | collective-permute-start | bytes 393224 | tf_op jit(solution)/shard_map/ppermute | solution.py:35
  96.0 2.7 %collective-permute-start.18 = (bf16[128,512]{1,0:T(8,128)(2,1)S(1)}, bf16[128,512]{1,0:T(8,128)(2,1)S(1)}, u32[]{:S(2)}, u32[]{:S(2)}) collective-permute-start(bf16[128,512]{1,0:T(8,128)(2,1)S(1)} %add_convert_fusion.8), channel_id=1, source_target_pairs={{0,14},{2,0},{4,2},{6,4},{8,6},{10,8},{12,10},{14,12},{1,15},{3,1}... | collective-permute-start | bytes 393224 | tf_op jit(solution)/shard_map/ppermute | solution.py:35
  98.8 2.2 %collective-permute-done.18 = bf16[128,512]{1,0:T(8,128)(2,1)S(1)} collective-permute-done((bf16[128,512]{1,0:T(8,128)(2,1)S(1)}, bf16[128,512]{1,0:T(8,128)(2,1)S(1)}, u32[]{:S(2)}, u32[]{:S(2)}) %collective-permute-start.18) | collective-permute-done | bytes 131104 | tf_op jit(solution)/shard_map/ppermute | solution.py:35
  101.1 3.5 %collective-permute-start.19 = (bf16[128,512]{1,0:T(8,128)(2,1)S(1)}, bf16[128,512]{1,0:T(8,128)(2,1)S(1)}, u32[]{:S(2)}, u32[]{:S(2)}) collective-permute-start(bf16[128,512]{1,0:T(8,128)(2,1)S(1)} %add_convert_fusion.7), channel_id=1, source_target_pairs={{0,14},{2,0},{4,2},{6,4},{8,6},{10,8},{12,10},{14,12},{1,15},{3,1}... | collective-permute-start | bytes 393224 | tf_op jit(solution)/shard_map/ppermute | solution.py:35
  104.6 0.3 collective-permute-done.29.up_b
  104.9 1.7 %collective-permute-done.19.down_a = bf16[128,512]{1,0:T(8,128)(2,1)S(1)} collective-permute-done((bf16[128,512]{1,0:T(8,128)(2,1)S(1)}, bf16[128,512]{1,0:T(8,128)(2,1)S(1)}, u32[]{:S(2)}, u32[]{:S(2)}) %collective-permute-start.19) | collective-permute-done | bytes 131104 | tf_op jit(solution)/shard_map/ppermute | solution.py:35
  106.6 0.9 finish.1
  107.5 9.1 %all-to-all-done.q_ref = bf16[32,16,2048]{2,1,0:T(8,128)(2,1)S(1)} async-done(((bf16[32,16,2048]{2,1,0:T(8,128)(2,1)}), bf16[32,16,2048]{2,1,0:T(8,128)(2,1)S(1)}, u32[]{:S(2)}, u32[]{:S(2)}) %all-to-all-start) | async-done | bytes 2097184 | tf_op jit(solution)/shard_map/all_to_all | solution.py:424
  116.6 15.7 %all_to_all.10.kv_ref = bf16[32,16,512]{2,1,0:T(8,128)(2,1)S(1)} all-to-all(bf16[32,16,512]{2,1,0:T(8,128)(2,1)S(1)} %bitcast.19), channel_id=1, replica_groups=mesh['dp'=16,'z'=8,'yl'=2] {'dp','yl'}, dimensions={0} | all-to-all | bytes 1048576 | tf_op jit(solution)/shard_map/all_to_all | solution.py:424
  132.3 2.0 %lay_out.1 = bf16[16,16,5120]{2,1,0:T(8,128)(2,1)} custom-call(bf16[32,16,2048]{2,1,0:T(8,128)(2,1)S(1)} %all-to-all-done.q_ref, bf16[32,16,512]{2,1,0:T(8,128)(2,1)S(1)} %all_to_all.10.kv_ref), custom_call_target="tpu_custom_call" | custom-call | tf_op jit(solution)/shard_map/lay_out/pallas_call | solution.py:296
  (104 shorter events, 0.7 us)
Async XLA Ops:
  0.0 32.1 %copy-start.17 = (s32[1,32,32]{2,1,0:T(8,128)S(1)}, s32[1,32,32]{2,1,0:T(8,128)}, u32[]{:S(2)}) copy-start(s32[1,32,32]{2,1,0:T(8,128)} %param.14) | copy-start | bytes 12292
  0.0 32.8 %copy-start.33 = (s32[1,8]{1,0:T(1,128)S(1)}, s32[1,8]{1,0:T(1,128)}, u32[]{:S(2)}) copy-start(s32[1,8]{1,0:T(1,128)} %param.13) | copy-start | bytes 100
  1.0 7.3 %collective-permute-start = (bf16[128,512]{1,0:T(8,128)(2,1)S(1)}, bf16[128,512]{1,0:T(8,128)(2,1)S(1)}, u32[]{:S(2)}, u32[]{:S(2)}) collective-permute-start(bf16[128,512]{1,0:T(8,128)(2,1)S(1)} %pad_maximum_fusion.1), channel_id=1, source_target_pairs={{0,1},{1,0},{2,3},{3,2},{4,5},{5,4},{6,7},{7,6},{8,9},{9,8},{10,11... | collective-permute-start | bytes 393224 | tf_op jit(solution)/shard_map/ppermute | solution.py:39
  8.3 30.5 %copy-start.18 = (bf16[128,512]{1,0:T(8,128)(2,1)}, bf16[128,512]{1,0:T(8,128)(2,1)S(1)}, u32[]{:S(2)}) copy-start(bf16[128,512]{1,0:T(8,128)(2,1)S(1)} %collective-permute-done.refs_1_) | copy-start | bytes 393220
  8.3 30.5 %collective-permute-start.15 = (bf16[128,4224]{1,0:T(8,128)(2,1)}, bf16[128,4224]{1,0:T(8,128)(2,1)S(1)}, u32[]{:S(2)}, u32[]{:S(2)}) collective-permute-start(bf16[128,4224]{1,0:T(8,128)(2,1)} %get-tuple-element.30), channel_id=1, source_target_pairs={{0,1},{1,0},{2,3},{3,2},{4,5},{5,4},{6,7},{7,6},{8,9},{9,8},{10,11... | collective-permute-start | bytes 3244040 | tf_op jit(solution)/shard_map/ppermute | solution.py:39
  8.4 9.5 %collective-permute-start.8 = (bf16[128,512]{1,0:T(8,128)(2,1)S(1)}, bf16[128,512]{1,0:T(8,128)(2,1)S(1)}, u32[]{:S(2)}, u32[]{:S(2)}) collective-permute-start(bf16[128,512]{1,0:T(8,128)(2,1)S(1)} %pad_maximum_fusion.1), channel_id=1, source_target_pairs={{0,15},{1,14},{2,1},{3,0},{4,3},{5,2},{6,5},{7,4},{8,7},{9,6},{10,... | collective-permute-start | bytes 393224 | tf_op jit(solution)/shard_map/ppermute | solution.py:44
  15.2 23.6 %copy-start.16 = (bf16[128,512]{1,0:T(8,128)(2,1)}, bf16[128,512]{1,0:T(8,128)(2,1)S(1)}, u32[]{:S(2)}) copy-start(bf16[128,512]{1,0:T(8,128)(2,1)S(1)} %pad_maximum_fusion.refs_0_) | copy-start | bytes 393220
  15.2 5.1 %collective-permute-start.1 = (bf16[128,512]{1,0:T(8,128)(2,1)S(1)}, bf16[128,512]{1,0:T(8,128)(2,1)S(1)}, u32[]{:S(2)}, u32[]{:S(2)}) collective-permute-start(bf16[128,512]{1,0:T(8,128)(2,1)S(1)} %pad_maximum_fusion.refs_0_), channel_id=1, source_target_pairs={{0,2},{2,4},{4,6},{6,8},{8,10},{10,12},{12,14},{14,0},{1,3},{3,5},... | collective-permute-start | bytes 393224 | tf_op jit(solution)/shard_map/ppermute | solution.py:35
  15.3 7.1 %collective-permute-start.2 = (bf16[128,512]{1,0:T(8,128)(2,1)S(1)}, bf16[128,512]{1,0:T(8,128)(2,1)S(1)}, u32[]{:S(2)}, u32[]{:S(2)}) collective-permute-start(bf16[128,512]{1,0:T(8,128)(2,1)S(1)} %pad_maximum_fusion.1), channel_id=1, source_target_pairs={{0,3},{1,2},{2,5},{3,4},{4,7},{5,6},{6,9},{7,8},{8,11},{9,10},{10,... | collective-permute-start | bytes 393224 | tf_op jit(solution)/shard_map/ppermute | solution.py:44
  15.4 7.0 %collective-permute-start.12 = (bf16[128,512]{1,0:T(8,128)(2,1)S(1)}, bf16[128,512]{1,0:T(8,128)(2,1)S(1)}, u32[]{:S(2)}, u32[]{:S(2)}) collective-permute-start(bf16[128,512]{1,0:T(8,128)(2,1)S(1)} %pad_maximum_fusion.refs_0_), channel_id=1, source_target_pairs={{0,14},{2,0},{4,2},{6,4},{8,6},{10,8},{12,10},{14,12},{1,15},{3,1}... | collective-permute-start | bytes 393224 | tf_op jit(solution)/shard_map/ppermute | solution.py:35
  18.0 20.9 %copy-start.19 = (bf16[128,512]{1,0:T(8,128)(2,1)}, bf16[128,512]{1,0:T(8,128)(2,1)S(1)}, u32[]{:S(2)}) copy-start(bf16[128,512]{1,0:T(8,128)(2,1)S(1)} %collective-permute-done.8.refs_15_) | copy-start | bytes 393220
  18.0 7.1 %collective-permute-start.9 = (bf16[128,512]{1,0:T(8,128)(2,1)S(1)}, bf16[128,512]{1,0:T(8,128)(2,1)S(1)}, u32[]{:S(2)}, u32[]{:S(2)}) collective-permute-start(bf16[128,512]{1,0:T(8,128)(2,1)S(1)} %collective-permute-done.8.refs_15_), channel_id=1, source_target_pairs={{0,14},{2,0},{4,2},{6,4},{8,6},{10,8},{12,10},{14,12},{1,15},{3,1}... | collective-permute-start | bytes 393224 | tf_op jit(solution)/shard_map/ppermute | solution.py:35
  20.3 18.5 %copy-start.20 = (bf16[128,512]{1,0:T(8,128)(2,1)}, bf16[128,512]{1,0:T(8,128)(2,1)S(1)}, u32[]{:S(2)}) copy-start(bf16[128,512]{1,0:T(8,128)(2,1)S(1)} %collective-permute-done.1.refs_2_) | copy-start | bytes 393220
  20.3 6.6 %collective-permute-start.3 = (bf16[128,512]{1,0:T(8,128)(2,1)S(1)}, bf16[128,512]{1,0:T(8,128)(2,1)S(1)}, u32[]{:S(2)}, u32[]{:S(2)}) collective-permute-start(bf16[128,512]{1,0:T(8,128)(2,1)S(1)} %collective-permute-done.1.refs_2_), channel_id=1, source_target_pairs={{0,2},{2,4},{4,6},{6,8},{8,10},{10,12},{12,14},{14,0},{1,3},{3,5},... | collective-permute-start | bytes 393224 | tf_op jit(solution)/shard_map/ppermute | solution.py:35
  22.4 5.0 %collective-permute-start.4 = (bf16[128,512]{1,0:T(8,128)(2,1)S(1)}, bf16[128,512]{1,0:T(8,128)(2,1)S(1)}, u32[]{:S(2)}, u32[]{:S(2)}) collective-permute-start(bf16[128,512]{1,0:T(8,128)(2,1)S(1)} %collective-permute-done.2.refs_3_), channel_id=1, source_target_pairs={{0,2},{2,4},{4,6},{6,8},{8,10},{10,12},{12,14},{14,0},{1,3},{3,5},... | collective-permute-start | bytes 393224 | tf_op jit(solution)/shard_map/ppermute | solution.py:35
  22.4 5.0 %collective-permute-start.13 = (bf16[128,512]{1,0:T(8,128)(2,1)S(1)}, bf16[128,512]{1,0:T(8,128)(2,1)S(1)}, u32[]{:S(2)}, u32[]{:S(2)}) collective-permute-start(bf16[128,512]{1,0:T(8,128)(2,1)S(1)} %collective-permute-done.12.refs_14_), channel_id=1, source_target_pairs={{0,14},{2,0},{4,2},{6,4},{8,6},{10,8},{12,10},{14,12},{1,15},{3,1}... | collective-permute-start | bytes 393224 | tf_op jit(solution)/shard_map/ppermute | solution.py:35
  25.1 5.0 %collective-permute-start.10 = (bf16[128,512]{1,0:T(8,128)(2,1)S(1)}, bf16[128,512]{1,0:T(8,128)(2,1)S(1)}, u32[]{:S(2)}, u32[]{:S(2)}) collective-permute-start(bf16[128,512]{1,0:T(8,128)(2,1)S(1)} %collective-permute-done.9.refs_13_), channel_id=1, source_target_pairs={{0,14},{2,0},{4,2},{6,4},{8,6},{10,8},{12,10},{14,12},{1,15},{3,1}... | collective-permute-start | bytes 393224 | tf_op jit(solution)/shard_map/ppermute | solution.py:35
  26.9 5.2 %collective-permute-start.5 = (bf16[128,512]{1,0:T(8,128)(2,1)S(1)}, bf16[128,512]{1,0:T(8,128)(2,1)S(1)}, u32[]{:S(2)}, u32[]{:S(2)}) collective-permute-start(bf16[128,512]{1,0:T(8,128)(2,1)S(1)} %collective-permute-done.3.refs_4_), channel_id=1, source_target_pairs={{0,2},{2,4},{4,6},{6,8},{8,10},{10,12},{12,14},{14,0},{1,3},{3,5},... | collective-permute-start | bytes 393224 | tf_op jit(solution)/shard_map/ppermute | solution.py:35
  27.4 6.8 %collective-permute-start.6 = (bf16[128,512]{1,0:T(8,128)(2,1)S(1)}, bf16[128,512]{1,0:T(8,128)(2,1)S(1)}, u32[]{:S(2)}, u32[]{:S(2)}) collective-permute-start(bf16[128,512]{1,0:T(8,128)(2,1)S(1)} %collective-permute-done.4.refs_5_), channel_id=1, source_target_pairs={{0,2},{2,4},{4,6},{6,8},{8,10},{10,12},{12,14},{14,0},{1,3},{3,5},... | collective-permute-start | bytes 393224 | tf_op jit(solution)/shard_map/ppermute | solution.py:35
  27.4 6.7 %collective-permute-start.14 = (bf16[128,512]{1,0:T(8,128)(2,1)S(1)}, bf16[128,512]{1,0:T(8,128)(2,1)S(1)}, u32[]{:S(2)}, u32[]{:S(2)}) collective-permute-start(bf16[128,512]{1,0:T(8,128)(2,1)S(1)} %collective-permute-done.13.refs_12_), channel_id=1, source_target_pairs={{0,14},{2,0},{4,2},{6,4},{8,6},{10,8},{12,10},{14,12},{1,15},{3,1}... | collective-permute-start | bytes 393224 | tf_op jit(solution)/shard_map/ppermute | solution.py:35
  30.1 4.7 %collective-permute-start.11 = (bf16[128,512]{1,0:T(8,128)(2,1)S(1)}, bf16[128,512]{1,0:T(8,128)(2,1)S(1)}, u32[]{:S(2)}, u32[]{:S(2)}) collective-permute-start(bf16[128,512]{1,0:T(8,128)(2,1)S(1)} %collective-permute-done.10.refs_11_), channel_id=1, source_target_pairs={{0,14},{2,0},{4,2},{6,4},{8,6},{10,8},{12,10},{14,12},{1,15},{3,1}... | collective-permute-start | bytes 393224 | tf_op jit(solution)/shard_map/ppermute | solution.py:35
  32.1 6.4 %collective-permute-start.7 = (bf16[128,512]{1,0:T(8,128)(2,1)S(1)}, bf16[128,512]{1,0:T(8,128)(2,1)S(1)}, u32[]{:S(2)}, u32[]{:S(2)}) collective-permute-start(bf16[128,512]{1,0:T(8,128)(2,1)S(1)} %collective-permute-done.5.refs_6_), channel_id=1, source_target_pairs={{0,2},{2,4},{4,6},{6,8},{8,10},{10,12},{12,14},{14,0},{1,3},{3,5},... | collective-permute-start | bytes 393224 | tf_op jit(solution)/shard_map/ppermute | solution.py:35
  63.1 23.5 %collective-permute-start.26 = (bf16[128,512]{1,0:T(8,128)(2,1)}, bf16[128,512]{1,0:T(8,128)(2,1)S(1)}, u32[]{:S(2)}, u32[]{:S(2)}) collective-permute-start(bf16[128,512]{1,0:T(8,128)(2,1)} %get-tuple-element.44), channel_id=1, source_target_pairs={{0,2},{2,4},{4,6},{6,8},{8,10},{10,12},{12,14},{14,0},{1,3},{3,5},... | collective-permute-start | bytes 393224 | tf_op jit(solution)/shard_map/ppermute | solution.py:35
  64.8 22.0 %collective-permute-start.23 = (bf16[128,512]{1,0:T(8,128)(2,1)}, bf16[128,512]{1,0:T(8,128)(2,1)S(1)}, u32[]{:S(2)}, u32[]{:S(2)}) collective-permute-start(bf16[128,512]{1,0:T(8,128)(2,1)} %get-tuple-element.41), channel_id=1, source_target_pairs={{0,14},{2,0},{4,2},{6,4},{8,6},{10,8},{12,10},{14,12},{1,15},{3,1}... | collective-permute-start | bytes 393224 | tf_op jit(solution)/shard_map/ppermute | solution.py:35
  65.9 23.7 %collective-permute-start.20 = (bf16[128,512]{1,0:T(8,128)(2,1)}, bf16[128,512]{1,0:T(8,128)(2,1)S(1)}, u32[]{:S(2)}, u32[]{:S(2)}) collective-permute-start(bf16[128,512]{1,0:T(8,128)(2,1)} %get-tuple-element.38), channel_id=1, source_target_pairs={{0,2},{2,4},{4,6},{6,8},{8,10},{10,12},{12,14},{14,0},{1,3},{3,5},... | collective-permute-start | bytes 393224 | tf_op jit(solution)/shard_map/ppermute | solution.py:35
  66.5 23.2 %collective-permute-start.16 = (bf16[128,512]{1,0:T(8,128)(2,1)}, bf16[128,512]{1,0:T(8,128)(2,1)S(1)}, u32[]{:S(2)}, u32[]{:S(2)}) collective-permute-start(bf16[128,512]{1,0:T(8,128)(2,1)} %get-tuple-element.34), channel_id=1, source_target_pairs={{0,14},{2,0},{4,2},{6,4},{8,6},{10,8},{12,10},{14,12},{1,15},{3,1}... | collective-permute-start | bytes 393224 | tf_op jit(solution)/shard_map/ppermute | solution.py:35
  68.5 18.1 %copy-start.15 = (bf16[128,512]{1,0:T(8,128)(2,1)S(1)}, bf16[128,512]{1,0:T(8,128)(2,1)}, u32[]{:S(2)}) copy-start(bf16[128,512]{1,0:T(8,128)(2,1)} %get-tuple-element.45) | copy-start | bytes 393220
  68.5 18.3 %copy-start.14 = (bf16[128,512]{1,0:T(8,128)(2,1)S(1)}, bf16[128,512]{1,0:T(8,128)(2,1)}, u32[]{:S(2)}) copy-start(bf16[128,512]{1,0:T(8,128)(2,1)} %get-tuple-element.42) | copy-start | bytes 393220
  68.5 21.0 %copy-start.13 = (bf16[128,512]{1,0:T(8,128)(2,1)S(1)}, bf16[128,512]{1,0:T(8,128)(2,1)}, u32[]{:S(2)}) copy-start(bf16[128,512]{1,0:T(8,128)(2,1)} %get-tuple-element.39) | copy-start | bytes 393220
  68.5 21.2 %copy-start.12 = (bf16[128,512]{1,0:T(8,128)(2,1)S(1)}, bf16[128,512]{1,0:T(8,128)(2,1)}, u32[]{:S(2)}) copy-start(bf16[128,512]{1,0:T(8,128)(2,1)} %get-tuple-element.35) | copy-start | bytes 393220
  68.5 24.3 %copy-start.11 = (bf16[128,512]{1,0:T(8,128)(2,1)S(1)}, bf16[128,512]{1,0:T(8,128)(2,1)}, u32[]{:S(2)}) copy-start(bf16[128,512]{1,0:T(8,128)(2,1)} %get-tuple-element.46) | copy-start | bytes 393220
  68.6 24.4 %copy-start.10 = (bf16[128,512]{1,0:T(8,128)(2,1)S(1)}, bf16[128,512]{1,0:T(8,128)(2,1)}, u32[]{:S(2)}) copy-start(bf16[128,512]{1,0:T(8,128)(2,1)} %get-tuple-element.43) | copy-start | bytes 393220
  68.6 48.0 %all-to-all-start = ((bf16[32,16,2048]{2,1,0:T(8,128)(2,1)}), bf16[32,16,2048]{2,1,0:T(8,128)(2,1)S(1)}, u32[]{:S(2)}, u32[]{:S(2)}) async-start(bf16[32,16,2048]{2,1,0:T(8,128)(2,1)} %bitcast.20), calls=%async_computation | async-start | bytes 4194304 | tf_op jit(solution)/shard_map/all_to_all | solution.py:424
  86.6 19.9 %copy-start.1 = (bf16[128,4224]{1,0:T(8,128)(2,1)S(1)}, bf16[128,4224]{1,0:T(8,128)(2,1)}, u32[]{:S(2)}) copy-start(bf16[128,4224]{1,0:T(8,128)(2,1)} %copy-done) | copy-start | bytes 3244036
  86.6 19.9 %copy-start.2 = (f32[128,512]{1,0:T(8,128)S(1)}, f32[128,512]{1,0:T(8,128)}, u32[]{:S(2)}) copy-start(f32[128,512]{1,0:T(8,128)} %get-tuple-element.32.own_a) | copy-start | bytes 786436
  86.6 19.9 %copy-start.3 = (f32[128,512]{1,0:T(8,128)S(1)}, f32[128,512]{1,0:T(8,128)}, u32[]{:S(2)}) copy-start(f32[128,512]{1,0:T(8,128)} %get-tuple-element.33.own_b) | copy-start | bytes 786436
  86.6 19.9 %copy-start.4 = (bf16[128,128]{1,0:T(8,128)(2,1)S(1)}, bf16[128,128]{1,0:T(8,128)(2,1)}, u32[]{:S(2)}) copy-start(bf16[128,128]{1,0:T(8,128)(2,1)} %get-tuple-element.31.refs_20_.extra_own) | copy-start | bytes 98308
  86.6 19.9 %copy-start.5 = (s32[2]{0:T(128)S(1)}, s32[2]{0:T(128)}, u32[]{:S(2)}) copy-start(s32[2]{0:T(128)} %pad_add_fusion.where_ref) | copy-start | bytes 28
  86.7 6.2 %collective-permute-start.27 = (bf16[128,512]{1,0:T(8,128)(2,1)S(1)}, bf16[128,512]{1,0:T(8,128)(2,1)S(1)}, u32[]{:S(2)}, u32[]{:S(2)}) collective-permute-start(bf16[128,512]{1,0:T(8,128)(2,1)S(1)} %add_convert_fusion.2), channel_id=1, source_target_pairs={{0,2},{2,4},{4,6},{6,8},{8,10},{10,12},{12,14},{14,0},{1,3},{3,5},... | collective-permute-start | bytes 393224 | tf_op jit(solution)/shard_map/ppermute | solution.py:35
  86.9 6.1 %collective-permute-start.24 = (bf16[128,512]{1,0:T(8,128)(2,1)S(1)}, bf16[128,512]{1,0:T(8,128)(2,1)S(1)}, u32[]{:S(2)}, u32[]{:S(2)}) collective-permute-start(bf16[128,512]{1,0:T(8,128)(2,1)S(1)} %add_convert_fusion.4), channel_id=1, source_target_pairs={{0,14},{2,0},{4,2},{6,4},{8,6},{10,8},{12,10},{14,12},{1,15},{3,1}... | collective-permute-start | bytes 393224 | tf_op jit(solution)/shard_map/ppermute | solution.py:35
  89.6 6.2 %collective-permute-start.21 = (bf16[128,512]{1,0:T(8,128)(2,1)S(1)}, bf16[128,512]{1,0:T(8,128)(2,1)S(1)}, u32[]{:S(2)}, u32[]{:S(2)}) collective-permute-start(bf16[128,512]{1,0:T(8,128)(2,1)S(1)} %add_convert_fusion.6), channel_id=1, source_target_pairs={{0,2},{2,4},{4,6},{6,8},{8,10},{10,12},{12,14},{14,0},{1,3},{3,5},... | collective-permute-start | bytes 393224 | tf_op jit(solution)/shard_map/ppermute | solution.py:35
  89.8 6.1 %collective-permute-start.17 = (bf16[128,512]{1,0:T(8,128)(2,1)S(1)}, bf16[128,512]{1,0:T(8,128)(2,1)S(1)}, u32[]{:S(2)}, u32[]{:S(2)}) collective-permute-start(bf16[128,512]{1,0:T(8,128)(2,1)S(1)} %add_convert_fusion.9), channel_id=1, source_target_pairs={{0,14},{2,0},{4,2},{6,4},{8,6},{10,8},{12,10},{14,12},{1,15},{3,1}... | collective-permute-start | bytes 393224 | tf_op jit(solution)/shard_map/ppermute | solution.py:35
  92.9 5.8 %collective-permute-start.28 = (bf16[128,512]{1,0:T(8,128)(2,1)S(1)}, bf16[128,512]{1,0:T(8,128)(2,1)S(1)}, u32[]{:S(2)}, u32[]{:S(2)}) collective-permute-start(bf16[128,512]{1,0:T(8,128)(2,1)S(1)} %add_convert_fusion.1), channel_id=1, source_target_pairs={{0,2},{2,4},{4,6},{6,8},{8,10},{10,12},{12,14},{14,0},{1,3},{3,5},... | collective-permute-start | bytes 393224 | tf_op jit(solution)/shard_map/ppermute | solution.py:35
  93.1 11.5 %collective-permute-start.25 = (bf16[128,512]{1,0:T(8,128)(2,1)S(1)}, bf16[128,512]{1,0:T(8,128)(2,1)S(1)}, u32[]{:S(2)}, u32[]{:S(2)}) collective-permute-start(bf16[128,512]{1,0:T(8,128)(2,1)S(1)} %add_convert_fusion.3), channel_id=1, source_target_pairs={{0,14},{2,0},{4,2},{6,4},{8,6},{10,8},{12,10},{14,12},{1,15},{3,1}... | collective-permute-start | bytes 393224 | tf_op jit(solution)/shard_map/ppermute | solution.py:35
  95.8 8.8 %collective-permute-start.22 = (bf16[128,512]{1,0:T(8,128)(2,1)S(1)}, bf16[128,512]{1,0:T(8,128)(2,1)S(1)}, u32[]{:S(2)}, u32[]{:S(2)}) collective-permute-start(bf16[128,512]{1,0:T(8,128)(2,1)S(1)} %add_convert_fusion.5), channel_id=1, source_target_pairs={{0,2},{2,4},{4,6},{6,8},{8,10},{10,12},{12,14},{14,0},{1,3},{3,5},... | collective-permute-start | bytes 393224 | tf_op jit(solution)/shard_map/ppermute | solution.py:35
  96.0 5.1 %collective-permute-start.18 = (bf16[128,512]{1,0:T(8,128)(2,1)S(1)}, bf16[128,512]{1,0:T(8,128)(2,1)S(1)}, u32[]{:S(2)}, u32[]{:S(2)}) collective-permute-start(bf16[128,512]{1,0:T(8,128)(2,1)S(1)} %add_convert_fusion.8), channel_id=1, source_target_pairs={{0,14},{2,0},{4,2},{6,4},{8,6},{10,8},{12,10},{14,12},{1,15},{3,1}... | collective-permute-start | bytes 393224 | tf_op jit(solution)/shard_map/ppermute | solution.py:35
  98.7 6.1 %collective-permute-start.29 = (bf16[128,512]{1,0:T(8,128)(2,1)S(1)}, bf16[128,512]{1,0:T(8,128)(2,1)S(1)}, u32[]{:S(2)}, u32[]{:S(2)}) collective-permute-start(bf16[128,512]{1,0:T(8,128)(2,1)S(1)} %add_convert_fusion), channel_id=1, source_target_pairs={{0,2},{2,4},{4,6},{6,8},{8,10},{10,12},{12,14},{14,0},{1,3},{3,5},... | collective-permute-start | bytes 393224 | tf_op jit(solution)/shard_map/ppermute | solution.py:35
  101.1 5.4 %collective-permute-start.19 = (bf16[128,512]{1,0:T(8,128)(2,1)S(1)}, bf16[128,512]{1,0:T(8,128)(2,1)S(1)}, u32[]{:S(2)}, u32[]{:S(2)}) collective-permute-start(bf16[128,512]{1,0:T(8,128)(2,1)S(1)} %add_convert_fusion.7), channel_id=1, source_target_pairs={{0,14},{2,0},{4,2},{6,4},{8,6},{10,8},{12,10},{14,12},{1,15},{3,1}... | collective-permute-start | bytes 393224 | tf_op jit(solution)/shard_map/ppermute | solution.py:35
  (17 other events, 157.9 us)

commit v3 on v2

--- a/solution.py
+++ b/solution.py
@@ -65,10 +65,12 @@
     def _prepare():
         acc[...] = jnp.zeros_like(acc)
         for r in range(NZ):
-            kbuf[r, 0:ROWS, :] = keys_in[2 * r][...]
-            kbuf[r, ROWS:BLK, :] = keys_in[2 * r + 1][...]
-            for g in range(2):
-                kt[r, g] = kbuf[r, :, g * HD : (g + 1) * HD].T
+            for part in range(2):
+                start = pl.multiple_of(((z - r) & (NZ - 1)) * BLK + (y ^ part) * ROWS, ROWS)
+                block = keys_in[2 * r + part][...]
+                kbuf[pl.ds(start, ROWS), :] = block
+                for g in range(2):
+                    kt[g, :, pl.ds(start, ROWS)] = block[:, g * HD : (g + 1) * HD].T
 
     @pl.when(step % (STEPS // 2) == 0)
     def _mask():
@@ -92,31 +94,30 @@
             high = jnp.where(end > base + ROWS - 1, jnp.minimum(high, end), high)
         last = last - 1
         i_blk = 4 * z + 2 * (y ^ half)
-        count = jnp.int32(0)
-        for r in range(NZ):
-            zb = (z - r) & (NZ - 1)
-            needed = (zb * BLK < high) & (zb * BLK + BLK > low)
-            active[count] = r
-            count = count + needed.astype(jnp.int32)
-
-            @pl.when(needed)
-            def _block(r=r, zb=zb):
-                for jb in range(4):
-                    j_blk = zb * 4 + 2 * (y ^ (jb // 2)) + jb % 2
-                    key_pos = j_blk * 64 + lax.broadcasted_iota(jnp.int32, (64, ROWS), 0)
-                    tier = jnp.where(
-                        lax.broadcasted_iota(jnp.int32, (1, ROWS), 1) < 64,
-                        tiers_ref[i_blk * 32 + j_blk],
-                        tiers_ref[(i_blk + 1) * 32 + j_blk],
-                    )
-                    reach = jnp.where(tier == 2, NZ * BLK, jnp.where(tier == 1, query_pos, -1))
-                    ok = (key_pos >= first) & (key_pos <= jnp.minimum(reach, last))
-                    bias[r, jb * 64 : (jb + 1) * 64, :] = jnp.where(ok, 0.0, NEG)
-
-        active[NZ] = count
+        low = low // ROWS
+        active[0] = low
+        active[1] = (high + ROWS - 1) // ROWS - low
+
+        def mask(n, carry):
+            for jb in range(2):
+                j_blk = 2 * n + jb
+                start = pl.multiple_of(j_blk * 64, 64)
+                key_pos = start + lax.broadcasted_iota(jnp.int32, (64, ROWS), 0)
+                tier = jnp.where(
+                    lax.broadcasted_iota(jnp.int32, (1, ROWS), 1) < 64,
+                    tiers_ref[i_blk * 32 + j_blk],
+                    tiers_ref[(i_blk + 1) * 32 + j_blk],
+                )
+                reach = jnp.where(tier == 2, NZ * BLK, jnp.where(tier == 1, query_pos, -1))
+                ok = (key_pos >= first) & (key_pos <= jnp.minimum(reach, last))
+                bias[pl.ds(start, 64), :] = jnp.where(ok, 0.0, NEG)
+            return carry
+
+        lax.fori_loop(low, low + active[1], mask, 0)
 
     kv_head = (step // (HEADS_KV // STEP_HEADS)) % 2
-    n_active = active[NZ]
+    first_block = active[0]
+    n_blocks = active[1]
     own = half == 0
     q_all = jnp.where(own, q_own[...], q_par[...])
     g_all = jnp.where(own, g_own[...], g_par[...])
@@ -130,54 +131,44 @@
     den[...] = jnp.zeros_like(den)
     dqt[...] = jnp.zeros_like(dqt)
 
-    def score(n, carry):
-        r = active[n]
-        s = lax.dot_general(kbuf[r, :, k_cols], q, NT, preferred_element_type=F32)
-        b = bias[r]
-        s = s * to_log2 + jnp.concatenate([b] * STEP_HEADS, axis=1)
-        sbuf[r] = s
-        s = s.reshape(BLK // 8, 8, WIDTH)
+    def over_keys(body):
+        def step_of(n, carry):
+            body(pl.multiple_of((first_block + 4 * n) * ROWS, ROWS), 4 * ROWS)
+            return carry
+
+        lax.fori_loop(0, n_blocks // 4, step_of, 0)
+        for size in (2, 1):
+
+            @pl.when((n_blocks & size) != 0)
+            def _rest(size=size):
+                done = n_blocks & ~(2 * size - 1)
+                body(pl.multiple_of((first_block + done) * ROWS, ROWS), size * ROWS)
+
+    def score(start, count):
+        rows = pl.ds(start, count)
+        s = lax.dot_general(kbuf[rows, k_cols], q, NT, preferred_element_type=F32)
+        s = s * to_log2 + jnp.concatenate([bias[rows, :]] * STEP_HEADS, axis=1)
+        sbuf[rows, :] = s
+        s = s.reshape(count // 8, 8, WIDTH)
         old = mx[...]
         new = jnp.maximum(old, jnp.max(s, axis=0))
         mx[...] = new
         den[...] = den[...] * jnp.exp2(old - new) + jnp.sum(jnp.exp2(s - new[None]), axis=0)
-        return carry
-
-    def score_pair(n, carry):
-        score(2 * n, 0)
-        score(2 * n + 1, 0)
-        return carry
-
-    lax.fori_loop(0, n_active // 2, score_pair, 0)
-
-    @pl.when(n_active % 2 == 1)
-    def _score_last():
-        score(n_active - 1, 0)
-
+
+    over_keys(score)
     top = jnp.max(mx[...], axis=0, keepdims=True)
     lse = top + jnp.log2(jnp.sum(den[...] * jnp.exp2(mx[...] - top), axis=0, keepdims=True))
 
-    def backward(n, carry):
-        r = active[n]
-        w = jnp.exp2(sbuf[r] - lse)
-        dp = lax.dot_general(kbuf[r, :, v_cols], g, NT, preferred_element_type=F32)
+    def backward(start, count):
+        rows = pl.ds(start, count)
+        w = jnp.exp2(sbuf[rows, :] - lse)
+        dp = lax.dot_general(kbuf[rows, v_cols], g, NT, preferred_element_type=F32)
         ds = (w * (dp - delta)).astype(BF16)
-        acc[r, :, v_cols] += lax.dot_general(w.astype(BF16), g, NN, preferred_element_type=F32)
-        acc[r, :, k_cols] += lax.dot_general(ds, q, NN, preferred_element_type=F32)
-        dqt[...] += lax.dot_general(kt[r, kv_head], ds, NN, preferred_element_type=F32)
-        return carry
-
-    def backward_pair(n, carry):
-        backward(2 * n, 0)
-        backward(2 * n + 1, 0)
-        return carry
-
-    lax.fori_loop(0, n_active // 2, backward_pair, 0)
-
-    @pl.when(n_active % 2 == 1)
-    def _backward_last():
-        backward(n_active - 1, 0)
-
+        acc[rows, v_cols] += lax.dot_general(w.astype(BF16), g, NN, preferred_element_type=F32)
+        acc[rows, k_cols] += lax.dot_general(ds, q, NN, preferred_element_type=F32)
+        dqt[...] += lax.dot_general(kt[kv_head, :, rows], ds, NN, preferred_element_type=F32)
+
+    over_keys(backward)
     low_dq = (dqt[...] * factor).astype(BF16)
     for h in range(STEP_HEADS):
         packed_ref[:, 0, :, h * HD : (h + 1) * HD] = (
@@ -191,9 +182,9 @@
         for r in range(NZ):
             for part in range(2):
                 out = kv_out[2 * r + part]
-                rows = slice(part * ROWS, (part + 1) * ROWS)
-                out[:, :HALF_KV] = (acc[r, rows, :HALF_KV] * factor).astype(out.dtype)
-                out[:, HALF_KV:] = acc[r, rows, HALF_KV:].astype(out.dtype)
+                rows = pl.ds(pl.multiple_of(((z - r) & (NZ - 1)) * BLK + (y ^ part) * ROWS, ROWS), ROWS)
+                out[:, :HALF_KV] = (acc[rows, :HALF_KV] * factor).astype(out.dtype)
+                out[:, HALF_KV:] = acc[rows, HALF_KV:].astype(out.dtype)
 
 
 def attention_grads(where, ends, tiers, keys, q_all, qg_par, g_all, extra_own):
@@ -227,17 +218,17 @@
             in_specs=[block] * 16 + [own, partner, own, partner_g, extra, extra_par],
             out_specs=[pl.BlockSpec((N_DP, 1, CAP, CHUNK), out_at)] + [block] * 16,
             scratch_shapes=[
-                pltpu.VMEM((NZ, BLK, 2 * HALF_KV), BF16),
-                pltpu.VMEM((NZ, 2, HD, BLK), BF16),
-                pltpu.VMEM((NZ, BLK, WIDTH), F32),
-                pltpu.VMEM((NZ, BLK, ROWS), F32),
-                pltpu.VMEM((NZ, BLK, 2 * HALF_KV), F32),
+                pltpu.VMEM((NZ * BLK, 2 * HALF_KV), BF16),
+                pltpu.VMEM((2, HD, NZ * BLK), BF16),
+                pltpu.VMEM((NZ * BLK, WIDTH), F32),
+                pltpu.VMEM((NZ * BLK, ROWS), F32),
+                pltpu.VMEM((NZ * BLK, 2 * HALF_KV), F32),
                 pltpu.VMEM((HD, WIDTH), F32),
                 pltpu.VMEM((SLOTS // 2, ROWS), BF16),
                 pltpu.VMEM((8, WIDTH), F32),
                 pltpu.VMEM((8, WIDTH), F32),
                 pltpu.VMEM((H // 2, ROWS), F32),
-                pltpu.SMEM((NZ + 1,), jnp.int32),
+                pltpu.SMEM((2,), jnp.int32),
             ],
         ),
         out_shape=[jax.ShapeDtypeStruct((N_DP, 2, CAP, HALF_Q), BF16)] + [kv_f32] * 2 + [kv_bf16] * 14,
@@ -379,14 +370,15 @@
     a = key_values(y)
     b = key_values(1 - y)
     keys_a = {0: a, 1: zshift(a, 1), 7: zshift(a, -1)}
-    keys_b = {0: yswap(b), 1: zshift_yswap(b, 1), 7: zshift_yswap(b, -1)}
+    keys_b = {0: yswap(b)}
     send, extra_own = prepare(y, q_all, g_all, forward_out[0], row_owners[0])
     send, keys_b[0] = lax.optimization_barrier((send, keys_b[0]))
     qg_par = yswap(send)
-    for hop in range(2, 4):
+    for hop in range(1, 4):
         for held in (keys_a, keys_b):
-            held[hop] = zshift(held[hop - 1], 1)
-            held[NZ - hop] = zshift(held[NZ - hop + 1], -1)
+            if hop not in held:
+                held[hop] = zshift(held[hop - 1], 1)
+                held[NZ - hop] = zshift(held[(NZ - hop + 1) % NZ], -1)
     keys_a[4] = zshift(keys_a[3], 1)
     keys_b[4] = zshift(keys_b[5], -1)
 

time: 133 us -> 129 us (0.970); the launches traced: 134 us -> 129 us
  Pallas kernels: 29.9 us -> 20.4 us
  starting transfers between devices: 61.5 us -> 69.5 us
  waiting for transfers between devices: 20.8 us -> 16.6 us
    ppermute x26 -> x28, starting transfers between devices: 34.4 us -> 53 us  [zshift(): return lax.ppermute(x, 'z', [(i, (i + by) % NZ) for i in range(NZ)])]
    pallas_call x1, Pallas kernels: 23.3 us -> 13.8 us  [attention_grads(): pl.pallas_call(grads_kernel, grid_spec=pltpu.PrefetchScalarGridSpec(num_s...]
    ppermute x2 -> x0, starting transfers between devices: 6.82 us -> none  [zshift_yswap(): return lax.ppermute(x, ('z', 'yl'), pairs)]
    all_to_all x1, starting transfers between devices: 18 us -> 14.2 us  [to_owners(): lax.all_to_all(rows.reshape(2 * N_DP, CAP, -1), ('dp', 'yl'), split_axis=...]
    ppermute x2 -> x0, waiting for transfers between devices: 2.05 us -> none  [zshift_yswap(): return lax.ppermute(x, ('z', 'yl'), pairs)]
    ppermute x26 -> x28, waiting for transfers between devices: 9.37 us -> 7.54 us  [zshift(): return lax.ppermute(x, 'z', [(i, (i + by) % NZ) for i in range(NZ)])]
  transfers between devices with their start and end apart: 31 -> 31, of which waited for: 12 -> 10; matrix products, arithmetic and copies ran while one was open for 3% -> 3% of each run, Pallas kernels for 3% -> 4%
where the time goes in v3:
time: 129 us
  starting transfers between devices  69.5 us (54%)
  Pallas kernels  20.4 us (16%)
  waiting for transfers between devices  16.6 us (13%)
  blocking collectives  15.7 us (12%)
  local copies, waits for them, and re-layouts  4.07 us (3%)
  other arithmetic  1.73 us (1%)
    ppermute x28, starting transfers between devices, zshift(): return lax.ppermute(x, 'z', [(i, (i + by) % NZ) for i in range(NZ)])  53 us
    all_to_all x1, blocking collectives, to_owners(): lax.all_to_all(rows.reshape(2 * N_DP, CAP, -1), ('dp', 'yl'), split_axis=...  15.7 us
    all_to_all x1, starting transfers between devices, to_owners(): lax.all_to_all(rows.reshape(2 * N_DP, CAP, -1), ('dp', 'yl'), split_axis=...  14.2 us
    pallas_call x1, Pallas kernels, attention_grads(): pl.pallas_call(grads_kernel, grid_spec=pltpu.PrefetchScalarGridSpec(num_s...  13.8 us
    all_to_all x1, waiting for transfers between devices, to_owners(): lax.all_to_all(rows.reshape(2 * N_DP, CAP, -1), ('dp', 'yl'), split_axis=...  9.08 us
    ppermute x28, waiting for transfers between devices, zshift(): return lax.ppermute(x, 'z', [(i, (i + by) % NZ) for i in range(NZ)])  7.54 us
    pallas_call x1, Pallas kernels, prepare(): pl.pallas_call(prepare_kernel, grid_spec=pltpu.PrefetchScalarGridSpec(num...  3.73 us
  transfers between devices with their start and end apart: 31, of which 10 were waited for; matrix products, arithmetic and copies ran while one was open for 3% of the time, Pallas kernels for 4%

profile of v3, /device:TPU:1, one launch (start us, length us, event | category | flops | bytes accessed | tf_op | source)
XLA Modules:
  0.0 128.6 jit_solution(12543920179920034589)
XLA Ops:
  0.0 1.0 dynamic-slice_bitcast_fusion
  1.0 2.2 %collective-permute-start = (bf16[128,512]{1,0:T(8,128)(2,1)S(1)}, bf16[128,512]{1,0:T(8,128)(2,1)S(1)}, u32[]{:S(2)}, u32[]{:S(2)}) collective-permute-start(bf16[128,512]{1,0:T(8,128)(2,1)S(1)} %pad_maximum_fusion.1), channel_id=1, source_target_pairs={{0,1},{1,0},{2,3},{3,2},{4,5},{5,4},{6,7},{7,6},{8,9},{9,8},{10,11... | collective-permute-start | bytes 393224 | tf_op jit(solution)/shard_map/ppermute | solution.py:39
  3.2 1.4 %copy.9.owners_ref = s32[128,1]{1,0:T(8,128)} copy(s32[128,1]{0,1:T(1,128)} %bitcast.26) | data formatting | bytes 1024 | tf_op jit(solution)/shard_map/squeeze | solution.py:374
  4.6 3.7 %prepare.1 = (bf16[128,4224]{1,0:T(8,128)(2,1)}, bf16[128,128]{1,0:T(8,128)(2,1)}) custom-call(s32[1]{0:T(128)} %bitcast.1.where_ref, bf16[128,4096]{1,0:T(8,128)(2,1)} %bitcast.22, bf16[128,4096]{1,0:T(8,128)(2,1)} %bitcast.24, bf16[128,4096]{1,0:T(8,128)(2,1)} %bitcast.21, s32[128,1]{1,0:T(8,128)} %copy.9.owners_ref), custom_call_target="tpu_custom_call" | custom-call | tf_op jit(solution)/shard_map/prepare/pallas_call | solution.py:338
  8.3 0.1 collective-permute-start.15
  8.5 1.9 %collective-permute-start.1 = (bf16[128,512]{1,0:T(8,128)(2,1)S(1)}, bf16[128,512]{1,0:T(8,128)(2,1)S(1)}, u32[]{:S(2)}, u32[]{:S(2)}) collective-permute-start(bf16[128,512]{1,0:T(8,128)(2,1)S(1)} %pad_maximum_fusion.refs_0_), channel_id=1, source_target_pairs={{0,2},{2,4},{4,6},{6,8},{8,10},{10,12},{12,14},{14,0},{1,3},{3,5},... | collective-permute-start | bytes 393224 | tf_op jit(solution)/shard_map/ppermute | solution.py:35
  10.3 4.0 %collective-permute-start.8 = (bf16[128,512]{1,0:T(8,128)(2,1)S(1)}, bf16[128,512]{1,0:T(8,128)(2,1)S(1)}, u32[]{:S(2)}, u32[]{:S(2)}) collective-permute-start(bf16[128,512]{1,0:T(8,128)(2,1)S(1)} %collective-permute-done.refs_1_), channel_id=1, source_target_pairs={{0,14},{2,0},{4,2},{6,4},{8,6},{10,8},{12,10},{14,12},{1,15},{3,1}... | collective-permute-start | bytes 393224 | tf_op jit(solution)/shard_map/ppermute | solution.py:35
  14.4 1.4 %collective-permute-start.12 = (bf16[128,512]{1,0:T(8,128)(2,1)S(1)}, bf16[128,512]{1,0:T(8,128)(2,1)S(1)}, u32[]{:S(2)}, u32[]{:S(2)}) collective-permute-start(bf16[128,512]{1,0:T(8,128)(2,1)S(1)} %pad_maximum_fusion.refs_0_), channel_id=1, source_target_pairs={{0,14},{2,0},{4,2},{6,4},{8,6},{10,8},{12,10},{14,12},{1,15},{3,1}... | collective-permute-start | bytes 393224 | tf_op jit(solution)/shard_map/ppermute | solution.py:35
  15.7 0.1 collective-permute-start.2
  15.8 0.8 collective-permute-done.1.refs_2_
  16.6 2.7 %collective-permute-start.9 = (bf16[128,512]{1,0:T(8,128)(2,1)S(1)}, bf16[128,512]{1,0:T(8,128)(2,1)S(1)}, u32[]{:S(2)}, u32[]{:S(2)}) collective-permute-start(bf16[128,512]{1,0:T(8,128)(2,1)S(1)} %collective-permute-done.8.refs_15_), channel_id=1, source_target_pairs={{0,14},{2,0},{4,2},{6,4},{8,6},{10,8},{12,10},{14,12},{1,15},{3,1}... | collective-permute-start | bytes 393224 | tf_op jit(solution)/shard_map/ppermute | solution.py:35
  19.4 2.7 %collective-permute-start.13 = (bf16[128,512]{1,0:T(8,128)(2,1)S(1)}, bf16[128,512]{1,0:T(8,128)(2,1)S(1)}, u32[]{:S(2)}, u32[]{:S(2)}) collective-permute-start(bf16[128,512]{1,0:T(8,128)(2,1)S(1)} %collective-permute-done.12.refs_14_), channel_id=1, source_target_pairs={{0,14},{2,0},{4,2},{6,4},{8,6},{10,8},{12,10},{14,12},{1,15},{3,1}... | collective-permute-start | bytes 393224 | tf_op jit(solution)/shard_map/ppermute | solution.py:35
  22.1 0.5 collective-permute-done.3.refs_4_
  22.7 2.7 %collective-permute-start.10 = (bf16[128,512]{1,0:T(8,128)(2,1)S(1)}, bf16[128,512]{1,0:T(8,128)(2,1)S(1)}, u32[]{:S(2)}, u32[]{:S(2)}) collective-permute-start(bf16[128,512]{1,0:T(8,128)(2,1)S(1)} %collective-permute-done.9.refs_13_), channel_id=1, source_target_pairs={{0,14},{2,0},{4,2},{6,4},{8,6},{10,8},{12,10},{14,12},{1,15},{3,1}... | collective-permute-start | bytes 393224 | tf_op jit(solution)/shard_map/ppermute | solution.py:35
  25.4 2.3 %collective-permute-start.14 = (bf16[128,512]{1,0:T(8,128)(2,1)S(1)}, bf16[128,512]{1,0:T(8,128)(2,1)S(1)}, u32[]{:S(2)}, u32[]{:S(2)}) collective-permute-start(bf16[128,512]{1,0:T(8,128)(2,1)S(1)} %collective-permute-done.13.refs_12_), channel_id=1, source_target_pairs={{0,14},{2,0},{4,2},{6,4},{8,6},{10,8},{12,10},{14,12},{1,15},{3,1}... | collective-permute-start | bytes 393224 | tf_op jit(solution)/shard_map/ppermute | solution.py:35
  27.6 0.9 collective-permute-done.5.refs_6_
  28.6 0.1 collective-permute-done.10.refs_11_
  28.7 3.2 %collective-permute-start.11 = (bf16[128,512]{1,0:T(8,128)(2,1)S(1)}, bf16[128,512]{1,0:T(8,128)(2,1)S(1)}, u32[]{:S(2)}, u32[]{:S(2)}) collective-permute-start(bf16[128,512]{1,0:T(8,128)(2,1)S(1)} %collective-permute-done.10.refs_11_), channel_id=1, source_target_pairs={{0,14},{2,0},{4,2},{6,4},{8,6},{10,8},{12,10},{14,12},{1,15},{3,1}... | collective-permute-start | bytes 393224 | tf_op jit(solution)/shard_map/ppermute | solution.py:35
  31.9 0.7 reshape_squeeze.3.tiers_ref
  32.6 0.7 reduce-window.9
  33.3 0.7 pad_add_fusion.where_ref
  34.0 0.8 collective-permute-done.7.refs_8_
  35.0 0.5 copy-done.31
  35.4 0.0 copy-done.32
  35.5 0.4 copy-done
  35.9 13.8 %grads.1 = (bf16[16,2,16,2048]{3,2,1,0:T(8,128)(2,1)}, f32[128,512]{1,0:T(8,128)}, f32[128,512]{1,0:T(8,128)}, bf16[128,512]{1,0:T(8,128)(2,1)}, bf16[128,512]{1...) custom-call(s32[2]{0:T(128)} %pad_add_fusion.where_ref, ...), custom_call_target="tpu_custom_call" | custom-call | flops 8000000000 | bytes 10485760 | tf_op jit(solution)/shard_map/grads/pallas_call | solution.py:213
  49.7 14.3 %collective-permute-start.26 = (bf16[128,512]{1,0:T(8,128)(2,1)}, bf16[128,512]{1,0:T(8,128)(2,1)S(1)}, u32[]{:S(2)}, u32[]{:S(2)}) collective-permute-start(bf16[128,512]{1,0:T(8,128)(2,1)} %get-tuple-element.44), channel_id=1, source_target_pairs={{0,2},{2,4},{4,6},{6,8},{8,10},{10,12},{12,14},{14,0},{1,3},{3,5},... | collective-permute-start | bytes 393224 | tf_op jit(solution)/shard_map/ppermute | solution.py:35
  64.0 1.5 %collective-permute-start.20 = (bf16[128,512]{1,0:T(8,128)(2,1)}, bf16[128,512]{1,0:T(8,128)(2,1)S(1)}, u32[]{:S(2)}, u32[]{:S(2)}) collective-permute-start(bf16[128,512]{1,0:T(8,128)(2,1)} %get-tuple-element.38), channel_id=1, source_target_pairs={{0,2},{2,4},{4,6},{6,8},{8,10},{10,12},{12,14},{14,0},{1,3},{3,5},... | collective-permute-start | bytes 393224 | tf_op jit(solution)/shard_map/ppermute | solution.py:35
  65.4 1.2 collective-permute-start.16
  66.7 14.2 %all-to-all-start = ((bf16[32,16,2048]{2,1,0:T(8,128)(2,1)}), bf16[32,16,2048]{2,1,0:T(8,128)(2,1)S(1)}, u32[]{:S(2)}, u32[]{:S(2)}) async-start(bf16[32,16,2048]{2,1,0:T(8,128)(2,1)} %bitcast.20), calls=%async_computation | async-start | bytes 4194304 | tf_op jit(solution)/shard_map/all_to_all | solution.py:416
  81.0 0.1 collective-permute-start.27
  81.2 2.7 %collective-permute-start.24 = (bf16[128,512]{1,0:T(8,128)(2,1)S(1)}, bf16[128,512]{1,0:T(8,128)(2,1)S(1)}, u32[]{:S(2)}, u32[]{:S(2)}) collective-permute-start(bf16[128,512]{1,0:T(8,128)(2,1)S(1)} %add_convert_fusion.4), channel_id=1, source_target_pairs={{0,14},{2,0},{4,2},{6,4},{8,6},{10,8},{12,10},{14,12},{1,15},{3,1}... | collective-permute-start | bytes 393224 | tf_op jit(solution)/shard_map/ppermute | solution.py:35
  83.9 0.1 collective-permute-start.21
  84.1 2.9 %collective-permute-start.17 = (bf16[128,512]{1,0:T(8,128)(2,1)S(1)}, bf16[128,512]{1,0:T(8,128)(2,1)S(1)}, u32[]{:S(2)}, u32[]{:S(2)}) collective-permute-start(bf16[128,512]{1,0:T(8,128)(2,1)S(1)} %add_convert_fusion.9), channel_id=1, source_target_pairs={{0,14},{2,0},{4,2},{6,4},{8,6},{10,8},{12,10},{14,12},{1,15},{3,1}... | collective-permute-start | bytes 393224 | tf_op jit(solution)/shard_map/ppermute | solution.py:35
  87.0 0.1 collective-permute-done.27
  87.2 0.1 collective-permute-start.28
  87.4 2.7 %collective-permute-start.25 = (bf16[128,512]{1,0:T(8,128)(2,1)S(1)}, bf16[128,512]{1,0:T(8,128)(2,1)S(1)}, u32[]{:S(2)}, u32[]{:S(2)}) collective-permute-start(bf16[128,512]{1,0:T(8,128)(2,1)S(1)} %add_convert_fusion.3), channel_id=1, source_target_pairs={{0,14},{2,0},{4,2},{6,4},{8,6},{10,8},{12,10},{14,12},{1,15},{3,1}... | collective-permute-start | bytes 393224 | tf_op jit(solution)/shard_map/ppermute | solution.py:35
  90.1 0.1 collective-permute-start.22
  90.3 2.7 %collective-permute-start.18 = (bf16[128,512]{1,0:T(8,128)(2,1)S(1)}, bf16[128,512]{1,0:T(8,128)(2,1)S(1)}, u32[]{:S(2)}, u32[]{:S(2)}) collective-permute-start(bf16[128,512]{1,0:T(8,128)(2,1)S(1)} %add_convert_fusion.8), channel_id=1, source_target_pairs={{0,14},{2,0},{4,2},{6,4},{8,6},{10,8},{12,10},{14,12},{1,15},{3,1}... | collective-permute-start | bytes 393224 | tf_op jit(solution)/shard_map/ppermute | solution.py:35
  93.1 0.1 collective-permute-start.29
  93.1 2.2 %collective-permute-done.18 = bf16[128,512]{1,0:T(8,128)(2,1)S(1)} collective-permute-done((bf16[128,512]{1,0:T(8,128)(2,1)S(1)}, bf16[128,512]{1,0:T(8,128)(2,1)S(1)}, u32[]{:S(2)}, u32[]{:S(2)}) %collective-permute-start.18) | collective-permute-done | bytes 131104 | tf_op jit(solution)/shard_map/ppermute | solution.py:35
  95.4 3.5 %collective-permute-start.19 = (bf16[128,512]{1,0:T(8,128)(2,1)S(1)}, bf16[128,512]{1,0:T(8,128)(2,1)S(1)}, u32[]{:S(2)}, u32[]{:S(2)}) collective-permute-start(bf16[128,512]{1,0:T(8,128)(2,1)S(1)} %add_convert_fusion.7), channel_id=1, source_target_pairs={{0,14},{2,0},{4,2},{6,4},{8,6},{10,8},{12,10},{14,12},{1,15},{3,1}... | collective-permute-start | bytes 393224 | tf_op jit(solution)/shard_map/ppermute | solution.py:35
  98.9 0.3 collective-permute-done.29.up_b
  99.2 1.7 %collective-permute-done.19.down_a = bf16[128,512]{1,0:T(8,128)(2,1)S(1)} collective-permute-done((bf16[128,512]{1,0:T(8,128)(2,1)S(1)}, bf16[128,512]{1,0:T(8,128)(2,1)S(1)}, u32[]{:S(2)}, u32[]{:S(2)}) %collective-permute-start.19) | collective-permute-done | bytes 131104 | tf_op jit(solution)/shard_map/ppermute | solution.py:35
  100.9 0.9 finish.1
  101.8 9.1 %all-to-all-done.q_ref = bf16[32,16,2048]{2,1,0:T(8,128)(2,1)S(1)} async-done(((bf16[32,16,2048]{2,1,0:T(8,128)(2,1)}), bf16[32,16,2048]{2,1,0:T(8,128)(2,1)S(1)}, u32[]{:S(2)}, u32[]{:S(2)}) %all-to-all-start) | async-done | bytes 2097184 | tf_op jit(solution)/shard_map/all_to_all | solution.py:416
  110.9 15.7 %all_to_all.10.kv_ref = bf16[32,16,512]{2,1,0:T(8,128)(2,1)S(1)} all-to-all(bf16[32,16,512]{2,1,0:T(8,128)(2,1)S(1)} %bitcast.19), channel_id=1, replica_groups=mesh['dp'=16,'z'=8,'yl'=2] {'dp','yl'}, dimensions={0} | all-to-all | bytes 1048576 | tf_op jit(solution)/shard_map/all_to_all | solution.py:416
  126.6 2.0 %lay_out.1 = bf16[16,16,5120]{2,1,0:T(8,128)(2,1)} custom-call(bf16[32,16,2048]{2,1,0:T(8,128)(2,1)S(1)} %all-to-all-done.q_ref, bf16[32,16,512]{2,1,0:T(8,128)(2,1)S(1)} %all_to_all.10.kv_ref), custom_call_target="tpu_custom_call" | custom-call | tf_op jit(solution)/shard_map/lay_out/pallas_call | solution.py:287
  (104 shorter events, 0.6 us)
Async XLA Ops:
  0.0 31.9 %copy-start.17 = (s32[1,32,32]{2,1,0:T(8,128)S(1)}, s32[1,32,32]{2,1,0:T(8,128)}, u32[]{:S(2)}) copy-start(s32[1,32,32]{2,1,0:T(8,128)} %param.14) | copy-start | bytes 12292
  0.0 32.6 %copy-start.33 = (s32[1,8]{1,0:T(1,128)S(1)}, s32[1,8]{1,0:T(1,128)}, u32[]{:S(2)}) copy-start(s32[1,8]{1,0:T(1,128)} %param.13) | copy-start | bytes 100
  1.0 7.3 %collective-permute-start = (bf16[128,512]{1,0:T(8,128)(2,1)S(1)}, bf16[128,512]{1,0:T(8,128)(2,1)S(1)}, u32[]{:S(2)}, u32[]{:S(2)}) collective-permute-start(bf16[128,512]{1,0:T(8,128)(2,1)S(1)} %pad_maximum_fusion.1), channel_id=1, source_target_pairs={{0,1},{1,0},{2,3},{3,2},{4,5},{5,4},{6,7},{7,6},{8,9},{9,8},{10,11... | collective-permute-start | bytes 393224 | tf_op jit(solution)/shard_map/ppermute | solution.py:39
  8.3 26.5 %copy-start.18 = (bf16[128,512]{1,0:T(8,128)(2,1)}, bf16[128,512]{1,0:T(8,128)(2,1)S(1)}, u32[]{:S(2)}) copy-start(bf16[128,512]{1,0:T(8,128)(2,1)S(1)} %collective-permute-done.refs_1_) | copy-start | bytes 393220
  8.3 26.5 %collective-permute-start.15 = (bf16[128,4224]{1,0:T(8,128)(2,1)}, bf16[128,4224]{1,0:T(8,128)(2,1)S(1)}, u32[]{:S(2)}, u32[]{:S(2)}) collective-permute-start(bf16[128,4224]{1,0:T(8,128)(2,1)} %get-tuple-element.30), channel_id=1, source_target_pairs={{0,1},{1,0},{2,3},{3,2},{4,5},{5,4},{6,7},{7,6},{8,9},{9,8},{10,11... | collective-permute-start | bytes 3244040 | tf_op jit(solution)/shard_map/ppermute | solution.py:39
  8.5 26.4 %copy-start.16 = (bf16[128,512]{1,0:T(8,128)(2,1)}, bf16[128,512]{1,0:T(8,128)(2,1)S(1)}, u32[]{:S(2)}) copy-start(bf16[128,512]{1,0:T(8,128)(2,1)S(1)} %pad_maximum_fusion.refs_0_) | copy-start | bytes 393220
  8.5 8.2 %collective-permute-start.1 = (bf16[128,512]{1,0:T(8,128)(2,1)S(1)}, bf16[128,512]{1,0:T(8,128)(2,1)S(1)}, u32[]{:S(2)}, u32[]{:S(2)}) collective-permute-start(bf16[128,512]{1,0:T(8,128)(2,1)S(1)} %pad_maximum_fusion.refs_0_), channel_id=1, source_target_pairs={{0,2},{2,4},{4,6},{6,8},{8,10},{10,12},{12,14},{14,0},{1,3},{3,5},... | collective-permute-start | bytes 393224 | tf_op jit(solution)/shard_map/ppermute | solution.py:35
  10.3 6.3 %collective-permute-start.8 = (bf16[128,512]{1,0:T(8,128)(2,1)S(1)}, bf16[128,512]{1,0:T(8,128)(2,1)S(1)}, u32[]{:S(2)}, u32[]{:S(2)}) collective-permute-start(bf16[128,512]{1,0:T(8,128)(2,1)S(1)} %collective-permute-done.refs_1_), channel_id=1, source_target_pairs={{0,14},{2,0},{4,2},{6,4},{8,6},{10,8},{12,10},{14,12},{1,15},{3,1}... | collective-permute-start | bytes 393224 | tf_op jit(solution)/shard_map/ppermute | solution.py:35
  14.4 5.0 %collective-permute-start.12 = (bf16[128,512]{1,0:T(8,128)(2,1)S(1)}, bf16[128,512]{1,0:T(8,128)(2,1)S(1)}, u32[]{:S(2)}, u32[]{:S(2)}) collective-permute-start(bf16[128,512]{1,0:T(8,128)(2,1)S(1)} %pad_maximum_fusion.refs_0_), channel_id=1, source_target_pairs={{0,14},{2,0},{4,2},{6,4},{8,6},{10,8},{12,10},{14,12},{1,15},{3,1}... | collective-permute-start | bytes 393224 | tf_op jit(solution)/shard_map/ppermute | solution.py:35
  15.7 6.4 %collective-permute-start.2 = (bf16[128,512]{1,0:T(8,128)(2,1)S(1)}, bf16[128,512]{1,0:T(8,128)(2,1)S(1)}, u32[]{:S(2)}, u32[]{:S(2)}) collective-permute-start(bf16[128,512]{1,0:T(8,128)(2,1)S(1)} %collective-permute-done.refs_1_), channel_id=1, source_target_pairs={{0,2},{2,4},{4,6},{6,8},{8,10},{10,12},{12,14},{14,0},{1,3},{3,5},... | collective-permute-start | bytes 393224 | tf_op jit(solution)/shard_map/ppermute | solution.py:35
  16.6 18.2 %copy-start.19 = (bf16[128,512]{1,0:T(8,128)(2,1)}, bf16[128,512]{1,0:T(8,128)(2,1)S(1)}, u32[]{:S(2)}) copy-start(bf16[128,512]{1,0:T(8,128)(2,1)S(1)} %collective-permute-done.1.refs_2_) | copy-start | bytes 393220
  16.6 6.0 %collective-permute-start.3 = (bf16[128,512]{1,0:T(8,128)(2,1)S(1)}, bf16[128,512]{1,0:T(8,128)(2,1)S(1)}, u32[]{:S(2)}, u32[]{:S(2)}) collective-permute-start(bf16[128,512]{1,0:T(8,128)(2,1)S(1)} %collective-permute-done.1.refs_2_), channel_id=1, source_target_pairs={{0,2},{2,4},{4,6},{6,8},{8,10},{10,12},{12,14},{14,0},{1,3},{3,5},... | collective-permute-start | bytes 393224 | tf_op jit(solution)/shard_map/ppermute | solution.py:35
  16.6 18.2 %copy-start.20 = (bf16[128,512]{1,0:T(8,128)(2,1)}, bf16[128,512]{1,0:T(8,128)(2,1)S(1)}, u32[]{:S(2)}) copy-start(bf16[128,512]{1,0:T(8,128)(2,1)S(1)} %collective-permute-done.8.refs_15_) | copy-start | bytes 393220
  16.6 6.0 %collective-permute-start.9 = (bf16[128,512]{1,0:T(8,128)(2,1)S(1)}, bf16[128,512]{1,0:T(8,128)(2,1)S(1)}, u32[]{:S(2)}, u32[]{:S(2)}) collective-permute-start(bf16[128,512]{1,0:T(8,128)(2,1)S(1)} %collective-permute-done.8.refs_15_), channel_id=1, source_target_pairs={{0,14},{2,0},{4,2},{6,4},{8,6},{10,8},{12,10},{14,12},{1,15},{3,1}... | collective-permute-start | bytes 393224 | tf_op jit(solution)/shard_map/ppermute | solution.py:35
  19.4 15.5 %copy-start.21 = (bf16[128,512]{1,0:T(8,128)(2,1)}, bf16[128,512]{1,0:T(8,128)(2,1)S(1)}, u32[]{:S(2)}) copy-start(bf16[128,512]{1,0:T(8,128)(2,1)S(1)} %collective-permute-done.12.refs_14_) | copy-start | bytes 393220
  19.4 6.0 %collective-permute-start.13 = (bf16[128,512]{1,0:T(8,128)(2,1)S(1)}, bf16[128,512]{1,0:T(8,128)(2,1)S(1)}, u32[]{:S(2)}, u32[]{:S(2)}) collective-permute-start(bf16[128,512]{1,0:T(8,128)(2,1)S(1)} %collective-permute-done.12.refs_14_), channel_id=1, source_target_pairs={{0,14},{2,0},{4,2},{6,4},{8,6},{10,8},{12,10},{14,12},{1,15},{3,1}... | collective-permute-start | bytes 393224 | tf_op jit(solution)/shard_map/ppermute | solution.py:35
  22.1 5.5 %collective-permute-start.4 = (bf16[128,512]{1,0:T(8,128)(2,1)S(1)}, bf16[128,512]{1,0:T(8,128)(2,1)S(1)}, u32[]{:S(2)}, u32[]{:S(2)}) collective-permute-start(bf16[128,512]{1,0:T(8,128)(2,1)S(1)} %collective-permute-done.2.refs_3_), channel_id=1, source_target_pairs={{0,2},{2,4},{4,6},{6,8},{8,10},{10,12},{12,14},{14,0},{1,3},{3,5},... | collective-permute-start | bytes 393224 | tf_op jit(solution)/shard_map/ppermute | solution.py:35
  22.7 5.9 %collective-permute-start.5 = (bf16[128,512]{1,0:T(8,128)(2,1)S(1)}, bf16[128,512]{1,0:T(8,128)(2,1)S(1)}, u32[]{:S(2)}, u32[]{:S(2)}) collective-permute-start(bf16[128,512]{1,0:T(8,128)(2,1)S(1)} %collective-permute-done.3.refs_4_), channel_id=1, source_target_pairs={{0,2},{2,4},{4,6},{6,8},{8,10},{10,12},{12,14},{14,0},{1,3},{3,5},... | collective-permute-start | bytes 393224 | tf_op jit(solution)/shard_map/ppermute | solution.py:35
  22.7 6.0 %collective-permute-start.10 = (bf16[128,512]{1,0:T(8,128)(2,1)S(1)}, bf16[128,512]{1,0:T(8,128)(2,1)S(1)}, u32[]{:S(2)}, u32[]{:S(2)}) collective-permute-start(bf16[128,512]{1,0:T(8,128)(2,1)S(1)} %collective-permute-done.9.refs_13_), channel_id=1, source_target_pairs={{0,14},{2,0},{4,2},{6,4},{8,6},{10,8},{12,10},{14,12},{1,15},{3,1}... | collective-permute-start | bytes 393224 | tf_op jit(solution)/shard_map/ppermute | solution.py:35
  25.4 8.6 %collective-permute-start.14 = (bf16[128,512]{1,0:T(8,128)(2,1)S(1)}, bf16[128,512]{1,0:T(8,128)(2,1)S(1)}, u32[]{:S(2)}, u32[]{:S(2)}) collective-permute-start(bf16[128,512]{1,0:T(8,128)(2,1)S(1)} %collective-permute-done.13.refs_12_), channel_id=1, source_target_pairs={{0,14},{2,0},{4,2},{6,4},{8,6},{10,8},{12,10},{14,12},{1,15},{3,1}... | collective-permute-start | bytes 393224 | tf_op jit(solution)/shard_map/ppermute | solution.py:35
  27.6 6.3 %collective-permute-start.6 = (bf16[128,512]{1,0:T(8,128)(2,1)S(1)}, bf16[128,512]{1,0:T(8,128)(2,1)S(1)}, u32[]{:S(2)}, u32[]{:S(2)}) collective-permute-start(bf16[128,512]{1,0:T(8,128)(2,1)S(1)} %collective-permute-done.4.refs_5_), channel_id=1, source_target_pairs={{0,2},{2,4},{4,6},{6,8},{8,10},{10,12},{12,14},{14,0},{1,3},{3,5},... | collective-permute-start | bytes 393224 | tf_op jit(solution)/shard_map/ppermute | solution.py:35
  28.6 6.2 %collective-permute-start.7 = (bf16[128,512]{1,0:T(8,128)(2,1)S(1)}, bf16[128,512]{1,0:T(8,128)(2,1)S(1)}, u32[]{:S(2)}, u32[]{:S(2)}) collective-permute-start(bf16[128,512]{1,0:T(8,128)(2,1)S(1)} %collective-permute-done.5.refs_6_), channel_id=1, source_target_pairs={{0,2},{2,4},{4,6},{6,8},{8,10},{10,12},{12,14},{14,0},{1,3},{3,5},... | collective-permute-start | bytes 393224 | tf_op jit(solution)/shard_map/ppermute | solution.py:35
  28.7 6.1 %collective-permute-start.11 = (bf16[128,512]{1,0:T(8,128)(2,1)S(1)}, bf16[128,512]{1,0:T(8,128)(2,1)S(1)}, u32[]{:S(2)}, u32[]{:S(2)}) collective-permute-start(bf16[128,512]{1,0:T(8,128)(2,1)S(1)} %collective-permute-done.10.refs_11_), channel_id=1, source_target_pairs={{0,14},{2,0},{4,2},{6,4},{8,6},{10,8},{12,10},{14,12},{1,15},{3,1}... | collective-permute-start | bytes 393224 | tf_op jit(solution)/shard_map/ppermute | solution.py:35
  49.7 31.3 %collective-permute-start.26 = (bf16[128,512]{1,0:T(8,128)(2,1)}, bf16[128,512]{1,0:T(8,128)(2,1)S(1)}, u32[]{:S(2)}, u32[]{:S(2)}) collective-permute-start(bf16[128,512]{1,0:T(8,128)(2,1)} %get-tuple-element.44), channel_id=1, source_target_pairs={{0,2},{2,4},{4,6},{6,8},{8,10},{10,12},{12,14},{14,0},{1,3},{3,5},... | collective-permute-start | bytes 393224 | tf_op jit(solution)/shard_map/ppermute | solution.py:35
  64.0 17.1 %collective-permute-start.23 = (bf16[128,512]{1,0:T(8,128)(2,1)}, bf16[128,512]{1,0:T(8,128)(2,1)S(1)}, u32[]{:S(2)}, u32[]{:S(2)}) collective-permute-start(bf16[128,512]{1,0:T(8,128)(2,1)} %get-tuple-element.41), channel_id=1, source_target_pairs={{0,14},{2,0},{4,2},{6,4},{8,6},{10,8},{12,10},{14,12},{1,15},{3,1}... | collective-permute-start | bytes 393224 | tf_op jit(solution)/shard_map/ppermute | solution.py:35
  64.0 19.9 %collective-permute-start.20 = (bf16[128,512]{1,0:T(8,128)(2,1)}, bf16[128,512]{1,0:T(8,128)(2,1)S(1)}, u32[]{:S(2)}, u32[]{:S(2)}) collective-permute-start(bf16[128,512]{1,0:T(8,128)(2,1)} %get-tuple-element.38), channel_id=1, source_target_pairs={{0,2},{2,4},{4,6},{6,8},{8,10},{10,12},{12,14},{14,0},{1,3},{3,5},... | collective-permute-start | bytes 393224 | tf_op jit(solution)/shard_map/ppermute | solution.py:35
  65.4 18.6 %collective-permute-start.16 = (bf16[128,512]{1,0:T(8,128)(2,1)}, bf16[128,512]{1,0:T(8,128)(2,1)S(1)}, u32[]{:S(2)}, u32[]{:S(2)}) collective-permute-start(bf16[128,512]{1,0:T(8,128)(2,1)} %get-tuple-element.34), channel_id=1, source_target_pairs={{0,14},{2,0},{4,2},{6,4},{8,6},{10,8},{12,10},{14,12},{1,15},{3,1}... | collective-permute-start | bytes 393224 | tf_op jit(solution)/shard_map/ppermute | solution.py:35
  66.7 17.2 %copy-start.13 = (bf16[128,512]{1,0:T(8,128)(2,1)S(1)}, bf16[128,512]{1,0:T(8,128)(2,1)}, u32[]{:S(2)}) copy-start(bf16[128,512]{1,0:T(8,128)(2,1)} %get-tuple-element.39) | copy-start | bytes 393220
  66.7 17.4 %copy-start.12 = (bf16[128,512]{1,0:T(8,128)(2,1)S(1)}, bf16[128,512]{1,0:T(8,128)(2,1)}, u32[]{:S(2)}) copy-start(bf16[128,512]{1,0:T(8,128)(2,1)} %get-tuple-element.35) | copy-start | bytes 393220
  66.7 20.5 %copy-start.11 = (bf16[128,512]{1,0:T(8,128)(2,1)S(1)}, bf16[128,512]{1,0:T(8,128)(2,1)}, u32[]{:S(2)}) copy-start(bf16[128,512]{1,0:T(8,128)(2,1)} %get-tuple-element.46) | copy-start | bytes 393220
  66.7 20.6 %copy-start.10 = (bf16[128,512]{1,0:T(8,128)(2,1)S(1)}, bf16[128,512]{1,0:T(8,128)(2,1)}, u32[]{:S(2)}) copy-start(bf16[128,512]{1,0:T(8,128)(2,1)} %get-tuple-element.43) | copy-start | bytes 393220
  66.7 44.2 %all-to-all-start = ((bf16[32,16,2048]{2,1,0:T(8,128)(2,1)}), bf16[32,16,2048]{2,1,0:T(8,128)(2,1)S(1)}, u32[]{:S(2)}, u32[]{:S(2)}) async-start(bf16[32,16,2048]{2,1,0:T(8,128)(2,1)} %bitcast.20), calls=%async_computation | async-start | bytes 4194304 | tf_op jit(solution)/shard_map/all_to_all | solution.py:416
  80.9 14.5 %copy-start.6 = (bf16[128,512]{1,0:T(8,128)(2,1)S(1)}, bf16[128,512]{1,0:T(8,128)(2,1)}, u32[]{:S(2)}) copy-start(bf16[128,512]{1,0:T(8,128)(2,1)} %get-tuple-element.37) | copy-start | bytes 393220
  80.9 19.9 %copy-start.1 = (bf16[128,4224]{1,0:T(8,128)(2,1)S(1)}, bf16[128,4224]{1,0:T(8,128)(2,1)}, u32[]{:S(2)}) copy-start(bf16[128,4224]{1,0:T(8,128)(2,1)} %copy-done) | copy-start | bytes 3244036
  80.9 19.9 %copy-start.2 = (f32[128,512]{1,0:T(8,128)S(1)}, f32[128,512]{1,0:T(8,128)}, u32[]{:S(2)}) copy-start(f32[128,512]{1,0:T(8,128)} %get-tuple-element.32.own_a) | copy-start | bytes 786436
  80.9 19.9 %copy-start.3 = (f32[128,512]{1,0:T(8,128)S(1)}, f32[128,512]{1,0:T(8,128)}, u32[]{:S(2)}) copy-start(f32[128,512]{1,0:T(8,128)} %get-tuple-element.33.own_b) | copy-start | bytes 786436
  80.9 19.9 %copy-start.4 = (bf16[128,128]{1,0:T(8,128)(2,1)S(1)}, bf16[128,128]{1,0:T(8,128)(2,1)}, u32[]{:S(2)}) copy-start(bf16[128,128]{1,0:T(8,128)(2,1)} %get-tuple-element.31.refs_20_.extra_own) | copy-start | bytes 98308
  80.9 19.9 %copy-start.5 = (s32[2]{0:T(128)S(1)}, s32[2]{0:T(128)}, u32[]{:S(2)}) copy-start(s32[2]{0:T(128)} %pad_add_fusion.where_ref) | copy-start | bytes 28
  81.0 6.2 %collective-permute-start.27 = (bf16[128,512]{1,0:T(8,128)(2,1)S(1)}, bf16[128,512]{1,0:T(8,128)(2,1)S(1)}, u32[]{:S(2)}, u32[]{:S(2)}) collective-permute-start(bf16[128,512]{1,0:T(8,128)(2,1)S(1)} %add_convert_fusion.2), channel_id=1, source_target_pairs={{0,2},{2,4},{4,6},{6,8},{8,10},{10,12},{12,14},{14,0},{1,3},{3,5},... | collective-permute-start | bytes 393224 | tf_op jit(solution)/shard_map/ppermute | solution.py:35
  81.2 6.1 %collective-permute-start.24 = (bf16[128,512]{1,0:T(8,128)(2,1)S(1)}, bf16[128,512]{1,0:T(8,128)(2,1)S(1)}, u32[]{:S(2)}, u32[]{:S(2)}) collective-permute-start(bf16[128,512]{1,0:T(8,128)(2,1)S(1)} %add_convert_fusion.4), channel_id=1, source_target_pairs={{0,14},{2,0},{4,2},{6,4},{8,6},{10,8},{12,10},{14,12},{1,15},{3,1}... | collective-permute-start | bytes 393224 | tf_op jit(solution)/shard_map/ppermute | solution.py:35
  83.9 6.2 %collective-permute-start.21 = (bf16[128,512]{1,0:T(8,128)(2,1)S(1)}, bf16[128,512]{1,0:T(8,128)(2,1)S(1)}, u32[]{:S(2)}, u32[]{:S(2)}) collective-permute-start(bf16[128,512]{1,0:T(8,128)(2,1)S(1)} %add_convert_fusion.6), channel_id=1, source_target_pairs={{0,2},{2,4},{4,6},{6,8},{8,10},{10,12},{12,14},{14,0},{1,3},{3,5},... | collective-permute-start | bytes 393224 | tf_op jit(solution)/shard_map/ppermute | solution.py:35
  84.1 6.1 %collective-permute-start.17 = (bf16[128,512]{1,0:T(8,128)(2,1)S(1)}, bf16[128,512]{1,0:T(8,128)(2,1)S(1)}, u32[]{:S(2)}, u32[]{:S(2)}) collective-permute-start(bf16[128,512]{1,0:T(8,128)(2,1)S(1)} %add_convert_fusion.9), channel_id=1, source_target_pairs={{0,14},{2,0},{4,2},{6,4},{8,6},{10,8},{12,10},{14,12},{1,15},{3,1}... | collective-permute-start | bytes 393224 | tf_op jit(solution)/shard_map/ppermute | solution.py:35
  87.2 5.8 %collective-permute-start.28 = (bf16[128,512]{1,0:T(8,128)(2,1)S(1)}, bf16[128,512]{1,0:T(8,128)(2,1)S(1)}, u32[]{:S(2)}, u32[]{:S(2)}) collective-permute-start(bf16[128,512]{1,0:T(8,128)(2,1)S(1)} %add_convert_fusion.1), channel_id=1, source_target_pairs={{0,2},{2,4},{4,6},{6,8},{8,10},{10,12},{12,14},{14,0},{1,3},{3,5},... | collective-permute-start | bytes 393224 | tf_op jit(solution)/shard_map/ppermute | solution.py:35
  87.4 11.5 %collective-permute-start.25 = (bf16[128,512]{1,0:T(8,128)(2,1)S(1)}, bf16[128,512]{1,0:T(8,128)(2,1)S(1)}, u32[]{:S(2)}, u32[]{:S(2)}) collective-permute-start(bf16[128,512]{1,0:T(8,128)(2,1)S(1)} %add_convert_fusion.3), channel_id=1, source_target_pairs={{0,14},{2,0},{4,2},{6,4},{8,6},{10,8},{12,10},{14,12},{1,15},{3,1}... | collective-permute-start | bytes 393224 | tf_op jit(solution)/shard_map/ppermute | solution.py:35
  90.1 8.8 %collective-permute-start.22 = (bf16[128,512]{1,0:T(8,128)(2,1)S(1)}, bf16[128,512]{1,0:T(8,128)(2,1)S(1)}, u32[]{:S(2)}, u32[]{:S(2)}) collective-permute-start(bf16[128,512]{1,0:T(8,128)(2,1)S(1)} %add_convert_fusion.5), channel_id=1, source_target_pairs={{0,2},{2,4},{4,6},{6,8},{8,10},{10,12},{12,14},{14,0},{1,3},{3,5},... | collective-permute-start | bytes 393224 | tf_op jit(solution)/shard_map/ppermute | solution.py:35
  90.3 5.1 %collective-permute-start.18 = (bf16[128,512]{1,0:T(8,128)(2,1)S(1)}, bf16[128,512]{1,0:T(8,128)(2,1)S(1)}, u32[]{:S(2)}, u32[]{:S(2)}) collective-permute-start(bf16[128,512]{1,0:T(8,128)(2,1)S(1)} %add_convert_fusion.8), channel_id=1, source_target_pairs={{0,14},{2,0},{4,2},{6,4},{8,6},{10,8},{12,10},{14,12},{1,15},{3,1}... | collective-permute-start | bytes 393224 | tf_op jit(solution)/shard_map/ppermute | solution.py:35
  93.1 6.1 %collective-permute-start.29 = (bf16[128,512]{1,0:T(8,128)(2,1)S(1)}, bf16[128,512]{1,0:T(8,128)(2,1)S(1)}, u32[]{:S(2)}, u32[]{:S(2)}) collective-permute-start(bf16[128,512]{1,0:T(8,128)(2,1)S(1)} %add_convert_fusion), channel_id=1, source_target_pairs={{0,2},{2,4},{4,6},{6,8},{8,10},{10,12},{12,14},{14,0},{1,3},{3,5},... | collective-permute-start | bytes 393224 | tf_op jit(solution)/shard_map/ppermute | solution.py:35
  95.4 5.4 %collective-permute-start.19 = (bf16[128,512]{1,0:T(8,128)(2,1)S(1)}, bf16[128,512]{1,0:T(8,128)(2,1)S(1)}, u32[]{:S(2)}, u32[]{:S(2)}) collective-permute-start(bf16[128,512]{1,0:T(8,128)(2,1)S(1)} %add_convert_fusion.7), channel_id=1, source_target_pairs={{0,14},{2,0},{4,2},{6,4},{8,6},{10,8},{12,10},{14,12},{1,15},{3,1}... | collective-permute-start | bytes 393224 | tf_op jit(solution)/shard_map/ppermute | solution.py:35
  (17 other events, 130.6 us)

commit v4 on v3

--- a/solution.py
+++ b/solution.py
@@ -17,11 +17,9 @@
 BLK = 2 * ROWS
 HALF_Q = H * HD // 2
 HALF_KV = KV * HD // 2
-HEADS_KV = H // KV
-STEP_HEADS = 8
-CHUNK = STEP_HEADS * HD
-WIDTH = STEP_HEADS * ROWS
-STEPS = 2 * HALF_Q // CHUNK
+HEADS = H // KV
+WIDTH = HEADS * ROWS
+CHUNK = HALF_Q
 SLOTS = N_DP * 2 * CAP
 LAY_OUT = 4
 NEG = -1e30
@@ -53,9 +51,9 @@
     keys_in = refs[0:16]
     q_own, q_par, g_own, g_par, extra_own, extra_par, packed_ref = refs[16:23]
     kv_out = refs[23:39]
-    (kbuf, kt, sbuf, bias, acc, dqt, onehot, mx, den, deltas, active) = refs[39:]
+    (kbuf, kt, sbuf, bias, acc, dqt, onehot, mx, den, deltas) = refs[39:]
     step = pl.program_id(0)
-    half = step // (STEPS // 2)
+    half = step
     z = where_ref[0]
     y = where_ref[1]
     factor = HD**-0.5
@@ -72,61 +70,62 @@
                 for g in range(2):
                     kt[g, :, pl.ds(start, ROWS)] = block[:, g * HD : (g + 1) * HD].T
 
-    @pl.when(step % (STEPS // 2) == 0)
-    def _mask():
-        extra = jnp.where(half == 0, extra_own[...], extra_par[...]).astype(F32).T
-        deltas[...] = extra[0 : H // 2] + extra[H // 2 : H] + extra[H : 3 * H // 2]
-        target = slots_of(extra, y ^ half)
-        base = z * BLK + ROWS * (y ^ half)
-        slot = lax.broadcasted_iota(jnp.int32, (SLOTS // 2, ROWS), 0)
-        slot = (slot // CAP) * (2 * CAP) + (y ^ half) * CAP + slot % CAP
-        onehot[...] = jnp.where(slot == target, 1.0, 0.0).astype(BF16)
-        query_pos = base + lax.broadcasted_iota(jnp.int32, (1, ROWS), 1)
-        first = jnp.zeros((1, ROWS), jnp.int32)
-        last = jnp.full((1, ROWS), NZ * BLK, jnp.int32)
-        low = jnp.int32(0)
-        high = jnp.int32(NZ * BLK)
-        for d in range(8):
-            end = ends_ref[d]
-            first = jnp.where(end <= query_pos, jnp.maximum(first, end), first)
-            last = jnp.where(end > query_pos, jnp.minimum(last, end), last)
-            low = jnp.where(end <= base, jnp.maximum(low, end), low)
-            high = jnp.where(end > base + ROWS - 1, jnp.minimum(high, end), high)
-        last = last - 1
-        i_blk = 4 * z + 2 * (y ^ half)
-        low = low // ROWS
-        active[0] = low
-        active[1] = (high + ROWS - 1) // ROWS - low
-
-        def mask(n, carry):
-            for jb in range(2):
-                j_blk = 2 * n + jb
-                start = pl.multiple_of(j_blk * 64, 64)
-                key_pos = start + lax.broadcasted_iota(jnp.int32, (64, ROWS), 0)
-                tier = jnp.where(
-                    lax.broadcasted_iota(jnp.int32, (1, ROWS), 1) < 64,
-                    tiers_ref[i_blk * 32 + j_blk],
-                    tiers_ref[(i_blk + 1) * 32 + j_blk],
-                )
-                reach = jnp.where(tier == 2, NZ * BLK, jnp.where(tier == 1, query_pos, -1))
-                ok = (key_pos >= first) & (key_pos <= jnp.minimum(reach, last))
-                bias[pl.ds(start, 64), :] = jnp.where(ok, 0.0, NEG)
-            return carry
-
-        lax.fori_loop(low, low + active[1], mask, 0)
-
-    kv_head = (step // (HEADS_KV // STEP_HEADS)) % 2
-    first_block = active[0]
-    n_blocks = active[1]
+    extra = jnp.where(half == 0, extra_own[...], extra_par[...]).astype(F32).T
+    deltas[...] = extra[0 : H // 2] + extra[H // 2 : H] + extra[H : 3 * H // 2]
+    target = slots_of(extra, y ^ half)
+    base = z * BLK + ROWS * (y ^ half)
+    slot = lax.broadcasted_iota(jnp.int32, (SLOTS // 2, ROWS), 0)
+    slot = (slot // CAP) * (2 * CAP) + (y ^ half) * CAP + slot % CAP
+    onehot[...] = jnp.where(slot == target, 1.0, 0.0).astype(BF16)
+    query_pos = base + lax.broadcasted_iota(jnp.int32, (1, ROWS), 1)
+    first = jnp.zeros((1, ROWS), jnp.int32)
+    last = jnp.full((1, ROWS), NZ * BLK, jnp.int32)
+    low = jnp.int32(0)
+    high = jnp.int32(NZ * BLK)
+    for d in range(8):
+        end = ends_ref[d]
+        first = jnp.where(end <= query_pos, jnp.maximum(first, end), first)
+        last = jnp.where(end > query_pos, jnp.minimum(last, end), last)
+        low = jnp.where(end <= base, jnp.maximum(low, end), low)
+        high = jnp.where(end > base + ROWS - 1, jnp.minimum(high, end), high)
+    last = last - 1
+    i_blk = 4 * z + 2 * (y ^ half)
+    low = low // ROWS
+    first_block = low
+    n_blocks = (high + ROWS - 1) // ROWS - low
+
+    def mask(n, carry):
+        for jb in range(2):
+            j_blk = 2 * n + jb
+            start = pl.multiple_of(j_blk * 64, 64)
+            key_pos = start + lax.broadcasted_iota(jnp.int32, (64, ROWS), 0)
+            tier = jnp.where(
+                lax.broadcasted_iota(jnp.int32, (1, ROWS), 1) < 64,
+                tiers_ref[i_blk * 32 + j_blk],
+                tiers_ref[(i_blk + 1) * 32 + j_blk],
+            )
+            reach = jnp.where(tier == 2, NZ * BLK, jnp.where(tier == 1, query_pos, -1))
+            ok = (key_pos >= first) & (key_pos <= jnp.minimum(reach, last))
+            bias[pl.ds(start, 64), :] = jnp.where(ok, 0.0, NEG)
+        return carry
+
+    lax.fori_loop(low, low + n_blocks, mask, 0)
+
     own = half == 0
     q_all = jnp.where(own, q_own[...], q_par[...])
     g_all = jnp.where(own, g_own[...], g_par[...])
-    q = jnp.concatenate([q_all[:, h * HD : (h + 1) * HD] for h in range(STEP_HEADS)], axis=0)
-    g = jnp.concatenate([g_all[:, h * HD : (h + 1) * HD] for h in range(STEP_HEADS)], axis=0)
-    head = (step % (STEPS // 2)) * STEP_HEADS
-    delta = jnp.concatenate([deltas[pl.ds(head + h, 1), :] for h in range(STEP_HEADS)], axis=1)
-    k_cols = pl.ds(pl.multiple_of(kv_head * HD, HD), HD)
-    v_cols = pl.ds(pl.multiple_of(HALF_KV + kv_head * HD, HD), HD)
+    groups = []
+    for kv_head in range(2):
+        heads = range(kv_head * HEADS, (kv_head + 1) * HEADS)
+        groups.append(
+            (
+                slice(kv_head * HD, (kv_head + 1) * HD),
+                slice(HALF_KV + kv_head * HD, HALF_KV + (kv_head + 1) * HD),
+                jnp.concatenate([q_all[:, h * HD : (h + 1) * HD] for h in heads], axis=0),
+                jnp.concatenate([g_all[:, h * HD : (h + 1) * HD] for h in heads], axis=0),
+                jnp.concatenate([deltas[h : h + 1, :] for h in heads], axis=1),
+            )
+        )
     mx[...] = jnp.full_like(mx, NEG)
     den[...] = jnp.zeros_like(den)
     dqt[...] = jnp.zeros_like(dqt)
@@ -146,38 +145,40 @@
 
     def score(start, count):
         rows = pl.ds(start, count)
-        s = lax.dot_general(kbuf[rows, k_cols], q, NT, preferred_element_type=F32)
-        s = s * to_log2 + jnp.concatenate([bias[rows, :]] * STEP_HEADS, axis=1)
-        sbuf[rows, :] = s
-        s = s.reshape(count // 8, 8, WIDTH)
-        old = mx[...]
-        new = jnp.maximum(old, jnp.max(s, axis=0))
-        mx[...] = new
-        den[...] = den[...] * jnp.exp2(old - new) + jnp.sum(jnp.exp2(s - new[None]), axis=0)
+        mask = jnp.concatenate([bias[rows, :]] * HEADS, axis=1)
+        for n, (k_cols, v_cols, q, g, delta) in enumerate(groups):
+            s = lax.dot_general(kbuf[rows, k_cols], q, NT, preferred_element_type=F32)
+            s = s * to_log2 + mask
+            sbuf[n, rows, :] = s
+            s = s.reshape(count // 8, 8, WIDTH)
+            old = mx[n]
+            new = jnp.maximum(old, jnp.max(s, axis=0))
+            mx[n] = new
+            den[n] = den[n] * jnp.exp2(old - new) + jnp.sum(jnp.exp2(s - new[None]), axis=0)
 
     over_keys(score)
-    top = jnp.max(mx[...], axis=0, keepdims=True)
-    lse = top + jnp.log2(jnp.sum(den[...] * jnp.exp2(mx[...] - top), axis=0, keepdims=True))
+    top = jnp.max(mx[...], axis=1, keepdims=True)
+    lse = top + jnp.log2(jnp.sum(den[...] * jnp.exp2(mx[...] - top), axis=1, keepdims=True))
 
     def backward(start, count):
         rows = pl.ds(start, count)
-        w = jnp.exp2(sbuf[rows, :] - lse)
-        dp = lax.dot_general(kbuf[rows, v_cols], g, NT, preferred_element_type=F32)
-        ds = (w * (dp - delta)).astype(BF16)
-        acc[rows, v_cols] += lax.dot_general(w.astype(BF16), g, NN, preferred_element_type=F32)
-        acc[rows, k_cols] += lax.dot_general(ds, q, NN, preferred_element_type=F32)
-        dqt[...] += lax.dot_general(kt[kv_head, :, rows], ds, NN, preferred_element_type=F32)
+        for n, (k_cols, v_cols, q, g, delta) in enumerate(groups):
+            w = jnp.exp2(sbuf[n, rows, :] - lse[n])
+            dp = lax.dot_general(kbuf[rows, v_cols], g, NT, preferred_element_type=F32)
+            ds = (w * (dp - delta)).astype(BF16)
+            acc[rows, v_cols] += lax.dot_general(w.astype(BF16), g, NN, preferred_element_type=F32)
+            acc[rows, k_cols] += lax.dot_general(ds, q, NN, preferred_element_type=F32)
+            dqt[n] += lax.dot_general(kt[n, :, rows], ds, NN, preferred_element_type=F32)
 
     over_keys(backward)
     low_dq = (dqt[...] * factor).astype(BF16)
-    for h in range(STEP_HEADS):
+    for h in range(2 * HEADS):
+        rows = low_dq[h // HEADS, :, (h % HEADS) * ROWS : (h % HEADS + 1) * ROWS]
         packed_ref[:, 0, :, h * HD : (h + 1) * HD] = (
-            lax.dot_general(onehot[...], low_dq[:, h * ROWS : (h + 1) * ROWS], NT, preferred_element_type=F32)
-            .astype(BF16)
-            .reshape(N_DP, CAP, HD)
+            lax.dot_general(onehot[...], rows, NT, preferred_element_type=F32).astype(BF16).reshape(N_DP, CAP, HD)
         )
 
-    @pl.when(step == STEPS - 1)
+    @pl.when(step == 1)
     def _finish():
         for r in range(NZ):
             for part in range(2):
@@ -191,44 +192,35 @@
     block = pl.BlockSpec((ROWS, 2 * HALF_KV), lambda c, where, ends, tiers: (0, 0))
     extra = pl.BlockSpec((ROWS, HD), lambda c, where, ends, tiers: (0, 0))
     extra_par = pl.BlockSpec((ROWS, HD), lambda c, where, ends, tiers: (0, 2 * HALF_Q // HD))
-    per_half = STEPS // 2
-
-    def own_at(c, where, ends, tiers):
-        return 0, where[1] * per_half + jnp.minimum(c, per_half - 1)
-
-    def partner_at(c, where, ends, tiers):
-        return 0, jnp.maximum(c - per_half, 0)
-
-    def partner_g_at(c, where, ends, tiers):
-        return 0, per_half + jnp.maximum(c - per_half, 0)
+
+    def at(column):
+        return pl.BlockSpec((ROWS, CHUNK), lambda c, where, ends, tiers: (0, column))
+
+    own = pl.BlockSpec((ROWS, CHUNK), lambda c, where, ends, tiers: (0, where[1]))
 
     def out_at(c, where, ends, tiers):
-        return 0, where[1] ^ (c // per_half), 0, c % per_half
-
-    own = pl.BlockSpec((ROWS, CHUNK), own_at)
-    partner = pl.BlockSpec((ROWS, CHUNK), partner_at)
-    partner_g = pl.BlockSpec((ROWS, CHUNK), partner_g_at)
+        return 0, where[1] ^ c, 0, 0
+
     kv_bf16 = jax.ShapeDtypeStruct((ROWS, 2 * HALF_KV), BF16)
     kv_f32 = jax.ShapeDtypeStruct((ROWS, 2 * HALF_KV), F32)
     return pl.pallas_call(
         grads_kernel,
         grid_spec=pltpu.PrefetchScalarGridSpec(
             num_scalar_prefetch=3,
-            grid=(STEPS,),
-            in_specs=[block] * 16 + [own, partner, own, partner_g, extra, extra_par],
+            grid=(2,),
+            in_specs=[block] * 16 + [own, at(0), own, at(1), extra, extra_par],
             out_specs=[pl.BlockSpec((N_DP, 1, CAP, CHUNK), out_at)] + [block] * 16,
             scratch_shapes=[
                 pltpu.VMEM((NZ * BLK, 2 * HALF_KV), BF16),
                 pltpu.VMEM((2, HD, NZ * BLK), BF16),
-                pltpu.VMEM((NZ * BLK, WIDTH), F32),
+                pltpu.VMEM((2, NZ * BLK, WIDTH), F32),
                 pltpu.VMEM((NZ * BLK, ROWS), F32),
                 pltpu.VMEM((NZ * BLK, 2 * HALF_KV), F32),
-                pltpu.VMEM((HD, WIDTH), F32),
+                pltpu.VMEM((2, HD, WIDTH), F32),
                 pltpu.VMEM((SLOTS // 2, ROWS), BF16),
-                pltpu.VMEM((8, WIDTH), F32),
-                pltpu.VMEM((8, WIDTH), F32),
+                pltpu.VMEM((2, 8, WIDTH), F32),
+                pltpu.VMEM((2, 8, WIDTH), F32),
                 pltpu.VMEM((H // 2, ROWS), F32),
-                pltpu.SMEM((2,), jnp.int32),
             ],
         ),
         out_shape=[jax.ShapeDtypeStruct((N_DP, 2, CAP, HALF_Q), BF16)] + [kv_f32] * 2 + [kv_bf16] * 14,

time: 129 us -> 126 us (0.977)
    all_to_all x1, starting transfers between devices: 14.2 us -> 11.9 us  [to_owners(): lax.all_to_all(rows.reshape(2 * N_DP, CAP, -1), ('dp', 'yl'), split_axis=...]
    pallas_call x1, Pallas kernels: 13.8 us -> 12.5 us  [attention_grads(): pl.pallas_call(grads_kernel, grid_spec=pltpu.PrefetchScalarGridSpec(num_s...]
where the time goes in v4:
time: 126 us
  starting transfers between devices  68.3 us (54%)
  Pallas kernels  19.2 us (15%)
  waiting for transfers between devices  16.8 us (13%)
  blocking collectives  15.7 us (12%)
  local copies, waits for them, and re-layouts  4.07 us (3%)
  other arithmetic  1.73 us (1%)
    ppermute x28, starting transfers between devices, zshift(): return lax.ppermute(x, 'z', [(i, (i + by) % NZ) for i in range(NZ)])  54 us
    all_to_all x1, blocking collectives, to_owners(): lax.all_to_all(rows.reshape(2 * N_DP, CAP, -1), ('dp', 'yl'), split_axis=...  15.7 us
    pallas_call x1, Pallas kernels, attention_grads(): pl.pallas_call(grads_kernel, grid_spec=pltpu.PrefetchScalarGridSpec(num_s...  12.5 us
    all_to_all x1, starting transfers between devices, to_owners(): lax.all_to_all(rows.reshape(2 * N_DP, CAP, -1), ('dp', 'yl'), split_axis=...  11.9 us
    all_to_all x1, waiting for transfers between devices, to_owners(): lax.all_to_all(rows.reshape(2 * N_DP, CAP, -1), ('dp', 'yl'), split_axis=...  9.25 us
    ppermute x28, waiting for transfers between devices, zshift(): return lax.ppermute(x, 'z', [(i, (i + by) % NZ) for i in range(NZ)])  7.59 us
    pallas_call x1, Pallas kernels, prepare(): pl.pallas_call(prepare_kernel, grid_spec=pltpu.PrefetchScalarGridSpec(num...  3.73 us
  transfers between devices with their start and end apart: 31, of which 10 were waited for; matrix products, arithmetic and copies ran while one was open for 3% of the time, Pallas kernels for 4%

profile of v4, /device:TPU:1, one launch (start us, length us, event | category | flops | bytes accessed | tf_op | source)
XLA Modules:
  0.0 126.3 jit_solution(4378449151710236553)
XLA Ops:
  0.0 1.0 dynamic-slice_bitcast_fusion
  1.0 2.2 %collective-permute-start = (bf16[128,512]{1,0:T(8,128)(2,1)S(1)}, bf16[128,512]{1,0:T(8,128)(2,1)S(1)}, u32[]{:S(2)}, u32[]{:S(2)}) collective-permute-start(bf16[128,512]{1,0:T(8,128)(2,1)S(1)} %pad_maximum_fusion.1), channel_id=1, source_target_pairs={{0,1},{1,0},{2,3},{3,2},{4,5},{5,4},{6,7},{7,6},{8,9},{9,8},{10,11... | collective-permute-start | bytes 393224 | tf_op jit(solution)/shard_map/ppermute | solution.py:37
  3.2 1.4 %copy.9.owners_ref = s32[128,1]{1,0:T(8,128)} copy(s32[128,1]{0,1:T(1,128)} %bitcast.26) | data formatting | bytes 1024 | tf_op jit(solution)/shard_map/squeeze | solution.py:366
  4.6 3.7 %prepare.1 = (bf16[128,4224]{1,0:T(8,128)(2,1)}, bf16[128,128]{1,0:T(8,128)(2,1)}) custom-call(s32[1]{0:T(128)} %bitcast.1.where_ref, bf16[128,4096]{1,0:T(8,128)(2,1)} %bitcast.22, bf16[128,4096]{1,0:T(8,128)(2,1)} %bitcast.24, bf16[128,4096]{1,0:T(8,128)(2,1)} %bitcast.21, s32[128,1]{1,0:T(8,128)} %copy.9.owners_ref), custom_call_target="tpu_custom_call" | custom-call | tf_op jit(solution)/shard_map/prepare/pallas_call | solution.py:330
  8.3 0.1 collective-permute-start.15
  8.5 1.9 %collective-permute-start.1 = (bf16[128,512]{1,0:T(8,128)(2,1)S(1)}, bf16[128,512]{1,0:T(8,128)(2,1)S(1)}, u32[]{:S(2)}, u32[]{:S(2)}) collective-permute-start(bf16[128,512]{1,0:T(8,128)(2,1)S(1)} %pad_maximum_fusion.refs_0_), channel_id=1, source_target_pairs={{0,2},{2,4},{4,6},{6,8},{8,10},{10,12},{12,14},{14,0},{1,3},{3,5},... | collective-permute-start | bytes 393224 | tf_op jit(solution)/shard_map/ppermute | solution.py:33
  10.3 4.0 %collective-permute-start.8 = (bf16[128,512]{1,0:T(8,128)(2,1)S(1)}, bf16[128,512]{1,0:T(8,128)(2,1)S(1)}, u32[]{:S(2)}, u32[]{:S(2)}) collective-permute-start(bf16[128,512]{1,0:T(8,128)(2,1)S(1)} %collective-permute-done.refs_1_), channel_id=1, source_target_pairs={{0,14},{2,0},{4,2},{6,4},{8,6},{10,8},{12,10},{14,12},{1,15},{3,1}... | collective-permute-start | bytes 393224 | tf_op jit(solution)/shard_map/ppermute | solution.py:33
  14.4 1.4 %collective-permute-start.12 = (bf16[128,512]{1,0:T(8,128)(2,1)S(1)}, bf16[128,512]{1,0:T(8,128)(2,1)S(1)}, u32[]{:S(2)}, u32[]{:S(2)}) collective-permute-start(bf16[128,512]{1,0:T(8,128)(2,1)S(1)} %pad_maximum_fusion.refs_0_), channel_id=1, source_target_pairs={{0,14},{2,0},{4,2},{6,4},{8,6},{10,8},{12,10},{14,12},{1,15},{3,1}... | collective-permute-start | bytes 393224 | tf_op jit(solution)/shard_map/ppermute | solution.py:33
  15.7 0.1 collective-permute-start.2
  15.8 0.8 collective-permute-done.1.refs_2_
  16.6 2.7 %collective-permute-start.9 = (bf16[128,512]{1,0:T(8,128)(2,1)S(1)}, bf16[128,512]{1,0:T(8,128)(2,1)S(1)}, u32[]{:S(2)}, u32[]{:S(2)}) collective-permute-start(bf16[128,512]{1,0:T(8,128)(2,1)S(1)} %collective-permute-done.8.refs_15_), channel_id=1, source_target_pairs={{0,14},{2,0},{4,2},{6,4},{8,6},{10,8},{12,10},{14,12},{1,15},{3,1}... | collective-permute-start | bytes 393224 | tf_op jit(solution)/shard_map/ppermute | solution.py:33
  19.4 2.7 %collective-permute-start.13 = (bf16[128,512]{1,0:T(8,128)(2,1)S(1)}, bf16[128,512]{1,0:T(8,128)(2,1)S(1)}, u32[]{:S(2)}, u32[]{:S(2)}) collective-permute-start(bf16[128,512]{1,0:T(8,128)(2,1)S(1)} %collective-permute-done.12.refs_14_), channel_id=1, source_target_pairs={{0,14},{2,0},{4,2},{6,4},{8,6},{10,8},{12,10},{14,12},{1,15},{3,1}... | collective-permute-start | bytes 393224 | tf_op jit(solution)/shard_map/ppermute | solution.py:33
  22.1 0.5 collective-permute-done.3.refs_4_
  22.7 2.7 %collective-permute-start.10 = (bf16[128,512]{1,0:T(8,128)(2,1)S(1)}, bf16[128,512]{1,0:T(8,128)(2,1)S(1)}, u32[]{:S(2)}, u32[]{:S(2)}) collective-permute-start(bf16[128,512]{1,0:T(8,128)(2,1)S(1)} %collective-permute-done.9.refs_13_), channel_id=1, source_target_pairs={{0,14},{2,0},{4,2},{6,4},{8,6},{10,8},{12,10},{14,12},{1,15},{3,1}... | collective-permute-start | bytes 393224 | tf_op jit(solution)/shard_map/ppermute | solution.py:33
  25.4 2.3 %collective-permute-start.14 = (bf16[128,512]{1,0:T(8,128)(2,1)S(1)}, bf16[128,512]{1,0:T(8,128)(2,1)S(1)}, u32[]{:S(2)}, u32[]{:S(2)}) collective-permute-start(bf16[128,512]{1,0:T(8,128)(2,1)S(1)} %collective-permute-done.13.refs_12_), channel_id=1, source_target_pairs={{0,14},{2,0},{4,2},{6,4},{8,6},{10,8},{12,10},{14,12},{1,15},{3,1}... | collective-permute-start | bytes 393224 | tf_op jit(solution)/shard_map/ppermute | solution.py:33
  27.6 0.9 collective-permute-done.5.refs_6_
  28.6 0.1 collective-permute-done.10.refs_11_
  28.7 3.2 %collective-permute-start.11 = (bf16[128,512]{1,0:T(8,128)(2,1)S(1)}, bf16[128,512]{1,0:T(8,128)(2,1)S(1)}, u32[]{:S(2)}, u32[]{:S(2)}) collective-permute-start(bf16[128,512]{1,0:T(8,128)(2,1)S(1)} %collective-permute-done.10.refs_11_), channel_id=1, source_target_pairs={{0,14},{2,0},{4,2},{6,4},{8,6},{10,8},{12,10},{14,12},{1,15},{3,1}... | collective-permute-start | bytes 393224 | tf_op jit(solution)/shard_map/ppermute | solution.py:33
  31.9 0.7 reshape_squeeze.3.tiers_ref
  32.6 0.7 reduce-window.9
  33.3 0.7 pad_add_fusion.where_ref
  34.0 0.8 collective-permute-done.7.refs_8_
  35.0 0.5 copy-done.31
  35.4 0.0 copy-done.32
  35.5 0.4 copy-done
  35.9 12.5 %grads.1 = (bf16[16,2,16,2048]{3,2,1,0:T(8,128)(2,1)}, f32[128,512]{1,0:T(8,128)}, f32[128,512]{1,0:T(8,128)}, bf16[128,512]{1,0:T(8,128)(2,1)}, bf16[128,512]{1...) custom-call(s32[2]{0:T(128)} %pad_add_fusion.where_ref, ...), custom_call_target="tpu_custom_call" | custom-call | flops 8000000000 | bytes 10485760 | tf_op jit(solution)/shard_map/grads/pallas_call | solution.py:206
  48.4 2.6 %collective-permute-start.26 = (bf16[128,512]{1,0:T(8,128)(2,1)}, bf16[128,512]{1,0:T(8,128)(2,1)S(1)}, u32[]{:S(2)}, u32[]{:S(2)}) collective-permute-start(bf16[128,512]{1,0:T(8,128)(2,1)} %get-tuple-element.44), channel_id=1, source_target_pairs={{0,2},{2,4},{4,6},{6,8},{8,10},{10,12},{12,14},{14,0},{1,3},{3,5},... | collective-permute-start | bytes 393224 | tf_op jit(solution)/shard_map/ppermute | solution.py:33
  51.0 12.9 %collective-permute-start.23 = (bf16[128,512]{1,0:T(8,128)(2,1)}, bf16[128,512]{1,0:T(8,128)(2,1)S(1)}, u32[]{:S(2)}, u32[]{:S(2)}) collective-permute-start(bf16[128,512]{1,0:T(8,128)(2,1)} %get-tuple-element.41), channel_id=1, source_target_pairs={{0,14},{2,0},{4,2},{6,4},{8,6},{10,8},{12,10},{14,12},{1,15},{3,1}... | collective-permute-start | bytes 393224 | tf_op jit(solution)/shard_map/ppermute | solution.py:33
  63.9 2.7 %collective-permute-start.16 = (bf16[128,512]{1,0:T(8,128)(2,1)}, bf16[128,512]{1,0:T(8,128)(2,1)S(1)}, u32[]{:S(2)}, u32[]{:S(2)}) collective-permute-start(bf16[128,512]{1,0:T(8,128)(2,1)} %get-tuple-element.34), channel_id=1, source_target_pairs={{0,14},{2,0},{4,2},{6,4},{8,6},{10,8},{12,10},{14,12},{1,15},{3,1}... | collective-permute-start | bytes 393224 | tf_op jit(solution)/shard_map/ppermute | solution.py:33
  66.6 11.9 %all-to-all-start = ((bf16[32,16,2048]{2,1,0:T(8,128)(2,1)}), bf16[32,16,2048]{2,1,0:T(8,128)(2,1)S(1)}, u32[]{:S(2)}, u32[]{:S(2)}) async-start(bf16[32,16,2048]{2,1,0:T(8,128)(2,1)} %bitcast.20), calls=%async_computation | async-start | bytes 4194304 | tf_op jit(solution)/shard_map/all_to_all | solution.py:408
  78.7 0.1 collective-permute-start.27
  78.9 2.7 %collective-permute-start.24 = (bf16[128,512]{1,0:T(8,128)(2,1)S(1)}, bf16[128,512]{1,0:T(8,128)(2,1)S(1)}, u32[]{:S(2)}, u32[]{:S(2)}) collective-permute-start(bf16[128,512]{1,0:T(8,128)(2,1)S(1)} %add_convert_fusion.4), channel_id=1, source_target_pairs={{0,14},{2,0},{4,2},{6,4},{8,6},{10,8},{12,10},{14,12},{1,15},{3,1}... | collective-permute-start | bytes 393224 | tf_op jit(solution)/shard_map/ppermute | solution.py:33
  81.6 0.1 collective-permute-start.21
  81.8 2.7 %collective-permute-start.17 = (bf16[128,512]{1,0:T(8,128)(2,1)S(1)}, bf16[128,512]{1,0:T(8,128)(2,1)S(1)}, u32[]{:S(2)}, u32[]{:S(2)}) collective-permute-start(bf16[128,512]{1,0:T(8,128)(2,1)S(1)} %add_convert_fusion.9), channel_id=1, source_target_pairs={{0,14},{2,0},{4,2},{6,4},{8,6},{10,8},{12,10},{14,12},{1,15},{3,1}... | collective-permute-start | bytes 393224 | tf_op jit(solution)/shard_map/ppermute | solution.py:33
  84.5 0.4 collective-permute-done.27
  84.9 0.1 collective-permute-start.28
  85.1 2.7 %collective-permute-start.25 = (bf16[128,512]{1,0:T(8,128)(2,1)S(1)}, bf16[128,512]{1,0:T(8,128)(2,1)S(1)}, u32[]{:S(2)}, u32[]{:S(2)}) collective-permute-start(bf16[128,512]{1,0:T(8,128)(2,1)S(1)} %add_convert_fusion.3), channel_id=1, source_target_pairs={{0,14},{2,0},{4,2},{6,4},{8,6},{10,8},{12,10},{14,12},{1,15},{3,1}... | collective-permute-start | bytes 393224 | tf_op jit(solution)/shard_map/ppermute | solution.py:33
  87.8 0.1 collective-permute-start.22
  88.0 2.7 %collective-permute-start.18 = (bf16[128,512]{1,0:T(8,128)(2,1)S(1)}, bf16[128,512]{1,0:T(8,128)(2,1)S(1)}, u32[]{:S(2)}, u32[]{:S(2)}) collective-permute-start(bf16[128,512]{1,0:T(8,128)(2,1)S(1)} %add_convert_fusion.8), channel_id=1, source_target_pairs={{0,14},{2,0},{4,2},{6,4},{8,6},{10,8},{12,10},{14,12},{1,15},{3,1}... | collective-permute-start | bytes 393224 | tf_op jit(solution)/shard_map/ppermute | solution.py:33
  90.8 0.1 collective-permute-start.29
  90.8 2.0 %collective-permute-done.18 = bf16[128,512]{1,0:T(8,128)(2,1)S(1)} collective-permute-done((bf16[128,512]{1,0:T(8,128)(2,1)S(1)}, bf16[128,512]{1,0:T(8,128)(2,1)S(1)}, u32[]{:S(2)}, u32[]{:S(2)}) %collective-permute-start.18) | collective-permute-done | bytes 131104 | tf_op jit(solution)/shard_map/ppermute | solution.py:33
  92.9 3.5 %collective-permute-start.19 = (bf16[128,512]{1,0:T(8,128)(2,1)S(1)}, bf16[128,512]{1,0:T(8,128)(2,1)S(1)}, u32[]{:S(2)}, u32[]{:S(2)}) collective-permute-start(bf16[128,512]{1,0:T(8,128)(2,1)S(1)} %add_convert_fusion.7), channel_id=1, source_target_pairs={{0,14},{2,0},{4,2},{6,4},{8,6},{10,8},{12,10},{14,12},{1,15},{3,1}... | collective-permute-start | bytes 393224 | tf_op jit(solution)/shard_map/ppermute | solution.py:33
  96.4 0.3 collective-permute-done.29.up_b
  96.7 1.7 %collective-permute-done.19.down_a = bf16[128,512]{1,0:T(8,128)(2,1)S(1)} collective-permute-done((bf16[128,512]{1,0:T(8,128)(2,1)S(1)}, bf16[128,512]{1,0:T(8,128)(2,1)S(1)}, u32[]{:S(2)}, u32[]{:S(2)}) %collective-permute-start.19) | collective-permute-done | bytes 131104 | tf_op jit(solution)/shard_map/ppermute | solution.py:33
  98.4 0.9 finish.1
  99.3 9.3 %all-to-all-done.q_ref = bf16[32,16,2048]{2,1,0:T(8,128)(2,1)S(1)} async-done(((bf16[32,16,2048]{2,1,0:T(8,128)(2,1)}), bf16[32,16,2048]{2,1,0:T(8,128)(2,1)S(1)}, u32[]{:S(2)}, u32[]{:S(2)}) %all-to-all-start) | async-done | bytes 2097184 | tf_op jit(solution)/shard_map/all_to_all | solution.py:408
  108.6 15.7 %all_to_all.10.kv_ref = bf16[32,16,512]{2,1,0:T(8,128)(2,1)S(1)} all-to-all(bf16[32,16,512]{2,1,0:T(8,128)(2,1)S(1)} %bitcast.19), channel_id=1, replica_groups=mesh['dp'=16,'z'=8,'yl'=2] {'dp','yl'}, dimensions={0} | all-to-all | bytes 1048576 | tf_op jit(solution)/shard_map/all_to_all | solution.py:408
  124.3 2.0 %lay_out.1 = bf16[16,16,5120]{2,1,0:T(8,128)(2,1)} custom-call(bf16[32,16,2048]{2,1,0:T(8,128)(2,1)S(1)} %all-to-all-done.q_ref, bf16[32,16,512]{2,1,0:T(8,128)(2,1)S(1)} %all_to_all.10.kv_ref), custom_call_target="tpu_custom_call" | custom-call | tf_op jit(solution)/shard_map/lay_out/pallas_call | solution.py:279
  (104 shorter events, 0.6 us)
Async XLA Ops:
  0.0 31.9 %copy-start.17 = (s32[1,32,32]{2,1,0:T(8,128)S(1)}, s32[1,32,32]{2,1,0:T(8,128)}, u32[]{:S(2)}) copy-start(s32[1,32,32]{2,1,0:T(8,128)} %param.14) | copy-start | bytes 12292
  0.0 32.6 %copy-start.33 = (s32[1,8]{1,0:T(1,128)S(1)}, s32[1,8]{1,0:T(1,128)}, u32[]{:S(2)}) copy-start(s32[1,8]{1,0:T(1,128)} %param.13) | copy-start | bytes 100
  1.0 7.3 %collective-permute-start = (bf16[128,512]{1,0:T(8,128)(2,1)S(1)}, bf16[128,512]{1,0:T(8,128)(2,1)S(1)}, u32[]{:S(2)}, u32[]{:S(2)}) collective-permute-start(bf16[128,512]{1,0:T(8,128)(2,1)S(1)} %pad_maximum_fusion.1), channel_id=1, source_target_pairs={{0,1},{1,0},{2,3},{3,2},{4,5},{5,4},{6,7},{7,6},{8,9},{9,8},{10,11... | collective-permute-start | bytes 393224 | tf_op jit(solution)/shard_map/ppermute | solution.py:37
  8.3 26.5 %copy-start.18 = (bf16[128,512]{1,0:T(8,128)(2,1)}, bf16[128,512]{1,0:T(8,128)(2,1)S(1)}, u32[]{:S(2)}) copy-start(bf16[128,512]{1,0:T(8,128)(2,1)S(1)} %collective-permute-done.refs_1_) | copy-start | bytes 393220
  8.3 26.5 %collective-permute-start.15 = (bf16[128,4224]{1,0:T(8,128)(2,1)}, bf16[128,4224]{1,0:T(8,128)(2,1)S(1)}, u32[]{:S(2)}, u32[]{:S(2)}) collective-permute-start(bf16[128,4224]{1,0:T(8,128)(2,1)} %get-tuple-element.30), channel_id=1, source_target_pairs={{0,1},{1,0},{2,3},{3,2},{4,5},{5,4},{6,7},{7,6},{8,9},{9,8},{10,11... | collective-permute-start | bytes 3244040 | tf_op jit(solution)/shard_map/ppermute | solution.py:37
  8.5 26.4 %copy-start.16 = (bf16[128,512]{1,0:T(8,128)(2,1)}, bf16[128,512]{1,0:T(8,128)(2,1)S(1)}, u32[]{:S(2)}) copy-start(bf16[128,512]{1,0:T(8,128)(2,1)S(1)} %pad_maximum_fusion.refs_0_) | copy-start | bytes 393220
  8.5 8.2 %collective-permute-start.1 = (bf16[128,512]{1,0:T(8,128)(2,1)S(1)}, bf16[128,512]{1,0:T(8,128)(2,1)S(1)}, u32[]{:S(2)}, u32[]{:S(2)}) collective-permute-start(bf16[128,512]{1,0:T(8,128)(2,1)S(1)} %pad_maximum_fusion.refs_0_), channel_id=1, source_target_pairs={{0,2},{2,4},{4,6},{6,8},{8,10},{10,12},{12,14},{14,0},{1,3},{3,5},... | collective-permute-start | bytes 393224 | tf_op jit(solution)/shard_map/ppermute | solution.py:33
  10.3 6.3 %collective-permute-start.8 = (bf16[128,512]{1,0:T(8,128)(2,1)S(1)}, bf16[128,512]{1,0:T(8,128)(2,1)S(1)}, u32[]{:S(2)}, u32[]{:S(2)}) collective-permute-start(bf16[128,512]{1,0:T(8,128)(2,1)S(1)} %collective-permute-done.refs_1_), channel_id=1, source_target_pairs={{0,14},{2,0},{4,2},{6,4},{8,6},{10,8},{12,10},{14,12},{1,15},{3,1}... | collective-permute-start | bytes 393224 | tf_op jit(solution)/shard_map/ppermute | solution.py:33
  14.4 5.0 %collective-permute-start.12 = (bf16[128,512]{1,0:T(8,128)(2,1)S(1)}, bf16[128,512]{1,0:T(8,128)(2,1)S(1)}, u32[]{:S(2)}, u32[]{:S(2)}) collective-permute-start(bf16[128,512]{1,0:T(8,128)(2,1)S(1)} %pad_maximum_fusion.refs_0_), channel_id=1, source_target_pairs={{0,14},{2,0},{4,2},{6,4},{8,6},{10,8},{12,10},{14,12},{1,15},{3,1}... | collective-permute-start | bytes 393224 | tf_op jit(solution)/shard_map/ppermute | solution.py:33
  15.7 6.4 %collective-permute-start.2 = (bf16[128,512]{1,0:T(8,128)(2,1)S(1)}, bf16[128,512]{1,0:T(8,128)(2,1)S(1)}, u32[]{:S(2)}, u32[]{:S(2)}) collective-permute-start(bf16[128,512]{1,0:T(8,128)(2,1)S(1)} %collective-permute-done.refs_1_), channel_id=1, source_target_pairs={{0,2},{2,4},{4,6},{6,8},{8,10},{10,12},{12,14},{14,0},{1,3},{3,5},... | collective-permute-start | bytes 393224 | tf_op jit(solution)/shard_map/ppermute | solution.py:33
  16.6 18.2 %copy-start.19 = (bf16[128,512]{1,0:T(8,128)(2,1)}, bf16[128,512]{1,0:T(8,128)(2,1)S(1)}, u32[]{:S(2)}) copy-start(bf16[128,512]{1,0:T(8,128)(2,1)S(1)} %collective-permute-done.1.refs_2_) | copy-start | bytes 393220
  16.6 6.0 %collective-permute-start.3 = (bf16[128,512]{1,0:T(8,128)(2,1)S(1)}, bf16[128,512]{1,0:T(8,128)(2,1)S(1)}, u32[]{:S(2)}, u32[]{:S(2)}) collective-permute-start(bf16[128,512]{1,0:T(8,128)(2,1)S(1)} %collective-permute-done.1.refs_2_), channel_id=1, source_target_pairs={{0,2},{2,4},{4,6},{6,8},{8,10},{10,12},{12,14},{14,0},{1,3},{3,5},... | collective-permute-start | bytes 393224 | tf_op jit(solution)/shard_map/ppermute | solution.py:33
  16.6 18.2 %copy-start.20 = (bf16[128,512]{1,0:T(8,128)(2,1)}, bf16[128,512]{1,0:T(8,128)(2,1)S(1)}, u32[]{:S(2)}) copy-start(bf16[128,512]{1,0:T(8,128)(2,1)S(1)} %collective-permute-done.8.refs_15_) | copy-start | bytes 393220
  16.6 6.0 %collective-permute-start.9 = (bf16[128,512]{1,0:T(8,128)(2,1)S(1)}, bf16[128,512]{1,0:T(8,128)(2,1)S(1)}, u32[]{:S(2)}, u32[]{:S(2)}) collective-permute-start(bf16[128,512]{1,0:T(8,128)(2,1)S(1)} %collective-permute-done.8.refs_15_), channel_id=1, source_target_pairs={{0,14},{2,0},{4,2},{6,4},{8,6},{10,8},{12,10},{14,12},{1,15},{3,1}... | collective-permute-start | bytes 393224 | tf_op jit(solution)/shard_map/ppermute | solution.py:33
  19.4 15.5 %copy-start.21 = (bf16[128,512]{1,0:T(8,128)(2,1)}, bf16[128,512]{1,0:T(8,128)(2,1)S(1)}, u32[]{:S(2)}) copy-start(bf16[128,512]{1,0:T(8,128)(2,1)S(1)} %collective-permute-done.12.refs_14_) | copy-start | bytes 393220
  19.4 6.0 %collective-permute-start.13 = (bf16[128,512]{1,0:T(8,128)(2,1)S(1)}, bf16[128,512]{1,0:T(8,128)(2,1)S(1)}, u32[]{:S(2)}, u32[]{:S(2)}) collective-permute-start(bf16[128,512]{1,0:T(8,128)(2,1)S(1)} %collective-permute-done.12.refs_14_), channel_id=1, source_target_pairs={{0,14},{2,0},{4,2},{6,4},{8,6},{10,8},{12,10},{14,12},{1,15},{3,1}... | collective-permute-start | bytes 393224 | tf_op jit(solution)/shard_map/ppermute | solution.py:33
  22.1 5.5 %collective-permute-start.4 = (bf16[128,512]{1,0:T(8,128)(2,1)S(1)}, bf16[128,512]{1,0:T(8,128)(2,1)S(1)}, u32[]{:S(2)}, u32[]{:S(2)}) collective-permute-start(bf16[128,512]{1,0:T(8,128)(2,1)S(1)} %collective-permute-done.2.refs_3_), channel_id=1, source_target_pairs={{0,2},{2,4},{4,6},{6,8},{8,10},{10,12},{12,14},{14,0},{1,3},{3,5},... | collective-permute-start | bytes 393224 | tf_op jit(solution)/shard_map/ppermute | solution.py:33
  22.7 5.9 %collective-permute-start.5 = (bf16[128,512]{1,0:T(8,128)(2,1)S(1)}, bf16[128,512]{1,0:T(8,128)(2,1)S(1)}, u32[]{:S(2)}, u32[]{:S(2)}) collective-permute-start(bf16[128,512]{1,0:T(8,128)(2,1)S(1)} %collective-permute-done.3.refs_4_), channel_id=1, source_target_pairs={{0,2},{2,4},{4,6},{6,8},{8,10},{10,12},{12,14},{14,0},{1,3},{3,5},... | collective-permute-start | bytes 393224 | tf_op jit(solution)/shard_map/ppermute | solution.py:33
  22.7 6.0 %collective-permute-start.10 = (bf16[128,512]{1,0:T(8,128)(2,1)S(1)}, bf16[128,512]{1,0:T(8,128)(2,1)S(1)}, u32[]{:S(2)}, u32[]{:S(2)}) collective-permute-start(bf16[128,512]{1,0:T(8,128)(2,1)S(1)} %collective-permute-done.9.refs_13_), channel_id=1, source_target_pairs={{0,14},{2,0},{4,2},{6,4},{8,6},{10,8},{12,10},{14,12},{1,15},{3,1}... | collective-permute-start | bytes 393224 | tf_op jit(solution)/shard_map/ppermute | solution.py:33
  25.4 8.6 %collective-permute-start.14 = (bf16[128,512]{1,0:T(8,128)(2,1)S(1)}, bf16[128,512]{1,0:T(8,128)(2,1)S(1)}, u32[]{:S(2)}, u32[]{:S(2)}) collective-permute-start(bf16[128,512]{1,0:T(8,128)(2,1)S(1)} %collective-permute-done.13.refs_12_), channel_id=1, source_target_pairs={{0,14},{2,0},{4,2},{6,4},{8,6},{10,8},{12,10},{14,12},{1,15},{3,1}... | collective-permute-start | bytes 393224 | tf_op jit(solution)/shard_map/ppermute | solution.py:33
  27.6 6.3 %collective-permute-start.6 = (bf16[128,512]{1,0:T(8,128)(2,1)S(1)}, bf16[128,512]{1,0:T(8,128)(2,1)S(1)}, u32[]{:S(2)}, u32[]{:S(2)}) collective-permute-start(bf16[128,512]{1,0:T(8,128)(2,1)S(1)} %collective-permute-done.4.refs_5_), channel_id=1, source_target_pairs={{0,2},{2,4},{4,6},{6,8},{8,10},{10,12},{12,14},{14,0},{1,3},{3,5},... | collective-permute-start | bytes 393224 | tf_op jit(solution)/shard_map/ppermute | solution.py:33
  28.6 6.2 %collective-permute-start.7 = (bf16[128,512]{1,0:T(8,128)(2,1)S(1)}, bf16[128,512]{1,0:T(8,128)(2,1)S(1)}, u32[]{:S(2)}, u32[]{:S(2)}) collective-permute-start(bf16[128,512]{1,0:T(8,128)(2,1)S(1)} %collective-permute-done.5.refs_6_), channel_id=1, source_target_pairs={{0,2},{2,4},{4,6},{6,8},{8,10},{10,12},{12,14},{14,0},{1,3},{3,5},... | collective-permute-start | bytes 393224 | tf_op jit(solution)/shard_map/ppermute | solution.py:33
  28.7 6.1 %collective-permute-start.11 = (bf16[128,512]{1,0:T(8,128)(2,1)S(1)}, bf16[128,512]{1,0:T(8,128)(2,1)S(1)}, u32[]{:S(2)}, u32[]{:S(2)}) collective-permute-start(bf16[128,512]{1,0:T(8,128)(2,1)S(1)} %collective-permute-done.10.refs_11_), channel_id=1, source_target_pairs={{0,14},{2,0},{4,2},{6,4},{8,6},{10,8},{12,10},{14,12},{1,15},{3,1}... | collective-permute-start | bytes 393224 | tf_op jit(solution)/shard_map/ppermute | solution.py:33
  48.4 30.3 %collective-permute-start.26 = (bf16[128,512]{1,0:T(8,128)(2,1)}, bf16[128,512]{1,0:T(8,128)(2,1)S(1)}, u32[]{:S(2)}, u32[]{:S(2)}) collective-permute-start(bf16[128,512]{1,0:T(8,128)(2,1)} %get-tuple-element.44), channel_id=1, source_target_pairs={{0,2},{2,4},{4,6},{6,8},{8,10},{10,12},{12,14},{14,0},{1,3},{3,5},... | collective-permute-start | bytes 393224 | tf_op jit(solution)/shard_map/ppermute | solution.py:33
  51.0 27.8 %collective-permute-start.23 = (bf16[128,512]{1,0:T(8,128)(2,1)}, bf16[128,512]{1,0:T(8,128)(2,1)S(1)}, u32[]{:S(2)}, u32[]{:S(2)}) collective-permute-start(bf16[128,512]{1,0:T(8,128)(2,1)} %get-tuple-element.41), channel_id=1, source_target_pairs={{0,14},{2,0},{4,2},{6,4},{8,6},{10,8},{12,10},{14,12},{1,15},{3,1}... | collective-permute-start | bytes 393224 | tf_op jit(solution)/shard_map/ppermute | solution.py:33
  63.9 17.7 %collective-permute-start.20 = (bf16[128,512]{1,0:T(8,128)(2,1)}, bf16[128,512]{1,0:T(8,128)(2,1)S(1)}, u32[]{:S(2)}, u32[]{:S(2)}) collective-permute-start(bf16[128,512]{1,0:T(8,128)(2,1)} %get-tuple-element.38), channel_id=1, source_target_pairs={{0,2},{2,4},{4,6},{6,8},{8,10},{10,12},{12,14},{14,0},{1,3},{3,5},... | collective-permute-start | bytes 393224 | tf_op jit(solution)/shard_map/ppermute | solution.py:33
  63.9 17.8 %collective-permute-start.16 = (bf16[128,512]{1,0:T(8,128)(2,1)}, bf16[128,512]{1,0:T(8,128)(2,1)S(1)}, u32[]{:S(2)}, u32[]{:S(2)}) collective-permute-start(bf16[128,512]{1,0:T(8,128)(2,1)} %get-tuple-element.34), channel_id=1, source_target_pairs={{0,14},{2,0},{4,2},{6,4},{8,6},{10,8},{12,10},{14,12},{1,15},{3,1}... | collective-permute-start | bytes 393224 | tf_op jit(solution)/shard_map/ppermute | solution.py:33
  66.6 15.0 %copy-start.13 = (bf16[128,512]{1,0:T(8,128)(2,1)S(1)}, bf16[128,512]{1,0:T(8,128)(2,1)}, u32[]{:S(2)}) copy-start(bf16[128,512]{1,0:T(8,128)(2,1)} %get-tuple-element.39) | copy-start | bytes 393220
  66.6 15.1 %copy-start.12 = (bf16[128,512]{1,0:T(8,128)(2,1)S(1)}, bf16[128,512]{1,0:T(8,128)(2,1)}, u32[]{:S(2)}) copy-start(bf16[128,512]{1,0:T(8,128)(2,1)} %get-tuple-element.35) | copy-start | bytes 393220
  66.6 18.3 %copy-start.11 = (bf16[128,512]{1,0:T(8,128)(2,1)S(1)}, bf16[128,512]{1,0:T(8,128)(2,1)}, u32[]{:S(2)}) copy-start(bf16[128,512]{1,0:T(8,128)(2,1)} %get-tuple-element.46) | copy-start | bytes 393220
  66.6 18.4 %copy-start.10 = (bf16[128,512]{1,0:T(8,128)(2,1)S(1)}, bf16[128,512]{1,0:T(8,128)(2,1)}, u32[]{:S(2)}) copy-start(bf16[128,512]{1,0:T(8,128)(2,1)} %get-tuple-element.43) | copy-start | bytes 393220
  66.6 42.0 %all-to-all-start = ((bf16[32,16,2048]{2,1,0:T(8,128)(2,1)}), bf16[32,16,2048]{2,1,0:T(8,128)(2,1)S(1)}, u32[]{:S(2)}, u32[]{:S(2)}) async-start(bf16[32,16,2048]{2,1,0:T(8,128)(2,1)} %bitcast.20), calls=%async_computation | async-start | bytes 4194304 | tf_op jit(solution)/shard_map/all_to_all | solution.py:408
  78.6 14.3 %copy-start.6 = (bf16[128,512]{1,0:T(8,128)(2,1)S(1)}, bf16[128,512]{1,0:T(8,128)(2,1)}, u32[]{:S(2)}) copy-start(bf16[128,512]{1,0:T(8,128)(2,1)} %get-tuple-element.37) | copy-start | bytes 393220
  78.6 19.8 %copy-start.1 = (bf16[128,4224]{1,0:T(8,128)(2,1)S(1)}, bf16[128,4224]{1,0:T(8,128)(2,1)}, u32[]{:S(2)}) copy-start(bf16[128,4224]{1,0:T(8,128)(2,1)} %copy-done) | copy-start | bytes 3244036
  78.6 19.8 %copy-start.2 = (f32[128,512]{1,0:T(8,128)S(1)}, f32[128,512]{1,0:T(8,128)}, u32[]{:S(2)}) copy-start(f32[128,512]{1,0:T(8,128)} %get-tuple-element.32.own_a) | copy-start | bytes 786436
  78.6 19.8 %copy-start.3 = (f32[128,512]{1,0:T(8,128)S(1)}, f32[128,512]{1,0:T(8,128)}, u32[]{:S(2)}) copy-start(f32[128,512]{1,0:T(8,128)} %get-tuple-element.33.own_b) | copy-start | bytes 786436
  78.6 19.7 %copy-start.4 = (bf16[128,128]{1,0:T(8,128)(2,1)S(1)}, bf16[128,128]{1,0:T(8,128)(2,1)}, u32[]{:S(2)}) copy-start(bf16[128,128]{1,0:T(8,128)(2,1)} %get-tuple-element.31.refs_20_.extra_own) | copy-start | bytes 98308
  78.6 19.7 %copy-start.5 = (s32[2]{0:T(128)S(1)}, s32[2]{0:T(128)}, u32[]{:S(2)}) copy-start(s32[2]{0:T(128)} %pad_add_fusion.where_ref) | copy-start | bytes 28
  78.7 6.2 %collective-permute-start.27 = (bf16[128,512]{1,0:T(8,128)(2,1)S(1)}, bf16[128,512]{1,0:T(8,128)(2,1)S(1)}, u32[]{:S(2)}, u32[]{:S(2)}) collective-permute-start(bf16[128,512]{1,0:T(8,128)(2,1)S(1)} %add_convert_fusion.2), channel_id=1, source_target_pairs={{0,2},{2,4},{4,6},{6,8},{8,10},{10,12},{12,14},{14,0},{1,3},{3,5},... | collective-permute-start | bytes 393224 | tf_op jit(solution)/shard_map/ppermute | solution.py:33
  78.9 6.1 %collective-permute-start.24 = (bf16[128,512]{1,0:T(8,128)(2,1)S(1)}, bf16[128,512]{1,0:T(8,128)(2,1)S(1)}, u32[]{:S(2)}, u32[]{:S(2)}) collective-permute-start(bf16[128,512]{1,0:T(8,128)(2,1)S(1)} %add_convert_fusion.4), channel_id=1, source_target_pairs={{0,14},{2,0},{4,2},{6,4},{8,6},{10,8},{12,10},{14,12},{1,15},{3,1}... | collective-permute-start | bytes 393224 | tf_op jit(solution)/shard_map/ppermute | solution.py:33
  81.6 6.2 %collective-permute-start.21 = (bf16[128,512]{1,0:T(8,128)(2,1)S(1)}, bf16[128,512]{1,0:T(8,128)(2,1)S(1)}, u32[]{:S(2)}, u32[]{:S(2)}) collective-permute-start(bf16[128,512]{1,0:T(8,128)(2,1)S(1)} %add_convert_fusion.6), channel_id=1, source_target_pairs={{0,2},{2,4},{4,6},{6,8},{8,10},{10,12},{12,14},{14,0},{1,3},{3,5},... | collective-permute-start | bytes 393224 | tf_op jit(solution)/shard_map/ppermute | solution.py:33
  81.8 6.1 %collective-permute-start.17 = (bf16[128,512]{1,0:T(8,128)(2,1)S(1)}, bf16[128,512]{1,0:T(8,128)(2,1)S(1)}, u32[]{:S(2)}, u32[]{:S(2)}) collective-permute-start(bf16[128,512]{1,0:T(8,128)(2,1)S(1)} %add_convert_fusion.9), channel_id=1, source_target_pairs={{0,14},{2,0},{4,2},{6,4},{8,6},{10,8},{12,10},{14,12},{1,15},{3,1}... | collective-permute-start | bytes 393224 | tf_op jit(solution)/shard_map/ppermute | solution.py:33
  84.9 5.8 %collective-permute-start.28 = (bf16[128,512]{1,0:T(8,128)(2,1)S(1)}, bf16[128,512]{1,0:T(8,128)(2,1)S(1)}, u32[]{:S(2)}, u32[]{:S(2)}) collective-permute-start(bf16[128,512]{1,0:T(8,128)(2,1)S(1)} %add_convert_fusion.1), channel_id=1, source_target_pairs={{0,2},{2,4},{4,6},{6,8},{8,10},{10,12},{12,14},{14,0},{1,3},{3,5},... | collective-permute-start | bytes 393224 | tf_op jit(solution)/shard_map/ppermute | solution.py:33
  85.1 11.4 %collective-permute-start.25 = (bf16[128,512]{1,0:T(8,128)(2,1)S(1)}, bf16[128,512]{1,0:T(8,128)(2,1)S(1)}, u32[]{:S(2)}, u32[]{:S(2)}) collective-permute-start(bf16[128,512]{1,0:T(8,128)(2,1)S(1)} %add_convert_fusion.3), channel_id=1, source_target_pairs={{0,14},{2,0},{4,2},{6,4},{8,6},{10,8},{12,10},{14,12},{1,15},{3,1}... | collective-permute-start | bytes 393224 | tf_op jit(solution)/shard_map/ppermute | solution.py:33
  87.8 8.6 %collective-permute-start.22 = (bf16[128,512]{1,0:T(8,128)(2,1)S(1)}, bf16[128,512]{1,0:T(8,128)(2,1)S(1)}, u32[]{:S(2)}, u32[]{:S(2)}) collective-permute-start(bf16[128,512]{1,0:T(8,128)(2,1)S(1)} %add_convert_fusion.5), channel_id=1, source_target_pairs={{0,2},{2,4},{4,6},{6,8},{8,10},{10,12},{12,14},{14,0},{1,3},{3,5},... | collective-permute-start | bytes 393224 | tf_op jit(solution)/shard_map/ppermute | solution.py:33
  88.0 4.9 %collective-permute-start.18 = (bf16[128,512]{1,0:T(8,128)(2,1)S(1)}, bf16[128,512]{1,0:T(8,128)(2,1)S(1)}, u32[]{:S(2)}, u32[]{:S(2)}) collective-permute-start(bf16[128,512]{1,0:T(8,128)(2,1)S(1)} %add_convert_fusion.8), channel_id=1, source_target_pairs={{0,14},{2,0},{4,2},{6,4},{8,6},{10,8},{12,10},{14,12},{1,15},{3,1}... | collective-permute-start | bytes 393224 | tf_op jit(solution)/shard_map/ppermute | solution.py:33
  90.8 6.0 %collective-permute-start.29 = (bf16[128,512]{1,0:T(8,128)(2,1)S(1)}, bf16[128,512]{1,0:T(8,128)(2,1)S(1)}, u32[]{:S(2)}, u32[]{:S(2)}) collective-permute-start(bf16[128,512]{1,0:T(8,128)(2,1)S(1)} %add_convert_fusion), channel_id=1, source_target_pairs={{0,2},{2,4},{4,6},{6,8},{8,10},{10,12},{12,14},{14,0},{1,3},{3,5},... | collective-permute-start | bytes 393224 | tf_op jit(solution)/shard_map/ppermute | solution.py:33
  92.9 5.4 %collective-permute-start.19 = (bf16[128,512]{1,0:T(8,128)(2,1)S(1)}, bf16[128,512]{1,0:T(8,128)(2,1)S(1)}, u32[]{:S(2)}, u32[]{:S(2)}) collective-permute-start(bf16[128,512]{1,0:T(8,128)(2,1)S(1)} %add_convert_fusion.7), channel_id=1, source_target_pairs={{0,14},{2,0},{4,2},{6,4},{8,6},{10,8},{12,10},{14,12},{1,15},{3,1}... | collective-permute-start | bytes 393224 | tf_op jit(solution)/shard_map/ppermute | solution.py:33
  (17 other events, 126.1 us)

commit v5 on v4

--- a/solution.py
+++ b/solution.py
@@ -21,7 +21,7 @@
 WIDTH = HEADS * ROWS
 CHUNK = HALF_Q
 SLOTS = N_DP * 2 * CAP
-LAY_OUT = 4
+LAY_OUT = 2
 NEG = -1e30
 F32 = jnp.float32
 BF16 = jnp.bfloat16
@@ -191,6 +191,7 @@
 def attention_grads(where, ends, tiers, keys, q_all, qg_par, g_all, extra_own):
     block = pl.BlockSpec((ROWS, 2 * HALF_KV), lambda c, where, ends, tiers: (0, 0))
     extra = pl.BlockSpec((ROWS, HD), lambda c, where, ends, tiers: (0, 0))
+    whole = pl.BlockSpec(memory_space=pltpu.VMEM)
     extra_par = pl.BlockSpec((ROWS, HD), lambda c, where, ends, tiers: (0, 2 * HALF_Q // HD))
 
     def at(column):
@@ -208,8 +209,8 @@
         grid_spec=pltpu.PrefetchScalarGridSpec(
             num_scalar_prefetch=3,
             grid=(2,),
-            in_specs=[block] * 16 + [own, at(0), own, at(1), extra, extra_par],
-            out_specs=[pl.BlockSpec((N_DP, 1, CAP, CHUNK), out_at)] + [block] * 16,
+            in_specs=[whole] * 16 + [own, at(0), own, at(1), extra, extra_par],
+            out_specs=[pl.BlockSpec((N_DP, 1, CAP, CHUNK), out_at)] + [whole] * 16,
             scratch_shapes=[
                 pltpu.VMEM((NZ * BLK, 2 * HALF_KV), BF16),
                 pltpu.VMEM((2, HD, NZ * BLK), BF16),
@@ -295,8 +296,9 @@
     y = where_ref[0]
     lane = lax.broadcasted_iota(jnp.int32, (ROWS, HD), 1)
     row = lax.broadcasted_iota(jnp.int32, (ROWS, HD), 0)
-    owners = jnp.broadcast_to(owners_ref[...].astype(F32), (ROWS, HD))
-    earlier = (owners == owners.T) & (lane < row)
+    others = jnp.broadcast_to(owners_ref[...].astype(F32), (ROWS, HD))
+    owners = others.T
+    earlier = (owners == others) & (lane < row)
     slots = jnp.sum(jnp.where(earlier, 1.0, 0.0), axis=1, keepdims=True)
     head = lax.broadcasted_iota(jnp.int32, (HALF_Q, HD), 0) // HD
     pick = jnp.where(head == lax.broadcasted_iota(jnp.int32, (HALF_Q, HD), 1), 1.0, 0.0).astype(BF16)
@@ -336,7 +338,7 @@
                 pl.BlockSpec((ROWS, HALF_Q), lambda n, where: (0, 1 - where[0])),
                 whole((ROWS, 2 * HALF_Q)),
                 whole((ROWS, 2 * HALF_Q)),
-                whole((ROWS, 1)),
+                whole((1, ROWS)),
             ],
             out_specs=[whole((ROWS, width)), whole((ROWS, HD))],
         ),
@@ -363,7 +365,7 @@
     b = key_values(1 - y)
     keys_a = {0: a, 1: zshift(a, 1), 7: zshift(a, -1)}
     keys_b = {0: yswap(b)}
-    send, extra_own = prepare(y, q_all, g_all, forward_out[0], row_owners[0])
+    send, extra_own = prepare(y, q_all, g_all, forward_out[0], row_owners[0].reshape(1, ROWS))
     send, keys_b[0] = lax.optimization_barrier((send, keys_b[0]))
     qg_par = yswap(send)
     for hop in range(1, 4):

time: 126 us -> 126 us (level); the launches traced: 126 us -> 125 us
  starting transfers between devices: 68.3 us -> 64.4 us
  waiting for transfers between devices: 16.8 us -> 19 us
  Pallas kernels: 19.2 us -> 20.7 us
  local copies, waits for them, and re-layouts: 4.07 us -> 2.69 us
    ppermute x28, starting transfers between devices: 54 us -> 49.1 us  [zshift(): return lax.ppermute(x, 'z', [(i, (i + by) % NZ) for i in range(NZ)])]
    ppermute x28, waiting for transfers between devices: 7.59 us -> 10.8 us  [zshift(): return lax.ppermute(x, 'z', [(i, (i + by) % NZ) for i in range(NZ)])]
    squeeze x1 -> x0, local copies, waits for them, and re-layouts: 1.38 us -> none  [per_device(): send, extra_own = prepare(y, q_all, g_all, forward_out[0], row_owners[0])]
  transfers between devices with their start and end apart: 31 -> 31, of which waited for: 10 -> 11; matrix products, arithmetic and copies ran while one was open for 3% -> 2% of each run, Pallas kernels for 4% -> 4%
where the time goes in v5:
time: 126 us; the launch traced here: 125 us
  starting transfers between devices  64.4 us (51%)
  Pallas kernels  20.7 us (16%)
  waiting for transfers between devices  19 us (15%)
  blocking collectives  15.7 us (12%)
  local copies, waits for them, and re-layouts  2.69 us (2%)
  other arithmetic  1.73 us (1%)
    ppermute x28, starting transfers between devices, zshift(): return lax.ppermute(x, 'z', [(i, (i + by) % NZ) for i in range(NZ)])  49.1 us
    all_to_all x1, blocking collectives, to_owners(): lax.all_to_all(rows.reshape(2 * N_DP, CAP, -1), ('dp', 'yl'), split_axis=...  15.7 us
    pallas_call x1, Pallas kernels, attention_grads(): pl.pallas_call(grads_kernel, grid_spec=pltpu.PrefetchScalarGridSpec(num_s...  13 us
    all_to_all x1, starting transfers between devices, to_owners(): lax.all_to_all(rows.reshape(2 * N_DP, CAP, -1), ('dp', 'yl'), split_axis=...  12.6 us
    ppermute x28, waiting for transfers between devices, zshift(): return lax.ppermute(x, 'z', [(i, (i + by) % NZ) for i in range(NZ)])  10.8 us
    all_to_all x1, waiting for transfers between devices, to_owners(): lax.all_to_all(rows.reshape(2 * N_DP, CAP, -1), ('dp', 'yl'), split_axis=...  8.14 us
    pallas_call x1, Pallas kernels, prepare(): pl.pallas_call(prepare_kernel, grid_spec=pltpu.PrefetchScalarGridSpec(num...  3.73 us
    pallas_call x1, Pallas kernels, lay_out(): pl.pallas_call(lay_out_kernel, grid=(N_DP // LAY_OUT,), in_specs=[whole,...  3.09 us
  transfers between devices with their start and end apart: 31, of which 11 were waited for; matrix products, arithmetic and copies ran while one was open for 2% of the time, Pallas kernels for 4%

profile of v5, /device:TPU:1, one launch (start us, length us, event | category | flops | bytes accessed | tf_op | source)
XLA Modules:
  0.0 124.7 jit_solution(5233115381266330091)
XLA Ops:
  0.0 1.0 dynamic-slice_bitcast_fusion
  1.0 2.2 %collective-permute-start = (bf16[128,512]{1,0:T(8,128)(2,1)S(1)}, bf16[128,512]{1,0:T(8,128)(2,1)S(1)}, u32[]{:S(2)}, u32[]{:S(2)}) collective-permute-start(bf16[128,512]{1,0:T(8,128)(2,1)S(1)} %pad_maximum_fusion.1), channel_id=1, source_target_pairs={{0,1},{1,0},{2,3},{3,2},{4,5},{5,4},{6,7},{7,6},{8,9},{9,8},{10,11... | collective-permute-start | bytes 393224 | tf_op jit(solution)/shard_map/ppermute | solution.py:37
  3.2 3.7 %prepare.1 = (bf16[128,4224]{1,0:T(8,128)(2,1)}, bf16[128,128]{1,0:T(8,128)(2,1)}) custom-call(s32[1]{0:T(128)} %bitcast.1.where_ref, bf16[128,4096]{1,0:T(8,128)(2,1)} %bitcast.22, bf16[128,4096]{1,0:T(8,128)(2,1)} %bitcast.24, bf16[128,4096]{1,0:T(8,128)(2,1)} %bitcast.21, s32[1,128]{1,0:T(1,128)} %bitcast.26), custom_call_target="tpu_custom_call" | custom-call | tf_op jit(solution)/shard_map/prepare/pallas_call | solution.py:332
  7.0 0.4 collective-permute-start.15
  7.4 1.9 %collective-permute-start.1 = (bf16[128,512]{1,0:T(8,128)(2,1)S(1)}, bf16[128,512]{1,0:T(8,128)(2,1)S(1)}, u32[]{:S(2)}, u32[]{:S(2)}) collective-permute-start(bf16[128,512]{1,0:T(8,128)(2,1)S(1)} %pad_maximum_fusion.refs_0_), channel_id=1, source_target_pairs={{0,2},{2,4},{4,6},{6,8},{8,10},{10,12},{12,14},{14,0},{1,3},{3,5},... | collective-permute-start | bytes 393224 | tf_op jit(solution)/shard_map/ppermute | solution.py:33
  9.3 4.0 %collective-permute-start.8 = (bf16[128,512]{1,0:T(8,128)(2,1)S(1)}, bf16[128,512]{1,0:T(8,128)(2,1)S(1)}, u32[]{:S(2)}, u32[]{:S(2)}) collective-permute-start(bf16[128,512]{1,0:T(8,128)(2,1)S(1)} %collective-permute-done.refs_1_), channel_id=1, source_target_pairs={{0,14},{2,0},{4,2},{6,4},{8,6},{10,8},{12,10},{14,12},{1,15},{3,1}... | collective-permute-start | bytes 393224 | tf_op jit(solution)/shard_map/ppermute | solution.py:33
  13.4 1.4 %collective-permute-start.12 = (bf16[128,512]{1,0:T(8,128)(2,1)S(1)}, bf16[128,512]{1,0:T(8,128)(2,1)S(1)}, u32[]{:S(2)}, u32[]{:S(2)}) collective-permute-start(bf16[128,512]{1,0:T(8,128)(2,1)S(1)} %pad_maximum_fusion.refs_0_), channel_id=1, source_target_pairs={{0,14},{2,0},{4,2},{6,4},{8,6},{10,8},{12,10},{14,12},{1,15},{3,1}... | collective-permute-start | bytes 393224 | tf_op jit(solution)/shard_map/ppermute | solution.py:33
  14.7 0.1 collective-permute-start.2
  14.8 0.8 collective-permute-done.1.refs_2_
  15.6 2.7 %collective-permute-start.9 = (bf16[128,512]{1,0:T(8,128)(2,1)S(1)}, bf16[128,512]{1,0:T(8,128)(2,1)S(1)}, u32[]{:S(2)}, u32[]{:S(2)}) collective-permute-start(bf16[128,512]{1,0:T(8,128)(2,1)S(1)} %collective-permute-done.8.refs_15_), channel_id=1, source_target_pairs={{0,14},{2,0},{4,2},{6,4},{8,6},{10,8},{12,10},{14,12},{1,15},{3,1}... | collective-permute-start | bytes 393224 | tf_op jit(solution)/shard_map/ppermute | solution.py:33
  18.4 2.1 %collective-permute-start.13 = (bf16[128,512]{1,0:T(8,128)(2,1)S(1)}, bf16[128,512]{1,0:T(8,128)(2,1)S(1)}, u32[]{:S(2)}, u32[]{:S(2)}) collective-permute-start(bf16[128,512]{1,0:T(8,128)(2,1)S(1)} %collective-permute-done.12.refs_14_), channel_id=1, source_target_pairs={{0,14},{2,0},{4,2},{6,4},{8,6},{10,8},{12,10},{14,12},{1,15},{3,1}... | collective-permute-start | bytes 393224 | tf_op jit(solution)/shard_map/ppermute | solution.py:33
  20.5 0.6 collective-permute-done.3.refs_4_
  21.2 2.8 %collective-permute-start.10 = (bf16[128,512]{1,0:T(8,128)(2,1)S(1)}, bf16[128,512]{1,0:T(8,128)(2,1)S(1)}, u32[]{:S(2)}, u32[]{:S(2)}) collective-permute-start(bf16[128,512]{1,0:T(8,128)(2,1)S(1)} %collective-permute-done.9.refs_13_), channel_id=1, source_target_pairs={{0,14},{2,0},{4,2},{6,4},{8,6},{10,8},{12,10},{14,12},{1,15},{3,1}... | collective-permute-start | bytes 393224 | tf_op jit(solution)/shard_map/ppermute | solution.py:33
  24.0 1.6 %collective-permute-start.14 = (bf16[128,512]{1,0:T(8,128)(2,1)S(1)}, bf16[128,512]{1,0:T(8,128)(2,1)S(1)}, u32[]{:S(2)}, u32[]{:S(2)}) collective-permute-start(bf16[128,512]{1,0:T(8,128)(2,1)S(1)} %collective-permute-done.13.refs_12_), channel_id=1, source_target_pairs={{0,14},{2,0},{4,2},{6,4},{8,6},{10,8},{12,10},{14,12},{1,15},{3,1}... | collective-permute-start | bytes 393224 | tf_op jit(solution)/shard_map/ppermute | solution.py:33
  25.6 0.1 collective-permute-done.4.refs_5_
  25.7 1.4 %collective-permute-done.5.refs_6_ = bf16[128,512]{1,0:T(8,128)(2,1)S(1)} collective-permute-done((bf16[128,512]{1,0:T(8,128)(2,1)S(1)}, bf16[128,512]{1,0:T(8,128)(2,1)S(1)}, u32[]{:S(2)}, u32[]{:S(2)}) %collective-permute-start.5) | collective-permute-done | bytes 131104 | tf_op jit(solution)/shard_map/ppermute | solution.py:33
  27.1 3.3 %collective-permute-start.11 = (bf16[128,512]{1,0:T(8,128)(2,1)S(1)}, bf16[128,512]{1,0:T(8,128)(2,1)S(1)}, u32[]{:S(2)}, u32[]{:S(2)}) collective-permute-start(bf16[128,512]{1,0:T(8,128)(2,1)S(1)} %collective-permute-done.10.refs_11_), channel_id=1, source_target_pairs={{0,14},{2,0},{4,2},{6,4},{8,6},{10,8},{12,10},{14,12},{1,15},{3,1}... | collective-permute-start | bytes 393224 | tf_op jit(solution)/shard_map/ppermute | solution.py:33
  30.5 0.7 reshape_squeeze.6.tiers_ref
  31.1 0.7 reduce-window.9
  31.8 0.7 pad_add_fusion.where_ref
  32.5 1.4 %collective-permute-done.7.refs_8_ = bf16[128,512]{1,0:T(8,128)(2,1)S(1)} collective-permute-done((bf16[128,512]{1,0:T(8,128)(2,1)S(1)}, bf16[128,512]{1,0:T(8,128)(2,1)S(1)}, u32[]{:S(2)}, u32[]{:S(2)}) %collective-permute-start.7) | collective-permute-done | bytes 131104 | tf_op jit(solution)/shard_map/ppermute | solution.py:33
  34.1 0.5 copy-done.31
  34.6 0.0 copy-done.32
  34.6 0.4 copy-done
  35.0 13.0 %grads.1 = (bf16[16,2,16,2048]{3,2,1,0:T(8,128)(2,1)}, f32[128,512]{1,0:T(8,128)}, f32[128,512]{1,0:T(8,128)}, bf16[128,512]{1,0:T(8,128)(2,1)}, bf16[128,512]{1...) custom-call(s32[2]{0:T(128)} %pad_add_fusion.where_ref, ...), custom_call_target="tpu_custom_call" | custom-call | flops 8000000000 | bytes 10485760 | tf_op jit(solution)/shard_map/grads/pallas_call | solution.py:207
  48.0 2.4 %collective-permute-start.26 = (bf16[128,512]{1,0:T(8,128)(2,1)}, bf16[128,512]{1,0:T(8,128)(2,1)S(1)}, u32[]{:S(2)}, u32[]{:S(2)}) collective-permute-start(bf16[128,512]{1,0:T(8,128)(2,1)} %get-tuple-element.44), channel_id=1, source_target_pairs={{0,2},{2,4},{4,6},{6,8},{8,10},{10,12},{12,14},{14,0},{1,3},{3,5},... | collective-permute-start | bytes 393224 | tf_op jit(solution)/shard_map/ppermute | solution.py:33
  50.4 0.6 collective-permute-start.23
  51.0 12.3 %collective-permute-start.20 = (bf16[128,512]{1,0:T(8,128)(2,1)}, bf16[128,512]{1,0:T(8,128)(2,1)S(1)}, u32[]{:S(2)}, u32[]{:S(2)}) collective-permute-start(bf16[128,512]{1,0:T(8,128)(2,1)} %get-tuple-element.38), channel_id=1, source_target_pairs={{0,2},{2,4},{4,6},{6,8},{8,10},{10,12},{12,14},{14,0},{1,3},{3,5},... | collective-permute-start | bytes 393224 | tf_op jit(solution)/shard_map/ppermute | solution.py:33
  63.3 12.6 %all-to-all-start = ((bf16[32,16,2048]{2,1,0:T(8,128)(2,1)}), bf16[32,16,2048]{2,1,0:T(8,128)(2,1)S(1)}, u32[]{:S(2)}, u32[]{:S(2)}) async-start(bf16[32,16,2048]{2,1,0:T(8,128)(2,1)} %bitcast.20), calls=%async_computation | async-start | bytes 4194304 | tf_op jit(solution)/shard_map/all_to_all | solution.py:410
  76.0 3.0 %collective-permute-start.27 = (bf16[128,512]{1,0:T(8,128)(2,1)S(1)}, bf16[128,512]{1,0:T(8,128)(2,1)S(1)}, u32[]{:S(2)}, u32[]{:S(2)}) collective-permute-start(bf16[128,512]{1,0:T(8,128)(2,1)S(1)} %add_convert_fusion.2), channel_id=1, source_target_pairs={{0,2},{2,4},{4,6},{6,8},{8,10},{10,12},{12,14},{14,0},{1,3},{3,5},... | collective-permute-start | bytes 393224 | tf_op jit(solution)/shard_map/ppermute | solution.py:33
  79.1 0.1 collective-permute-start.24
  79.2 1.8 %collective-permute-start.21 = (bf16[128,512]{1,0:T(8,128)(2,1)S(1)}, bf16[128,512]{1,0:T(8,128)(2,1)S(1)}, u32[]{:S(2)}, u32[]{:S(2)}) collective-permute-start(bf16[128,512]{1,0:T(8,128)(2,1)S(1)} %add_convert_fusion.6), channel_id=1, source_target_pairs={{0,2},{2,4},{4,6},{6,8},{8,10},{10,12},{12,14},{14,0},{1,3},{3,5},... | collective-permute-start | bytes 393224 | tf_op jit(solution)/shard_map/ppermute | solution.py:33
  81.1 1.0 collective-permute-start.17
  82.2 1.8 %collective-permute-start.28 = (bf16[128,512]{1,0:T(8,128)(2,1)S(1)}, bf16[128,512]{1,0:T(8,128)(2,1)S(1)}, u32[]{:S(2)}, u32[]{:S(2)}) collective-permute-start(bf16[128,512]{1,0:T(8,128)(2,1)S(1)} %add_convert_fusion.1), channel_id=1, source_target_pairs={{0,2},{2,4},{4,6},{6,8},{8,10},{10,12},{12,14},{14,0},{1,3},{3,5},... | collective-permute-start | bytes 393224 | tf_op jit(solution)/shard_map/ppermute | solution.py:33
  84.0 0.3 collective-permute-done.24
  84.3 1.0 collective-permute-start.25
  85.4 1.4 %collective-permute-start.22 = (bf16[128,512]{1,0:T(8,128)(2,1)S(1)}, bf16[128,512]{1,0:T(8,128)(2,1)S(1)}, u32[]{:S(2)}, u32[]{:S(2)}) collective-permute-start(bf16[128,512]{1,0:T(8,128)(2,1)S(1)} %add_convert_fusion.5), channel_id=1, source_target_pairs={{0,2},{2,4},{4,6},{6,8},{8,10},{10,12},{12,14},{14,0},{1,3},{3,5},... | collective-permute-start | bytes 393224 | tf_op jit(solution)/shard_map/ppermute | solution.py:33
  86.8 0.3 collective-permute-done.17
  87.2 1.1 collective-permute-start.18
  88.3 0.8 collective-permute-start.29
  89.1 3.0 %collective-permute-done.18 = bf16[128,512]{1,0:T(8,128)(2,1)S(1)} collective-permute-done((bf16[128,512]{1,0:T(8,128)(2,1)S(1)}, bf16[128,512]{1,0:T(8,128)(2,1)S(1)}, u32[]{:S(2)}, u32[]{:S(2)}) %collective-permute-start.18) | collective-permute-done | bytes 131104 | tf_op jit(solution)/shard_map/ppermute | solution.py:33
  92.1 1.7 %collective-permute-start.19 = (bf16[128,512]{1,0:T(8,128)(2,1)S(1)}, bf16[128,512]{1,0:T(8,128)(2,1)S(1)}, u32[]{:S(2)}, u32[]{:S(2)}) collective-permute-start(bf16[128,512]{1,0:T(8,128)(2,1)S(1)} %add_convert_fusion.7), channel_id=1, source_target_pairs={{0,14},{2,0},{4,2},{6,4},{8,6},{10,8},{12,10},{14,12},{1,15},{3,1}... | collective-permute-start | bytes 393224 | tf_op jit(solution)/shard_map/ppermute | solution.py:33
  93.9 0.3 collective-permute-done.29.up_b
  94.2 2.6 %collective-permute-done.19.down_a = bf16[128,512]{1,0:T(8,128)(2,1)S(1)} collective-permute-done((bf16[128,512]{1,0:T(8,128)(2,1)S(1)}, bf16[128,512]{1,0:T(8,128)(2,1)S(1)}, u32[]{:S(2)}, u32[]{:S(2)}) %collective-permute-start.19) | collective-permute-done | bytes 131104 | tf_op jit(solution)/shard_map/ppermute | solution.py:33
  96.8 0.9 finish.1
  97.7 8.1 %all-to-all-done.q_ref = bf16[32,16,2048]{2,1,0:T(8,128)(2,1)S(1)} async-done(((bf16[32,16,2048]{2,1,0:T(8,128)(2,1)}), bf16[32,16,2048]{2,1,0:T(8,128)(2,1)S(1)}, u32[]{:S(2)}, u32[]{:S(2)}) %all-to-all-start) | async-done | bytes 2097184 | tf_op jit(solution)/shard_map/all_to_all | solution.py:410
  105.9 15.7 %all_to_all.10.kv_ref = bf16[32,16,512]{2,1,0:T(8,128)(2,1)S(1)} all-to-all(bf16[32,16,512]{2,1,0:T(8,128)(2,1)S(1)} %bitcast.19), channel_id=1, replica_groups=mesh['dp'=16,'z'=8,'yl'=2] {'dp','yl'}, dimensions={0} | all-to-all | bytes 1048576 | tf_op jit(solution)/shard_map/all_to_all | solution.py:410
  121.6 3.1 %lay_out.1 = bf16[16,16,5120]{2,1,0:T(8,128)(2,1)} custom-call(bf16[32,16,2048]{2,1,0:T(8,128)(2,1)S(1)} %all-to-all-done.q_ref, bf16[32,16,512]{2,1,0:T(8,128)(2,1)S(1)} %all_to_all.10.kv_ref), custom_call_target="tpu_custom_call" | custom-call | tf_op jit(solution)/shard_map/lay_out/pallas_call | solution.py:280
  (103 shorter events, 0.6 us)
Async XLA Ops:
  0.0 30.5 %copy-start.17 = (s32[1,32,32]{2,1,0:T(8,128)S(1)}, s32[1,32,32]{2,1,0:T(8,128)}, u32[]{:S(2)}) copy-start(s32[1,32,32]{2,1,0:T(8,128)} %param.14) | copy-start | bytes 12292
  0.0 31.1 %copy-start.33 = (s32[1,8]{1,0:T(1,128)S(1)}, s32[1,8]{1,0:T(1,128)}, u32[]{:S(2)}) copy-start(s32[1,8]{1,0:T(1,128)} %param.13) | copy-start | bytes 100
  1.0 5.9 %collective-permute-start = (bf16[128,512]{1,0:T(8,128)(2,1)S(1)}, bf16[128,512]{1,0:T(8,128)(2,1)S(1)}, u32[]{:S(2)}, u32[]{:S(2)}) collective-permute-start(bf16[128,512]{1,0:T(8,128)(2,1)S(1)} %pad_maximum_fusion.1), channel_id=1, source_target_pairs={{0,1},{1,0},{2,3},{3,2},{4,5},{5,4},{6,7},{7,6},{8,9},{9,8},{10,11... | collective-permute-start | bytes 393224 | tf_op jit(solution)/shard_map/ppermute | solution.py:37
  6.9 27.0 %copy-start.18 = (bf16[128,512]{1,0:T(8,128)(2,1)}, bf16[128,512]{1,0:T(8,128)(2,1)S(1)}, u32[]{:S(2)}) copy-start(bf16[128,512]{1,0:T(8,128)(2,1)S(1)} %collective-permute-done.refs_1_) | copy-start | bytes 393220
  7.0 27.0 %collective-permute-start.15 = (bf16[128,4224]{1,0:T(8,128)(2,1)}, bf16[128,4224]{1,0:T(8,128)(2,1)S(1)}, u32[]{:S(2)}, u32[]{:S(2)}) collective-permute-start(bf16[128,4224]{1,0:T(8,128)(2,1)} %get-tuple-element.30), channel_id=1, source_target_pairs={{0,1},{1,0},{2,3},{3,2},{4,5},{5,4},{6,7},{7,6},{8,9},{9,8},{10,11... | collective-permute-start | bytes 3244040 | tf_op jit(solution)/shard_map/ppermute | solution.py:37
  7.4 26.5 %copy-start.16 = (bf16[128,512]{1,0:T(8,128)(2,1)}, bf16[128,512]{1,0:T(8,128)(2,1)S(1)}, u32[]{:S(2)}) copy-start(bf16[128,512]{1,0:T(8,128)(2,1)S(1)} %pad_maximum_fusion.refs_0_) | copy-start | bytes 393220
  7.4 8.2 %collective-permute-start.1 = (bf16[128,512]{1,0:T(8,128)(2,1)S(1)}, bf16[128,512]{1,0:T(8,128)(2,1)S(1)}, u32[]{:S(2)}, u32[]{:S(2)}) collective-permute-start(bf16[128,512]{1,0:T(8,128)(2,1)S(1)} %pad_maximum_fusion.refs_0_), channel_id=1, source_target_pairs={{0,2},{2,4},{4,6},{6,8},{8,10},{10,12},{12,14},{14,0},{1,3},{3,5},... | collective-permute-start | bytes 393224 | tf_op jit(solution)/shard_map/ppermute | solution.py:33
  9.3 6.3 %collective-permute-start.8 = (bf16[128,512]{1,0:T(8,128)(2,1)S(1)}, bf16[128,512]{1,0:T(8,128)(2,1)S(1)}, u32[]{:S(2)}, u32[]{:S(2)}) collective-permute-start(bf16[128,512]{1,0:T(8,128)(2,1)S(1)} %collective-permute-done.refs_1_), channel_id=1, source_target_pairs={{0,14},{2,0},{4,2},{6,4},{8,6},{10,8},{12,10},{14,12},{1,15},{3,1}... | collective-permute-start | bytes 393224 | tf_op jit(solution)/shard_map/ppermute | solution.py:33
  13.4 5.0 %collective-permute-start.12 = (bf16[128,512]{1,0:T(8,128)(2,1)S(1)}, bf16[128,512]{1,0:T(8,128)(2,1)S(1)}, u32[]{:S(2)}, u32[]{:S(2)}) collective-permute-start(bf16[128,512]{1,0:T(8,128)(2,1)S(1)} %pad_maximum_fusion.refs_0_), channel_id=1, source_target_pairs={{0,14},{2,0},{4,2},{6,4},{8,6},{10,8},{12,10},{14,12},{1,15},{3,1}... | collective-permute-start | bytes 393224 | tf_op jit(solution)/shard_map/ppermute | solution.py:33
  14.7 5.8 %collective-permute-start.2 = (bf16[128,512]{1,0:T(8,128)(2,1)S(1)}, bf16[128,512]{1,0:T(8,128)(2,1)S(1)}, u32[]{:S(2)}, u32[]{:S(2)}) collective-permute-start(bf16[128,512]{1,0:T(8,128)(2,1)S(1)} %collective-permute-done.refs_1_), channel_id=1, source_target_pairs={{0,2},{2,4},{4,6},{6,8},{8,10},{10,12},{12,14},{14,0},{1,3},{3,5},... | collective-permute-start | bytes 393224 | tf_op jit(solution)/shard_map/ppermute | solution.py:33
  15.6 18.3 %copy-start.19 = (bf16[128,512]{1,0:T(8,128)(2,1)}, bf16[128,512]{1,0:T(8,128)(2,1)S(1)}, u32[]{:S(2)}) copy-start(bf16[128,512]{1,0:T(8,128)(2,1)S(1)} %collective-permute-done.1.refs_2_) | copy-start | bytes 393220
  15.6 5.5 %collective-permute-start.3 = (bf16[128,512]{1,0:T(8,128)(2,1)S(1)}, bf16[128,512]{1,0:T(8,128)(2,1)S(1)}, u32[]{:S(2)}, u32[]{:S(2)}) collective-permute-start(bf16[128,512]{1,0:T(8,128)(2,1)S(1)} %collective-permute-done.1.refs_2_), channel_id=1, source_target_pairs={{0,2},{2,4},{4,6},{6,8},{8,10},{10,12},{12,14},{14,0},{1,3},{3,5},... | collective-permute-start | bytes 393224 | tf_op jit(solution)/shard_map/ppermute | solution.py:33
  15.6 18.3 %copy-start.20 = (bf16[128,512]{1,0:T(8,128)(2,1)}, bf16[128,512]{1,0:T(8,128)(2,1)S(1)}, u32[]{:S(2)}) copy-start(bf16[128,512]{1,0:T(8,128)(2,1)S(1)} %collective-permute-done.8.refs_15_) | copy-start | bytes 393220
  15.6 5.5 %collective-permute-start.9 = (bf16[128,512]{1,0:T(8,128)(2,1)S(1)}, bf16[128,512]{1,0:T(8,128)(2,1)S(1)}, u32[]{:S(2)}, u32[]{:S(2)}) collective-permute-start(bf16[128,512]{1,0:T(8,128)(2,1)S(1)} %collective-permute-done.8.refs_15_), channel_id=1, source_target_pairs={{0,14},{2,0},{4,2},{6,4},{8,6},{10,8},{12,10},{14,12},{1,15},{3,1}... | collective-permute-start | bytes 393224 | tf_op jit(solution)/shard_map/ppermute | solution.py:33
  18.4 5.6 %collective-permute-start.13 = (bf16[128,512]{1,0:T(8,128)(2,1)S(1)}, bf16[128,512]{1,0:T(8,128)(2,1)S(1)}, u32[]{:S(2)}, u32[]{:S(2)}) collective-permute-start(bf16[128,512]{1,0:T(8,128)(2,1)S(1)} %collective-permute-done.12.refs_14_), channel_id=1, source_target_pairs={{0,14},{2,0},{4,2},{6,4},{8,6},{10,8},{12,10},{14,12},{1,15},{3,1}... | collective-permute-start | bytes 393224 | tf_op jit(solution)/shard_map/ppermute | solution.py:33
  20.5 5.2 %collective-permute-start.4 = (bf16[128,512]{1,0:T(8,128)(2,1)S(1)}, bf16[128,512]{1,0:T(8,128)(2,1)S(1)}, u32[]{:S(2)}, u32[]{:S(2)}) collective-permute-start(bf16[128,512]{1,0:T(8,128)(2,1)S(1)} %collective-permute-done.2.refs_3_), channel_id=1, source_target_pairs={{0,2},{2,4},{4,6},{6,8},{8,10},{10,12},{12,14},{14,0},{1,3},{3,5},... | collective-permute-start | bytes 393224 | tf_op jit(solution)/shard_map/ppermute | solution.py:33
  21.2 5.9 %collective-permute-start.5 = (bf16[128,512]{1,0:T(8,128)(2,1)S(1)}, bf16[128,512]{1,0:T(8,128)(2,1)S(1)}, u32[]{:S(2)}, u32[]{:S(2)}) collective-permute-start(bf16[128,512]{1,0:T(8,128)(2,1)S(1)} %collective-permute-done.3.refs_4_), channel_id=1, source_target_pairs={{0,2},{2,4},{4,6},{6,8},{8,10},{10,12},{12,14},{14,0},{1,3},{3,5},... | collective-permute-start | bytes 393224 | tf_op jit(solution)/shard_map/ppermute | solution.py:33
  21.2 5.9 %collective-permute-start.10 = (bf16[128,512]{1,0:T(8,128)(2,1)S(1)}, bf16[128,512]{1,0:T(8,128)(2,1)S(1)}, u32[]{:S(2)}, u32[]{:S(2)}) collective-permute-start(bf16[128,512]{1,0:T(8,128)(2,1)S(1)} %collective-permute-done.9.refs_13_), channel_id=1, source_target_pairs={{0,14},{2,0},{4,2},{6,4},{8,6},{10,8},{12,10},{14,12},{1,15},{3,1}... | collective-permute-start | bytes 393224 | tf_op jit(solution)/shard_map/ppermute | solution.py:33
  24.0 8.5 %collective-permute-start.14 = (bf16[128,512]{1,0:T(8,128)(2,1)S(1)}, bf16[128,512]{1,0:T(8,128)(2,1)S(1)}, u32[]{:S(2)}, u32[]{:S(2)}) collective-permute-start(bf16[128,512]{1,0:T(8,128)(2,1)S(1)} %collective-permute-done.13.refs_12_), channel_id=1, source_target_pairs={{0,14},{2,0},{4,2},{6,4},{8,6},{10,8},{12,10},{14,12},{1,15},{3,1}... | collective-permute-start | bytes 393224 | tf_op jit(solution)/shard_map/ppermute | solution.py:33
  25.7 6.8 %collective-permute-start.6 = (bf16[128,512]{1,0:T(8,128)(2,1)S(1)}, bf16[128,512]{1,0:T(8,128)(2,1)S(1)}, u32[]{:S(2)}, u32[]{:S(2)}) collective-permute-start(bf16[128,512]{1,0:T(8,128)(2,1)S(1)} %collective-permute-done.4.refs_5_), channel_id=1, source_target_pairs={{0,2},{2,4},{4,6},{6,8},{8,10},{10,12},{12,14},{14,0},{1,3},{3,5},... | collective-permute-start | bytes 393224 | tf_op jit(solution)/shard_map/ppermute | solution.py:33
  27.1 6.8 %collective-permute-start.7 = (bf16[128,512]{1,0:T(8,128)(2,1)S(1)}, bf16[128,512]{1,0:T(8,128)(2,1)S(1)}, u32[]{:S(2)}, u32[]{:S(2)}) collective-permute-start(bf16[128,512]{1,0:T(8,128)(2,1)S(1)} %collective-permute-done.5.refs_6_), channel_id=1, source_target_pairs={{0,2},{2,4},{4,6},{6,8},{8,10},{10,12},{12,14},{14,0},{1,3},{3,5},... | collective-permute-start | bytes 393224 | tf_op jit(solution)/shard_map/ppermute | solution.py:33
  27.1 6.8 %collective-permute-start.11 = (bf16[128,512]{1,0:T(8,128)(2,1)S(1)}, bf16[128,512]{1,0:T(8,128)(2,1)S(1)}, u32[]{:S(2)}, u32[]{:S(2)}) collective-permute-start(bf16[128,512]{1,0:T(8,128)(2,1)S(1)} %collective-permute-done.10.refs_11_), channel_id=1, source_target_pairs={{0,14},{2,0},{4,2},{6,4},{8,6},{10,8},{12,10},{14,12},{1,15},{3,1}... | collective-permute-start | bytes 393224 | tf_op jit(solution)/shard_map/ppermute | solution.py:33
  48.0 28.0 %collective-permute-start.26 = (bf16[128,512]{1,0:T(8,128)(2,1)}, bf16[128,512]{1,0:T(8,128)(2,1)S(1)}, u32[]{:S(2)}, u32[]{:S(2)}) collective-permute-start(bf16[128,512]{1,0:T(8,128)(2,1)} %get-tuple-element.44), channel_id=1, source_target_pairs={{0,2},{2,4},{4,6},{6,8},{8,10},{10,12},{12,14},{14,0},{1,3},{3,5},... | collective-permute-start | bytes 393224 | tf_op jit(solution)/shard_map/ppermute | solution.py:33
  50.4 28.7 %collective-permute-start.23 = (bf16[128,512]{1,0:T(8,128)(2,1)}, bf16[128,512]{1,0:T(8,128)(2,1)S(1)}, u32[]{:S(2)}, u32[]{:S(2)}) collective-permute-start(bf16[128,512]{1,0:T(8,128)(2,1)} %get-tuple-element.41), channel_id=1, source_target_pairs={{0,14},{2,0},{4,2},{6,4},{8,6},{10,8},{12,10},{14,12},{1,15},{3,1}... | collective-permute-start | bytes 393224 | tf_op jit(solution)/shard_map/ppermute | solution.py:33
  51.0 28.2 %collective-permute-start.20 = (bf16[128,512]{1,0:T(8,128)(2,1)}, bf16[128,512]{1,0:T(8,128)(2,1)S(1)}, u32[]{:S(2)}, u32[]{:S(2)}) collective-permute-start(bf16[128,512]{1,0:T(8,128)(2,1)} %get-tuple-element.38), channel_id=1, source_target_pairs={{0,2},{2,4},{4,6},{6,8},{8,10},{10,12},{12,14},{14,0},{1,3},{3,5},... | collective-permute-start | bytes 393224 | tf_op jit(solution)/shard_map/ppermute | solution.py:33
  63.2 17.8 %collective-permute-start.16 = (bf16[128,512]{1,0:T(8,128)(2,1)}, bf16[128,512]{1,0:T(8,128)(2,1)S(1)}, u32[]{:S(2)}, u32[]{:S(2)}) collective-permute-start(bf16[128,512]{1,0:T(8,128)(2,1)} %get-tuple-element.34), channel_id=1, source_target_pairs={{0,14},{2,0},{4,2},{6,4},{8,6},{10,8},{12,10},{14,12},{1,15},{3,1}... | collective-permute-start | bytes 393224 | tf_op jit(solution)/shard_map/ppermute | solution.py:33
  63.2 15.8 %copy-start.14 = (bf16[128,512]{1,0:T(8,128)(2,1)S(1)}, bf16[128,512]{1,0:T(8,128)(2,1)}, u32[]{:S(2)}) copy-start(bf16[128,512]{1,0:T(8,128)(2,1)} %get-tuple-element.42) | copy-start | bytes 393220
  63.2 15.9 %copy-start.13 = (bf16[128,512]{1,0:T(8,128)(2,1)S(1)}, bf16[128,512]{1,0:T(8,128)(2,1)}, u32[]{:S(2)}) copy-start(bf16[128,512]{1,0:T(8,128)(2,1)} %get-tuple-element.39) | copy-start | bytes 393220
  63.2 17.8 %copy-start.12 = (bf16[128,512]{1,0:T(8,128)(2,1)S(1)}, bf16[128,512]{1,0:T(8,128)(2,1)}, u32[]{:S(2)}) copy-start(bf16[128,512]{1,0:T(8,128)(2,1)} %get-tuple-element.35) | copy-start | bytes 393220
  63.3 18.9 %copy-start.11 = (bf16[128,512]{1,0:T(8,128)(2,1)S(1)}, bf16[128,512]{1,0:T(8,128)(2,1)}, u32[]{:S(2)}) copy-start(bf16[128,512]{1,0:T(8,128)(2,1)} %get-tuple-element.46) | copy-start | bytes 393220
  63.3 21.0 %copy-start.10 = (bf16[128,512]{1,0:T(8,128)(2,1)S(1)}, bf16[128,512]{1,0:T(8,128)(2,1)}, u32[]{:S(2)}) copy-start(bf16[128,512]{1,0:T(8,128)(2,1)} %get-tuple-element.43) | copy-start | bytes 393220
  63.3 42.6 %all-to-all-start = ((bf16[32,16,2048]{2,1,0:T(8,128)(2,1)}), bf16[32,16,2048]{2,1,0:T(8,128)(2,1)S(1)}, u32[]{:S(2)}, u32[]{:S(2)}) async-start(bf16[32,16,2048]{2,1,0:T(8,128)(2,1)} %bitcast.20), calls=%async_computation | async-start | bytes 4194304 | tf_op jit(solution)/shard_map/all_to_all | solution.py:410
  75.9 16.2 %copy-start.6 = (bf16[128,512]{1,0:T(8,128)(2,1)S(1)}, bf16[128,512]{1,0:T(8,128)(2,1)}, u32[]{:S(2)}) copy-start(bf16[128,512]{1,0:T(8,128)(2,1)} %get-tuple-element.37) | copy-start | bytes 393220
  75.9 20.9 %copy-start.1 = (bf16[128,4224]{1,0:T(8,128)(2,1)S(1)}, bf16[128,4224]{1,0:T(8,128)(2,1)}, u32[]{:S(2)}) copy-start(bf16[128,4224]{1,0:T(8,128)(2,1)} %copy-done) | copy-start | bytes 3244036
  75.9 20.9 %copy-start.2 = (f32[128,512]{1,0:T(8,128)S(1)}, f32[128,512]{1,0:T(8,128)}, u32[]{:S(2)}) copy-start(f32[128,512]{1,0:T(8,128)} %get-tuple-element.32.own_a) | copy-start | bytes 786436
  75.9 20.9 %copy-start.3 = (f32[128,512]{1,0:T(8,128)S(1)}, f32[128,512]{1,0:T(8,128)}, u32[]{:S(2)}) copy-start(f32[128,512]{1,0:T(8,128)} %get-tuple-element.33.own_b) | copy-start | bytes 786436
  75.9 20.9 %copy-start.4 = (bf16[128,128]{1,0:T(8,128)(2,1)S(1)}, bf16[128,128]{1,0:T(8,128)(2,1)}, u32[]{:S(2)}) copy-start(bf16[128,128]{1,0:T(8,128)(2,1)} %get-tuple-element.31.refs_20_.extra_own) | copy-start | bytes 98308
  75.9 20.9 %copy-start.5 = (s32[2]{0:T(128)S(1)}, s32[2]{0:T(128)}, u32[]{:S(2)}) copy-start(s32[2]{0:T(128)} %pad_add_fusion.where_ref) | copy-start | bytes 28
  76.0 6.2 %collective-permute-start.27 = (bf16[128,512]{1,0:T(8,128)(2,1)S(1)}, bf16[128,512]{1,0:T(8,128)(2,1)S(1)}, u32[]{:S(2)}, u32[]{:S(2)}) collective-permute-start(bf16[128,512]{1,0:T(8,128)(2,1)S(1)} %add_convert_fusion.2), channel_id=1, source_target_pairs={{0,2},{2,4},{4,6},{6,8},{8,10},{10,12},{12,14},{14,0},{1,3},{3,5},... | collective-permute-start | bytes 393224 | tf_op jit(solution)/shard_map/ppermute | solution.py:33
  79.1 5.2 %collective-permute-start.24 = (bf16[128,512]{1,0:T(8,128)(2,1)S(1)}, bf16[128,512]{1,0:T(8,128)(2,1)S(1)}, u32[]{:S(2)}, u32[]{:S(2)}) collective-permute-start(bf16[128,512]{1,0:T(8,128)(2,1)S(1)} %add_convert_fusion.4), channel_id=1, source_target_pairs={{0,14},{2,0},{4,2},{6,4},{8,6},{10,8},{12,10},{14,12},{1,15},{3,1}... | collective-permute-start | bytes 393224 | tf_op jit(solution)/shard_map/ppermute | solution.py:33
  79.2 6.1 %collective-permute-start.21 = (bf16[128,512]{1,0:T(8,128)(2,1)S(1)}, bf16[128,512]{1,0:T(8,128)(2,1)S(1)}, u32[]{:S(2)}, u32[]{:S(2)}) collective-permute-start(bf16[128,512]{1,0:T(8,128)(2,1)S(1)} %add_convert_fusion.6), channel_id=1, source_target_pairs={{0,2},{2,4},{4,6},{6,8},{8,10},{10,12},{12,14},{14,0},{1,3},{3,5},... | collective-permute-start | bytes 393224 | tf_op jit(solution)/shard_map/ppermute | solution.py:33
  81.1 6.0 %collective-permute-start.17 = (bf16[128,512]{1,0:T(8,128)(2,1)S(1)}, bf16[128,512]{1,0:T(8,128)(2,1)S(1)}, u32[]{:S(2)}, u32[]{:S(2)}) collective-permute-start(bf16[128,512]{1,0:T(8,128)(2,1)S(1)} %add_convert_fusion.9), channel_id=1, source_target_pairs={{0,14},{2,0},{4,2},{6,4},{8,6},{10,8},{12,10},{14,12},{1,15},{3,1}... | collective-permute-start | bytes 393224 | tf_op jit(solution)/shard_map/ppermute | solution.py:33
  82.2 6.1 %collective-permute-start.28 = (bf16[128,512]{1,0:T(8,128)(2,1)S(1)}, bf16[128,512]{1,0:T(8,128)(2,1)S(1)}, u32[]{:S(2)}, u32[]{:S(2)}) collective-permute-start(bf16[128,512]{1,0:T(8,128)(2,1)S(1)} %add_convert_fusion.1), channel_id=1, source_target_pairs={{0,2},{2,4},{4,6},{6,8},{8,10},{10,12},{12,14},{14,0},{1,3},{3,5},... | collective-permute-start | bytes 393224 | tf_op jit(solution)/shard_map/ppermute | solution.py:33
  84.3 9.6 %collective-permute-start.25 = (bf16[128,512]{1,0:T(8,128)(2,1)S(1)}, bf16[128,512]{1,0:T(8,128)(2,1)S(1)}, u32[]{:S(2)}, u32[]{:S(2)}) collective-permute-start(bf16[128,512]{1,0:T(8,128)(2,1)S(1)} %add_convert_fusion.3), channel_id=1, source_target_pairs={{0,14},{2,0},{4,2},{6,4},{8,6},{10,8},{12,10},{14,12},{1,15},{3,1}... | collective-permute-start | bytes 393224 | tf_op jit(solution)/shard_map/ppermute | solution.py:33
  85.4 8.5 %collective-permute-start.22 = (bf16[128,512]{1,0:T(8,128)(2,1)S(1)}, bf16[128,512]{1,0:T(8,128)(2,1)S(1)}, u32[]{:S(2)}, u32[]{:S(2)}) collective-permute-start(bf16[128,512]{1,0:T(8,128)(2,1)S(1)} %add_convert_fusion.5), channel_id=1, source_target_pairs={{0,2},{2,4},{4,6},{6,8},{8,10},{10,12},{12,14},{14,0},{1,3},{3,5},... | collective-permute-start | bytes 393224 | tf_op jit(solution)/shard_map/ppermute | solution.py:33
  87.2 5.0 %collective-permute-start.18 = (bf16[128,512]{1,0:T(8,128)(2,1)S(1)}, bf16[128,512]{1,0:T(8,128)(2,1)S(1)}, u32[]{:S(2)}, u32[]{:S(2)}) collective-permute-start(bf16[128,512]{1,0:T(8,128)(2,1)S(1)} %add_convert_fusion.8), channel_id=1, source_target_pairs={{0,14},{2,0},{4,2},{6,4},{8,6},{10,8},{12,10},{14,12},{1,15},{3,1}... | collective-permute-start | bytes 393224 | tf_op jit(solution)/shard_map/ppermute | solution.py:33
  88.3 5.9 %collective-permute-start.29 = (bf16[128,512]{1,0:T(8,128)(2,1)S(1)}, bf16[128,512]{1,0:T(8,128)(2,1)S(1)}, u32[]{:S(2)}, u32[]{:S(2)}) collective-permute-start(bf16[128,512]{1,0:T(8,128)(2,1)S(1)} %add_convert_fusion), channel_id=1, source_target_pairs={{0,2},{2,4},{4,6},{6,8},{8,10},{10,12},{12,14},{14,0},{1,3},{3,5},... | collective-permute-start | bytes 393224 | tf_op jit(solution)/shard_map/ppermute | solution.py:33
  92.1 4.6 %collective-permute-start.19 = (bf16[128,512]{1,0:T(8,128)(2,1)S(1)}, bf16[128,512]{1,0:T(8,128)(2,1)S(1)}, u32[]{:S(2)}, u32[]{:S(2)}) collective-permute-start(bf16[128,512]{1,0:T(8,128)(2,1)S(1)} %add_convert_fusion.7), channel_id=1, source_target_pairs={{0,14},{2,0},{4,2},{6,4},{8,6},{10,8},{12,10},{14,12},{1,15},{3,1}... | collective-permute-start | bytes 393224 | tf_op jit(solution)/shard_map/ppermute | solution.py:33
  (17 other events, 138.3 us)
